TPU v7x, 256 devices: a whole 4x4x8 slice. The times are simulated.
256 devices in a mesh: segment: 16 (over x_lo, y, core), tile: 16 (over x_hi, z).
Axes of the slice: x: 4 (x_hi: 2, x_lo: 2; x = x_hi * 2 + x_lo), y: 4, z: 8, core: 2. Of those that a mesh axis runs over, the one named last changes fastest.
Arguments:
- features: bfloat16 [8, 48, 128, 320], P(None, 'tile'), may hold values from -27 to 27
- timesteps: int32 [8], replicated, may hold values from 0 to 999
- plan: int32 [8], replicated, may hold values from 0 to 7, each once
- conv_weight: bfloat16 [16, 2880, 320], P('segment'), may hold values from -0.109375 to 0.109375
- skip_weight: bfloat16 [16, 320, 320], P('segment'), may hold values from -0.3125 to 0.3125
- time_weight: float32 [16, 320, 320], P('segment'), may hold values from -0.3125 to 0.3125
- norm_gain: float32 [16, 320], P('segment'), may hold values from 0.5 to 1.5
- norm_bias: float32 [16, 320], P('segment'), may hold values from -3 to 3
Outputs:
- activations: bfloat16 [16, 8, 48, 128, 320], P('segment', None, 'tile')
All inputs are finite; a program needn't handle non-finite values.
Results may differ from a plain program's by a relative error of at most 0.017.
Values may be sent and summed in bfloat16 or wider, within the bound.
No kernel may reach another device: no remote copies, remote signals or barrier semaphores. Data moves between devices by JAX's collectives and lax.ppermute only.
A program may use at most 64 MiB of HBM per device.

v0:
```python
import math

import jax
import jax.numpy as jnp
from jax import lax
from jax.sharding import PartitionSpec as P

GROUPS = 32


def with_halo(array, sides, width):
    for axis, dim in sides:
        peers, length = (lax.axis_size(axis), array.shape[dim])
        up = [(i, (i + 1) % peers) for i in range(peers - 1)]
        down = [(j, i) for i, j in up]
        last = lax.slice_in_dim(array, length - width, length, axis=dim)
        initial = lax.slice_in_dim(array, 0, width, axis=dim)
        before = lax.ppermute(last, axis, up)
        after = lax.ppermute(initial, axis, down)
        array = jnp.concatenate([before, array, after], axis=dim)
    return array


def shifted(block, axis, distance):
    devices = range(lax.axis_size(axis))
    route = [(i - distance, i) for i in devices if i - distance in devices]
    return lax.ppermute(block, axis, route)


def from_partner(value, axis, bit):
    mask = 2**bit
    pairs = [(source, source ^ mask) for source in range(lax.axis_size(axis))]
    return lax.ppermute(value, axis, pairs)


def sinusoid(steps, half_width):
    rates = jnp.exp(-math.log(10000.0) * jnp.arange(half_width, dtype=jnp.float32) / half_width)
    angles = steps.astype(jnp.float32)[:, None] * rates[None, :]
    return jnp.concatenate([jnp.cos(angles), jnp.sin(angles)], axis=-1)


def convolve(padded, kernel, height, width):
    channels = padded.shape[-1]
    patches = jnp.concatenate(
        [
            padded[row_shift : row_shift + height, col_shift : col_shift + width]
            for row_shift in range(3)
            for col_shift in range(3)
        ],
        axis=-1,
    )
    product = jnp.dot(
        patches.reshape(height * width, 9 * channels), kernel, preferred_element_type=jnp.float32
    )
    return product.reshape(height, width, kernel.shape[1])


def on_device(
    features, timesteps, plan, conv_weight, skip_weight, time_weight, norm_gain, norm_bias
):
    segments = lax.axis_size("segment")
    position = lax.axis_index("segment")
    tiles = lax.axis_size("tile")
    micro, rows, width, channels = features.shape
    down_count = segments // 4
    first_up = segments - down_count
    ticks = micro + segments - 1
    kernel = conv_weight[0]
    lateral_map = skip_weight[0]
    gains = norm_gain[0]
    biases = norm_bias[0]
    encoded = sinusoid(timesteps[plan], time_weight.shape[1] // 2)
    embedded_all = jnp.dot(encoded, time_weight[0], precision=lax.Precision.HIGHEST)
    members = float(rows * tiles * width * (channels // GROUPS))
    is_up = position >= first_up

    def res_block(hidden_in, lateral, embedded, is_valid):
        summed = hidden_in.astype(jnp.float32)

        def with_lateral():
            projected = jnp.dot(
                lateral.reshape(rows * width, channels),
                lateral_map,
                preferred_element_type=jnp.float32,
            )
            return summed + projected.reshape(rows, width, channels)

        summed = lax.cond(is_up & is_valid, with_lateral, lambda: summed)
        grouped = summed.reshape(rows * width, GROUPS, channels // GROUPS)
        totals, squares = lax.psum(
            (jnp.sum(grouped, axis=(0, 2)), jnp.sum(grouped * grouped, axis=(0, 2))), "tile"
        )
        average = totals / members
        variance = jnp.maximum(squares / members - average * average, 0.0)
        centred = grouped - average[None, :, None]
        normed = (centred * lax.rsqrt(variance + 1e-05)[None, :, None]).reshape(
            rows, width, channels
        ) * gains + biases
        lifted = (jax.nn.silu(normed) + embedded).astype(jnp.bfloat16)
        extended = with_halo(lifted, (("tile", 0),), 1)
        padded = jnp.pad(extended, ((0, 0), (1, 1), (0, 0)))
        convolved = lax.cond(
            is_valid,
            lambda: convolve(padded, kernel, rows, width),
            lambda: jnp.zeros((rows, width, channels), jnp.float32),
        )
        return (summed + convolved).astype(jnp.bfloat16)

    def tick(step, carry):
        incoming, saved, mirrored = carry
        slot_index = step - position
        is_valid = (slot_index >= 0) & (slot_index < micro)
        clipped = jnp.clip(slot_index, 0, micro - 1)
        sample = lax.dynamic_index_in_dim(plan, clipped, 0, keepdims=False)
        entering = lax.dynamic_index_in_dim(features, sample, 0, keepdims=False)
        hidden_in = jnp.where(position == 0, entering, incoming)
        lateral = lax.dynamic_index_in_dim(mirrored, clipped, 0, keepdims=False)
        embedded = lax.dynamic_index_in_dim(embedded_all, clipped, 0, keepdims=False)
        result = res_block(hidden_in, lateral, embedded, is_valid)
        kept = jnp.where(
            is_valid, result, lax.dynamic_index_in_dim(saved, clipped, 0, keepdims=False)
        )
        saved = lax.dynamic_update_index_in_dim(saved, kept, clipped, 0)
        incoming = shifted(result, "segment", 1)
        return (incoming, saved, mirrored)

    empty_block = jnp.zeros((rows, width, channels), jnp.bfloat16)
    empty_slots = jnp.zeros((micro, rows, width, channels), jnp.bfloat16)
    carry = (empty_block, empty_slots, empty_slots)
    carry = lax.fori_loop(0, first_up, lambda step, state: tick(step, state), carry)
    incoming, saved, mirrored = carry
    arrived = saved
    for bit_index in range(segments.bit_length() - 1):
        arrived = from_partner(arrived, "segment", bit_index)
    mirrored = arrived
    carry = lax.fori_loop(
        first_up, ticks, lambda step, state: tick(step, state), (incoming, saved, mirrored)
    )
    return carry[1][None]


def solution(mesh):
    placed = (
        P(None, "tile", None, None),
        P(),
        P(),
        P("segment", None, None),
        P("segment", None, None),
        P("segment", None, None),
        P("segment", None),
        P("segment", None),
    )
    return jax.shard_map(
        on_device,
        mesh=mesh,
        in_specs=placed,
        out_specs=P("segment", None, "tile", None, None),
        check_vma=False,
    )
```

profile of v0, /device:TPU:59, one launch (start us, length us, event | category | flops | bytes accessed | tf_op | source)
XLA Modules:
  0.0 1667.3 jit_solution(5403234914341964746)
XLA Ops:
  5.5 753.9 %while.34 = (s32[]{:T(128)}, bf16[3,128,320]{1,2,0:T(8,128)(2,1)S(1)}, bf16[8,3,128,320]{2,3,1,0:T(8,128)(2,1)}, s32[]{:T(128)}, pred[]{:T(512)}, /*index=5*/pre...) while((s32[]{:T(128)}, ...), condition=%wide.region_11.12_spmd, body=%wide.region_0.11_spmd.sunk | while | flops 789176512 | bytes 25756932 | solution.py:130
  252.5 32.9 %all-reduce.6 = (f32[32]{0:T(128)S(1)}, f32[32]{0:T(128)S(1)}) all-reduce(f32[32]{0:T(128)S(1)} %reduce_sum.108, f32[32]{0:T(128)S(1)} %reduce_sum.110), channel_id=1, replica_groups=mesh['segment'=16,'tile'=16] {'tile'}, use_global_device_ids=true, to_apply=%region_8.8 | all-reduce | flops 64 | bytes 512 | tf_op jit(solution)/shard_map/while/body/eval_jaxpr/psum | solution.py:90
  316.4 32.9 %all-reduce.6 = (f32[32]{0:T(128)S(1)}, f32[32]{0:T(128)S(1)}) all-reduce(f32[32]{0:T(128)S(1)} %reduce_sum.108, f32[32]{0:T(128)S(1)} %reduce_sum.110), channel_id=1, replica_groups=mesh['segment'=16,'tile'=16] {'tile'}, use_global_device_ids=true, to_apply=%region_8.8 | all-reduce | flops 64 | bytes 512 | tf_op jit(solution)/shard_map/while/body/eval_jaxpr/psum | solution.py:90
  380.3 32.9 %all-reduce.6 = (f32[32]{0:T(128)S(1)}, f32[32]{0:T(128)S(1)}) all-reduce(f32[32]{0:T(128)S(1)} %reduce_sum.108, f32[32]{0:T(128)S(1)} %reduce_sum.110), channel_id=1, replica_groups=mesh['segment'=16,'tile'=16] {'tile'}, use_global_device_ids=true, to_apply=%region_8.8 | all-reduce | flops 64 | bytes 512 | tf_op jit(solution)/shard_map/while/body/eval_jaxpr/psum | solution.py:90
  444.2 32.9 %all-reduce.6 = (f32[32]{0:T(128)S(1)}, f32[32]{0:T(128)S(1)}) all-reduce(f32[32]{0:T(128)S(1)} %reduce_sum.108, f32[32]{0:T(128)S(1)} %reduce_sum.110), channel_id=1, replica_groups=mesh['segment'=16,'tile'=16] {'tile'}, use_global_device_ids=true, to_apply=%region_8.8 | all-reduce | flops 64 | bytes 512 | tf_op jit(solution)/shard_map/while/body/eval_jaxpr/psum | solution.py:90
  508.0 32.9 %all-reduce.6 = (f32[32]{0:T(128)S(1)}, f32[32]{0:T(128)S(1)}) all-reduce(f32[32]{0:T(128)S(1)} %reduce_sum.108, f32[32]{0:T(128)S(1)} %reduce_sum.110), channel_id=1, replica_groups=mesh['segment'=16,'tile'=16] {'tile'}, use_global_device_ids=true, to_apply=%region_8.8 | all-reduce | flops 64 | bytes 512 | tf_op jit(solution)/shard_map/while/body/eval_jaxpr/psum | solution.py:90
  571.9 32.9 %all-reduce.6 = (f32[32]{0:T(128)S(1)}, f32[32]{0:T(128)S(1)}) all-reduce(f32[32]{0:T(128)S(1)} %reduce_sum.108, f32[32]{0:T(128)S(1)} %reduce_sum.110), channel_id=1, replica_groups=mesh['segment'=16,'tile'=16] {'tile'}, use_global_device_ids=true, to_apply=%region_8.8 | all-reduce | flops 64 | bytes 512 | tf_op jit(solution)/shard_map/while/body/eval_jaxpr/psum | solution.py:90
  635.8 32.9 %all-reduce.6 = (f32[32]{0:T(128)S(1)}, f32[32]{0:T(128)S(1)}) all-reduce(f32[32]{0:T(128)S(1)} %reduce_sum.108, f32[32]{0:T(128)S(1)} %reduce_sum.110), channel_id=1, replica_groups=mesh['segment'=16,'tile'=16] {'tile'}, use_global_device_ids=true, to_apply=%region_8.8 | all-reduce | flops 64 | bytes 512 | tf_op jit(solution)/shard_map/while/body/eval_jaxpr/psum | solution.py:90
  699.7 32.9 %all-reduce.6 = (f32[32]{0:T(128)S(1)}, f32[32]{0:T(128)S(1)}) all-reduce(f32[32]{0:T(128)S(1)} %reduce_sum.108, f32[32]{0:T(128)S(1)} %reduce_sum.110), channel_id=1, replica_groups=mesh['segment'=16,'tile'=16] {'tile'}, use_global_device_ids=true, to_apply=%region_8.8 | all-reduce | flops 64 | bytes 512 | tf_op jit(solution)/shard_map/while/body/eval_jaxpr/psum | solution.py:90
  768.5 43.4 %collective-permute-done.7 = bf16[8,3,128,320]{2,3,1,0:T(8,128)(2,1)S(1)} collective-permute-done((bf16[8,3,128,320]{2,3,1,0:T(8,128)(2,1)S(1)}, bf16[8,3,128,320]{2,3,1,0:T(8,128)(2,1)S(1)}, u32[]{:S(2)}, u32[]{:S(2)}) %collective-permute-start.7) | collective-permute-done | bytes 1966112 | tf_op jit(solution)/shard_map/ppermute | solution.py:33
  811.9 37.0 %collective-permute-start.8 = (bf16[8,3,128,320]{2,3,1,0:T(8,128)(2,1)S(1)}, bf16[8,3,128,320]{2,3,1,0:T(8,128)(2,1)}, u32[]{:S(2)}, u32[]{:S(2)}) collective-permute-start(bf16[8,3,128,320]{2,3,1,0:T(8,128)(2,1)S(1)} %collective-permute-done.7), channel_id=1, source_target_pairs={{0,64},{16,80},{32,96},{48,112},{64,0},{80,16},{96,32},{112,48},{1... | collective-permute-start | bytes 5898248 | tf_op jit(solution)/shard_map/ppermute | solution.py:33
  848.9 42.4 %collective-permute-done.8 = bf16[8,3,128,320]{2,3,1,0:T(8,128)(2,1)} collective-permute-done((bf16[8,3,128,320]{2,3,1,0:T(8,128)(2,1)S(1)}, bf16[8,3,128,320]{2,3,1,0:T(8,128)(2,1)}, u32[]{:S(2)}, u32[]{:S(2)}) %collective-permute-start.8) | collective-permute-done | bytes 1966112 | tf_op jit(solution)/shard_map/ppermute | solution.py:33
  891.3 43.2 %collective-permute-done.9 = bf16[8,3,128,320]{2,3,1,0:T(8,128)(2,1)} collective-permute-done((bf16[8,3,128,320]{2,3,1,0:T(8,128)(2,1)}, bf16[8,3,128,320]{2,3,1,0:T(8,128)(2,1)}, u32[]{:S(2)}, u32[]{:S(2)}) %collective-permute-start.9) | collective-permute-done | bytes 1966112 | tf_op jit(solution)/shard_map/ppermute | solution.py:33
  934.5 732.9 %while.35 = (s32[]{:T(128)}, bf16[3,128,320]{1,2,0:T(8,128)(2,1)S(1)}, bf16[8,3,128,320]{2,3,1,0:T(8,128)(2,1)}, s32[]{:T(128)}, pred[]{:T(512)}, /*index=5*/pre...) while((s32[]{:T(128)}, ...), condition=%wide.region_23.24_spmd, body=%wide.region_12.23_spmd.sunk | while | flops 789176512 | bytes 26003756 | solution.py:136
  938.6 33.1 %all-reduce.7 = (f32[32]{0:T(128)S(1)}, f32[32]{0:T(128)S(1)}) all-reduce(f32[32]{0:T(128)S(1)} %reduce_sum.113, f32[32]{0:T(128)S(1)} %reduce_sum.115), channel_id=1, replica_groups=mesh['segment'=16,'tile'=16] {'tile'}, use_global_device_ids=true, to_apply=%region_20.20 | all-reduce | flops 64 | bytes 512 | tf_op jit(solution)/shard_map/while/body/eval_jaxpr/psum | solution.py:90
  1000.3 33.0 %all-reduce.7 = (f32[32]{0:T(128)S(1)}, f32[32]{0:T(128)S(1)}) all-reduce(f32[32]{0:T(128)S(1)} %reduce_sum.113, f32[32]{0:T(128)S(1)} %reduce_sum.115), channel_id=1, replica_groups=mesh['segment'=16,'tile'=16] {'tile'}, use_global_device_ids=true, to_apply=%region_20.20 | all-reduce | flops 64 | bytes 512 | tf_op jit(solution)/shard_map/while/body/eval_jaxpr/psum | solution.py:90
  1133.4 32.9 %all-reduce.7 = (f32[32]{0:T(128)S(1)}, f32[32]{0:T(128)S(1)}) all-reduce(f32[32]{0:T(128)S(1)} %reduce_sum.113, f32[32]{0:T(128)S(1)} %reduce_sum.115), channel_id=1, replica_groups=mesh['segment'=16,'tile'=16] {'tile'}, use_global_device_ids=true, to_apply=%region_20.20 | all-reduce | flops 64 | bytes 512 | tf_op jit(solution)/shard_map/while/body/eval_jaxpr/psum | solution.py:90
  1201.3 33.0 %all-reduce.7 = (f32[32]{0:T(128)S(1)}, f32[32]{0:T(128)S(1)}) all-reduce(f32[32]{0:T(128)S(1)} %reduce_sum.113, f32[32]{0:T(128)S(1)} %reduce_sum.115), channel_id=1, replica_groups=mesh['segment'=16,'tile'=16] {'tile'}, use_global_device_ids=true, to_apply=%region_20.20 | all-reduce | flops 64 | bytes 512 | tf_op jit(solution)/shard_map/while/body/eval_jaxpr/psum | solution.py:90
  1269.3 32.9 %all-reduce.7 = (f32[32]{0:T(128)S(1)}, f32[32]{0:T(128)S(1)}) all-reduce(f32[32]{0:T(128)S(1)} %reduce_sum.113, f32[32]{0:T(128)S(1)} %reduce_sum.115), channel_id=1, replica_groups=mesh['segment'=16,'tile'=16] {'tile'}, use_global_device_ids=true, to_apply=%region_20.20 | all-reduce | flops 64 | bytes 512 | tf_op jit(solution)/shard_map/while/body/eval_jaxpr/psum | solution.py:90
  1337.2 32.9 %all-reduce.7 = (f32[32]{0:T(128)S(1)}, f32[32]{0:T(128)S(1)}) all-reduce(f32[32]{0:T(128)S(1)} %reduce_sum.113, f32[32]{0:T(128)S(1)} %reduce_sum.115), channel_id=1, replica_groups=mesh['segment'=16,'tile'=16] {'tile'}, use_global_device_ids=true, to_apply=%region_20.20 | all-reduce | flops 64 | bytes 512 | tf_op jit(solution)/shard_map/while/body/eval_jaxpr/psum | solution.py:90
  1405.1 32.9 %all-reduce.7 = (f32[32]{0:T(128)S(1)}, f32[32]{0:T(128)S(1)}) all-reduce(f32[32]{0:T(128)S(1)} %reduce_sum.113, f32[32]{0:T(128)S(1)} %reduce_sum.115), channel_id=1, replica_groups=mesh['segment'=16,'tile'=16] {'tile'}, use_global_device_ids=true, to_apply=%region_20.20 | all-reduce | flops 64 | bytes 512 | tf_op jit(solution)/shard_map/while/body/eval_jaxpr/psum | solution.py:90
  1473.1 32.9 %all-reduce.7 = (f32[32]{0:T(128)S(1)}, f32[32]{0:T(128)S(1)}) all-reduce(f32[32]{0:T(128)S(1)} %reduce_sum.113, f32[32]{0:T(128)S(1)} %reduce_sum.115), channel_id=1, replica_groups=mesh['segment'=16,'tile'=16] {'tile'}, use_global_device_ids=true, to_apply=%region_20.20 | all-reduce | flops 64 | bytes 512 | tf_op jit(solution)/shard_map/while/body/eval_jaxpr/psum | solution.py:90
  1541.0 32.9 %all-reduce.7 = (f32[32]{0:T(128)S(1)}, f32[32]{0:T(128)S(1)}) all-reduce(f32[32]{0:T(128)S(1)} %reduce_sum.113, f32[32]{0:T(128)S(1)} %reduce_sum.115), channel_id=1, replica_groups=mesh['segment'=16,'tile'=16] {'tile'}, use_global_device_ids=true, to_apply=%region_20.20 | all-reduce | flops 64 | bytes 512 | tf_op jit(solution)/shard_map/while/body/eval_jaxpr/psum | solution.py:90
  1608.9 32.8 %all-reduce.7 = (f32[32]{0:T(128)S(1)}, f32[32]{0:T(128)S(1)}) all-reduce(f32[32]{0:T(128)S(1)} %reduce_sum.113, f32[32]{0:T(128)S(1)} %reduce_sum.115), channel_id=1, replica_groups=mesh['segment'=16,'tile'=16] {'tile'}, use_global_device_ids=true, to_apply=%region_20.20 | all-reduce | flops 64 | bytes 512 | tf_op jit(solution)/shard_map/while/body/eval_jaxpr/psum | solution.py:90
  (790 shorter events, 895.8 us)
Async XLA Ops:
  111.5 16.1 collective-permute-start.2
  171.8 16.1 collective-permute-start.2
  232.2 16.1 collective-permute-start.2
  296.3 15.9 collective-permute-start.2
  360.2 15.9 collective-permute-start.2
  424.1 15.9 collective-permute-start.2
  487.9 15.9 collective-permute-start.2
  551.8 15.9 collective-permute-start.2
  615.7 15.9 collective-permute-start.2
  679.6 15.9 collective-permute-start.2
  743.5 15.9 collective-permute-start.2
  767.9 44.0 %collective-permute-start.7 = (bf16[8,3,128,320]{2,3,1,0:T(8,128)(2,1)S(1)}, bf16[8,3,128,320]{2,3,1,0:T(8,128)(2,1)S(1)}, u32[]{:S(2)}, u32[]{:S(2)}) collective-permute-start(bf16[8,3,128,320]{2,3,1,0:T(8,128)(2,1)S(1)} %collective-permute-done.6), channel_id=1, source_target_pairs={{0,32},{16,48},{32,0},{48,16},{64,96},{80,112},{96,64},{112,80},{1... | collective-permute-start | bytes 5898248 | tf_op jit(solution)/shard_map/ppermute | solution.py:33
  811.9 79.4 %collective-permute-start.8 = (bf16[8,3,128,320]{2,3,1,0:T(8,128)(2,1)S(1)}, bf16[8,3,128,320]{2,3,1,0:T(8,128)(2,1)}, u32[]{:S(2)}, u32[]{:S(2)}) collective-permute-start(bf16[8,3,128,320]{2,3,1,0:T(8,128)(2,1)S(1)} %collective-permute-done.7), channel_id=1, source_target_pairs={{0,64},{16,80},{32,96},{48,112},{64,0},{80,16},{96,32},{112,48},{1... | collective-permute-start | bytes 5898248 | tf_op jit(solution)/shard_map/ppermute | solution.py:33
  891.3 43.2 %collective-permute-start.9 = (bf16[8,3,128,320]{2,3,1,0:T(8,128)(2,1)}, bf16[8,3,128,320]{2,3,1,0:T(8,128)(2,1)}, u32[]{:S(2)}, u32[]{:S(2)}) collective-permute-start(bf16[8,3,128,320]{2,3,1,0:T(8,128)(2,1)} %collective-permute-done.8), channel_id=1, source_target_pairs={{0,128},{16,144},{32,160},{48,176},{64,192},{80,208},{96,224},{112... | collective-permute-start | bytes 5898248 | tf_op jit(solution)/shard_map/ppermute | solution.py:33
  982.2 14.0 collective-permute-start.5
  1044.2 15.9 collective-permute-start.5
  1107.8 20.3 %collective-permute-start.5 = (bf16[3,128,320]{1,2,0:T(8,128)(2,1)S(1)}, bf16[3,128,320]{1,2,0:T(8,128)(2,1)S(1)}, u32[]{:S(2)}, u32[]{:S(2)}) collective-permute-start(bf16[3,128,320]{1,2,0:T(8,128)(2,1)S(1)} %get-tuple-element.994), channel_id=1, source_target_pairs={{0,16},{16,32},{32,48},{48,64},{64,80},{80,96},{96,112},{112,128},... | collective-permute-start | bytes 737288 | tf_op jit(solution)/shard_map/while/body/eval_jaxpr/ppermute | solution.py:27
  1180.0 15.9 collective-permute-start.5
  1248.0 15.9 collective-permute-start.5
  1315.9 15.9 collective-permute-start.5
  1383.8 15.9 collective-permute-start.5
  1451.7 15.9 collective-permute-start.5
  1519.7 15.9 collective-permute-start.5
  1587.6 15.9 collective-permute-start.5
  (61 other events, 345.5 us)
where the time goes:
time: 1690 us; the launch traced here: 1670 us
  blocking collectives  745 us (44%)
  waiting for transfers between devices  516 us (31%)
  starting transfers between devices  211 us (12%)
  local copies, waits for them, and re-layouts  68 us (4%)
  other arithmetic  60.6 us (4%)
  loops' own time  47.3 us (3%)
  matrix products  19.7 us (1%)
    psum x23, blocking collectives, res_block(): lax.psum((jnp.sum(grouped, axis=(0, 2)), jnp.sum(grouped * grouped, axis=...  745 us
    ppermute x23, waiting for transfers between devices, shifted(): return lax.ppermute(block, axis, route)  331 us
    ppermute x4, waiting for transfers between devices, from_partner(): return lax.ppermute(value, axis, pairs)  133 us
    ppermute x23, starting transfers between devices, with_halo(): after = lax.ppermute(initial, axis, down)  94.3 us
    ppermute x23, waiting for transfers between devices, with_halo(): before = lax.ppermute(last, axis, up)  51.6 us
    ppermute x23, starting transfers between devices, with_halo(): before = lax.ppermute(last, axis, up)  45 us
    ppermute x4, starting transfers between devices, from_partner(): return lax.ppermute(value, axis, pairs)  42.3 us
  transfers between devices with their start and end apart: 73, of which 50 were waited for; matrix products, arithmetic and copies ran while one was open for 1% of the time, Pallas kernels for 0%

commit v1 on v0

v1 whole, which is shorter than its diff:
```python
import functools
import math

import jax
import jax.numpy as jnp
from jax import lax
from jax.experimental import pallas as pl
from jax.experimental.pallas import tpu as pltpu
from jax.sharding import PartitionSpec as P

BLOCKS, MICRO, TILES, DOWN = 16, 8, 16, 4
WIDTH, CH, GROUP = 128, 320, 10
CAT = 3 * CH
TAPS = 9 * CH
ROWS = 12
PIECE = 3 * CH
OWN = ROWS * CH
MEMBERS = float(48 * WIDTH * GROUP)
MIB = 1024 * 1024
LEAD = 2944
FULL = LEAD + 384
STATS = 48
BF, F32 = jnp.bfloat16, jnp.float32
ANY = pl.BlockSpec(memory_space=pl.ANY)
VM = pl.BlockSpec(memory_space=pltpu.VMEM)
SM = pl.BlockSpec(memory_space=pltpu.SMEM)
BOTH = ("segment", "tile")

PAIRS = ((0, 1), (2, 6), (3, 7), (4, 8), (5, 9), (10, 14), (11, 15), (12, 13))
FETCH_AFTER = {0: 3, 2: 4, 4: 5, 6: 6, 8: 7}
SWAP_AFTER = {0: 1, 1: 2, 2: 3, 3: 4, 6: 5, 8: 6, 10: 7}
GROUPS = ((2, 3, 4, 5, 6, 7), (8, 9, 10, 11), (0, 1, 12, 13, 14, 15))
SPREAD_AFTER = {9: 0, 13: 1}
COLUMN = {0: 4, 1: 5, 2: 1, 3: 5, 4: 2, 5: 6, 6: 3, 7: 7, 8: 4, 9: 1, 10: 5, 11: 6, 12: 6, 13: 2, 14: 7, 15: 0}


def place(slot, quarter):
    tile = (slot // 4) * 8 + 2 * (slot % 4) + (quarter in (1, 2))
    return (quarter // 2) * TILES + tile


def helper(block, slot, quarter):
    if block == BLOCKS - 1:
        return place(slot, quarter)
    segment = 2 * COLUMN[block] + slot // 4
    return segment * TILES + quarter // 2 * 8 + place(slot, quarter) % 8


def chunk_at(turn, k):
    return pl.multiple_of(lax.rem(k + turn, 4) * PIECE, PIECE)


def send_sums(info, totals, squares, source, near, cross, stats):
    ones = jnp.ones((8, WIDTH), F32)
    rows = jnp.concatenate(
        [
            lax.dot_general(
                ones,
                part,
                (((1,), (1,)), ((), ())),
                precision=lax.Precision.HIGHEST,
                preferred_element_type=F32,
            )[0:1]
            for part in (totals, squares)
        ],
        axis=0,
    )
    high = rows.astype(BF).astype(F32)
    left = rows - high
    middle = left.astype(BF).astype(F32)
    low = left - middle
    coded = jnp.concatenate([high, middle, low, jnp.zeros((10, CH), F32)], axis=0)
    coded = jnp.concatenate([coded, jnp.zeros((16, 64), F32)], axis=1).astype(BF)
    even = lax.rem(info[0], 2) == 0
    first, last = source[0:CH, :], source[OWN - CH : OWN, :]
    near[0:CH, :] = jnp.where(even, last, first)
    cross[0:CH, :] = jnp.where(even, first, last)
    for i in range(3):
        part = coded[:, i * 128 : (i + 1) * 128]
        near[CH + 16 * i : CH + 16 * (i + 1), :] = part
        cross[CH + 16 * i : CH + 16 * (i + 1), :] = part
        stats[16 * i : 16 * (i + 1), :] = part


def first_body(info, *refs):
    pieces, (near, cross, stats, whole), (xs, sem) = refs[:4], refs[4:8], refs[8:]

    @pl.when(info[2] == 1)
    def _():
        copies = [
            pltpu.make_async_copy(pieces[k], xs.at[pl.ds(chunk_at(info[1], k), PIECE)], sem.at[k])
            for k in range(4)
        ]
        for copy in copies:
            copy.start()
        for copy in copies:
            copy.wait()
        final = pltpu.make_async_copy(xs, whole, sem.at[0])
        final.start()
        totals = squares = jnp.zeros((CH, WIDTH), F32)
        for r in range(ROWS):
            row = xs[r * CH : (r + 1) * CH, :].astype(F32)
            totals, squares = totals + row, squares + row * row
        send_sums(info, totals, squares, xs, near, cross, stats)
        final.wait()


def block_body(at_core, next_core, up_in, up_out, last, info, *refs):
    refs = list(refs)

    def take(n):
        got = refs[:n]
        del refs[:n]
        return got

    source, near, cross, own_stats, far_stats, member = take(6)
    weights = take(2)
    if up_in:
        lateral_edges = take(2)
    if up_out:
        (lateral,), nexts = take(1), take(2)
    if last:
        passing = take(last)
    wholes = take(4 if last else 1)
    if not last:
        near_out, cross_out, stats_out = take(3)
    if up_out:
        (summed_out,) = take(1)
    xs, ws, cat, result, totals, squares, in_sem, w_sem, out_sem = take(9)
    if up_in:
        (sk_in,) = take(1)
    if up_out:
        ls, sk, sums, l_sem = take(4)

    @pl.when(info[2] == 1)
    def _():
        core = info[0] // 2
        x_copy = pltpu.make_async_copy(source, xs, in_sem.at[0])
        x_copy.start()
        lead, tail = pl.ds(0, LEAD), pl.ds(LEAD, FULL - LEAD)
        for at in range(2):

            @pl.when((core == at_core) == (at == 0))
            def _():
                pltpu.make_async_copy(weights[at].at[:, lead], ws, w_sem.at[0]).start()
                if up_in:
                    pltpu.make_async_copy(weights[at].at[:, tail], sk_in, w_sem.at[1]).start()

        if up_out:
            lateral_copy = pltpu.make_async_copy(lateral, ls, l_sem.at[0])
            lateral_copy.start()
            for at in range(2):

                @pl.when((core == next_core) == (at == 0))
                def _():
                    pltpu.make_async_copy(nexts[at].at[:, tail], sk, l_sem.at[1]).start()

        coded = [jnp.concatenate([ref[a + 16 * i : a + 16 * i + 16, :] for i in range(3)], axis=1)
                 for ref, a in ((own_stats, 0), (far_stats, 0), (near, CH), (cross, CH))]
        coded = jnp.concatenate(coded, axis=0)[:, 0:CH]
        groups = lax.dot_general(
            member[...], coded, (((1,), (1,)), ((), ())), preferred_element_type=F32
        )
        kind = lax.rem(lax.broadcasted_iota(jnp.int32, (CH, 64), 1), 16)
        even_kind = lax.rem(kind, 2) == 0
        mean = jnp.sum(jnp.where(even_kind, groups, 0.0), axis=1, keepdims=True) / MEMBERS
        mean_sq = jnp.sum(jnp.where(even_kind, 0.0, groups), axis=1, keepdims=True) / MEMBERS
        variance = jnp.maximum(mean_sq - mean * mean, 0.0)
        pltpu.make_async_copy(weights[0].at[:, lead], ws, w_sem.at[0]).wait()
        tailing = ws[:, TAPS : TAPS + 64].astype(F32)
        params = tailing[:, 0:16] + tailing[:, 16:32] + tailing[:, 32:48]
        lane = lax.broadcasted_iota(jnp.int32, (CH, 16), 1)
        shift = jnp.sum(jnp.where(lane == info[1] + 8, params, 0.0), axis=1, keepdims=True)
        wide = (CH, WIDTH)
        gain = jnp.broadcast_to(params[:, 0:1] * lax.rsqrt(variance + 1e-5) * 0.5, wide)
        bias = jnp.broadcast_to(params[:, 1:2] * 0.5, wide)
        mean = jnp.broadcast_to(mean, wide)
        shift = jnp.broadcast_to(shift, wide)
        column = lax.broadcasted_iota(jnp.int32, wide, 1)

        def lift(x, row, keep=None):
            h = (x - mean) * gain + bias
            lifted = h * jnp.tanh(h) + h + shift
            if keep is not None:
                lifted = jnp.where(keep, lifted, 0.0)
            left = jnp.where(column == 0, 0.0, pltpu.roll(lifted, 1, 1)).astype(BF)
            right = jnp.where(column == WIDTH - 1, 0.0, pltpu.roll(lifted, WIDTH - 1, 1)).astype(BF)
            cols = pl.ds(row * WIDTH, WIDTH)
            if not isinstance(row, int):
                cols = pl.ds(pl.multiple_of(row * WIDTH, WIDTH), WIDTH)
            cat[0:CH, cols] = left
            cat[CH : 2 * CH, cols] = lifted.astype(BF)
            cat[2 * CH : 3 * CH, cols] = right

        even = lax.rem(info[0], 2) == 0
        near_rows, cross_rows = near[0:CH, :].astype(F32), cross[0:CH, :].astype(F32)
        if up_in:
            pltpu.make_async_copy(weights[0].at[:, tail], sk_in, w_sem.at[1]).wait()
            skip_in = sk_in[:, 0:CH]
            near_rows, cross_rows = (
                rows + jnp.dot(skip_in, edge[0:CH, :], preferred_element_type=F32)
                for rows, edge in zip((near_rows, cross_rows), lateral_edges)
            )
        lift(jnp.where(even, cross_rows, near_rows), 0, info[0] > 0)
        lift(jnp.where(even, near_rows, cross_rows), ROWS + 1, info[0] < 3)
        x_copy.wait()

        def own_row(r):
            return pl.ds(pl.multiple_of(r * CH, CH), CH)

        @pl.loop(0, ROWS)
        def _(r):
            lift(xs[own_row(r), :].astype(F32), r + 1)

        if up_out:
            lateral_copy.wait()
            pltpu.make_async_copy(nexts[0].at[:, tail], sk, l_sem.at[1]).wait()
            skip = sk[:, 0:CH]
        totals[...] = jnp.zeros(wide, F32)
        squares[...] = jnp.zeros(wide, F32)

        @pl.loop(0, ROWS // 2)
        def _(pair):
            convolved = sum(
                jnp.dot(
                    ws[:, dy * CAT : (dy + 1) * CAT],
                    cat[:, pl.ds(pl.multiple_of((2 * pair + dy) * WIDTH, WIDTH), 2 * WIDTH)],
                    preferred_element_type=F32,
                )
                for dy in range(3)
            )
            rows = [own_row(2 * pair), own_row(2 * pair + 1)]
            if up_out:
                both = jnp.concatenate([ls[row, :] for row in rows], axis=1)
                projected = jnp.dot(skip, both, preferred_element_type=F32)
            for half, row in enumerate(rows):
                cols = slice(half * WIDTH, (half + 1) * WIDTH)
                kept = (xs[row, :].astype(F32) + convolved[:, cols]).astype(BF)
                result[row, :] = kept
                if not last:
                    following = kept.astype(F32)
                    if up_out:
                        following = following + projected[:, cols]
                        sums[row, :] = following
                    totals[...] += following
                    squares[...] += following * following

        if last:
            finals = [
                pltpu.make_async_copy(
                    result.at[pl.ds(chunk_at(info[1], k), PIECE)], wholes[k], out_sem.at[k]
                )
                for k in range(4)
            ]
        else:
            finals = [pltpu.make_async_copy(result, wholes[0], out_sem.at[0])]
        if up_out:
            finals.append(pltpu.make_async_copy(sums, summed_out, out_sem.at[1]))
        for copy in finals:
            copy.start()
        if not last:
            send_sums(info, totals[...], squares[...], result, near_out, cross_out, stats_out)
        for copy in finals:
            copy.wait()

    if last:
        hand_on(info, passing, wholes, result, in_sem, out_sem)


def hand_on(info, passing, outs, held, in_sem, out_sem):
    for at, ref in enumerate(passing):

        @pl.when(info[3] == at)
        def _():
            arrive = pltpu.make_async_copy(ref, held, in_sem.at[0])
            arrive.start()
            arrive.wait()
            copies = [
                pltpu.make_async_copy(
                    held.at[pl.ds(chunk_at(info[4], k), PIECE)], outs[k], out_sem.at[k]
                )
                for k in range(4)
            ]
            for copy in copies:
                copy.start()
            for copy in copies:
                copy.wait()


EXCHANGED = [
    jax.ShapeDtypeStruct((CH + STATS, WIDTH), BF),
    jax.ShapeDtypeStruct((CH + STATS, WIDTH), BF),
    jax.ShapeDtypeStruct((STATS, WIDTH), BF),
]
WHOLE = jax.ShapeDtypeStruct((OWN, WIDTH), BF)
PART = jax.ShapeDtypeStruct((PIECE, WIDTH), BF)


def first_call(info, pieces):
    return pl.pallas_call(
        first_body,
        out_shape=EXCHANGED + [WHOLE],
        in_specs=[SM] + [ANY] * 4,
        out_specs=[VM] * 3 + [ANY],
        scratch_shapes=[pltpu.VMEM((OWN, WIDTH), BF), pltpu.SemaphoreType.DMA((4,))],
        compiler_params=pltpu.CompilerParams(vmem_limit_bytes=16 * MIB),
        name="first_sums",
    )(info, *pieces)


def block_call(cores, info, source, exchanged, member, weights, lateral_edges, lateral, nexts, passing):
    up_in, up_out, last = lateral_edges is not None, lateral is not None, len(passing)
    operands = [source, *exchanged, member, *weights]
    specs = [ANY] + [VM] * 5 + [ANY] * 2
    shapes, out_specs = [WHOLE] + EXCHANGED, [ANY] + [VM] * 3
    if last:
        shapes, out_specs = [PART] * 4, [ANY] * 4
    scratch = [
        pltpu.VMEM((OWN, WIDTH), F32 if up_in else BF),
        pltpu.VMEM((CH, LEAD), BF),
        pltpu.VMEM((CAT, (ROWS + 2) * WIDTH), BF),
        pltpu.VMEM((OWN, WIDTH), BF),
        pltpu.VMEM((CH, WIDTH), F32),
        pltpu.VMEM((CH, WIDTH), F32),
        pltpu.SemaphoreType.DMA((1,)),
        pltpu.SemaphoreType.DMA((2,)),
        pltpu.SemaphoreType.DMA((4,)),
    ]
    if up_in:
        operands += list(lateral_edges)
        specs += [VM] * 2
        scratch.append(pltpu.VMEM((CH, FULL - LEAD), BF))
    if up_out:
        operands += [lateral, *nexts]
        specs += [ANY] * 3
        shapes = shapes + [jax.ShapeDtypeStruct((OWN, WIDTH), F32)]
        out_specs = out_specs + [ANY]
        scratch += [
            pltpu.VMEM((OWN, WIDTH), BF),
            pltpu.VMEM((CH, FULL - LEAD), BF),
            pltpu.VMEM((OWN, WIDTH), F32),
            pltpu.SemaphoreType.DMA((2,)),
        ]
    operands += passing
    specs += [ANY] * last
    out = pl.pallas_call(
        functools.partial(block_body, *cores, up_in, up_out, last),
        out_shape=shapes,
        in_specs=[SM] + specs,
        out_specs=out_specs,
        scratch_shapes=scratch,
        compiler_params=pltpu.CompilerParams(vmem_limit_bytes=40 * MIB),
        cost_estimate=pl.CostEstimate(
            flops=2 * OWN * WIDTH * TAPS, bytes_accessed=4 * MIB, transcendentals=OWN * WIDTH
        ),
        name="res_block",
    )(info, *operands)
    if last:
        return out, None, None
    return out[0], out[1:4], out[4] if up_out else None


def split_body(count, info, *refs):
    hand_on(info, refs[:count], refs[count : count + 4], *refs[count + 4 :])


def split(info, wholes):
    return pl.pallas_call(
        functools.partial(split_body, len(wholes)),
        out_shape=[PART] * 4,
        in_specs=[SM] + [ANY] * len(wholes),
        out_specs=[ANY] * 4,
        scratch_shapes=[
            pltpu.VMEM((OWN, WIDTH), BF),
            pltpu.SemaphoreType.DMA((1,)),
            pltpu.SemaphoreType.DMA((4,)),
        ],
        compiler_params=pltpu.CompilerParams(vmem_limit_bytes=16 * MIB),
        name="split",
    )(info, *wholes)


def collect_body(groups, info, *refs):
    out, held, in_sem, out_sem = refs[-4:]
    for at in range(groups):

        @pl.when(info[0] == at)
        def _():
            copies = []
            for k in range(4):
                for high in range(2):
                    slot, n = 4 * high + lax.rem(info[1] + 4 - k, 4), 2 * k + high
                    copies.append(
                        (
                            pltpu.make_async_copy(refs[at * 8 + n], held.at[n], in_sem.at[n]),
                            pltpu.make_async_copy(held.at[n], out.at[slot], out_sem.at[n]),
                        )
                    )
            for arrive, _ in copies:
                arrive.start()
            for arrive, leave in copies:
                arrive.wait()
                leave.start()
            for _, leave in copies:
                leave.wait()


def collect(info, received):
    flat = [piece for group in received for piece in group]
    return pl.pallas_call(
        functools.partial(collect_body, len(received)),
        out_shape=jax.ShapeDtypeStruct((MICRO, PIECE, WIDTH), BF),
        in_specs=[SM] + [ANY] * len(flat),
        out_specs=ANY,
        scratch_shapes=[
            pltpu.VMEM((MICRO, PIECE, WIDTH), BF),
            pltpu.SemaphoreType.DMA((8,)),
            pltpu.SemaphoreType.DMA((8,)),
        ],
        compiler_params=pltpu.CompilerParams(vmem_limit_bytes=16 * MIB),
        name="collect",
    )(info, *flat)


def sinusoid(steps, half_width):
    rates = jnp.exp(-math.log(10000.0) * jnp.arange(half_width, dtype=F32) / half_width)
    angles = steps.astype(F32)[:, None] * rates[None, :]
    return jnp.concatenate([jnp.cos(angles), jnp.sin(angles)], axis=-1)


def on_device(
    features, timesteps, plan, conv_weight, skip_weight, time_weight, norm_gain, norm_bias
):
    segment, tile = lax.axis_index("segment"), lax.axis_index("tile")
    core, odd = segment % 2, tile % 2
    quarter = jnp.where(odd == 1, 1 + core, 3 * core)
    slot = 4 * (tile // 8) + (tile % 8) // 2
    active = (segment < 2).astype(jnp.int32)
    passed = 4 * core + (tile % 8) // 2

    def info_for(group):
        pick = jnp.full((), -1, jnp.int32)
        for at, block in enumerate(group):
            if block < BLOCKS - 1:
                pick = jnp.where(segment // 2 == COLUMN[block], at, pick)
        return jnp.stack([quarter, slot, active, pick, passed]).astype(jnp.int32)

    info = info_for(())

    served = lax.dynamic_index_in_dim(
        features, plan[jnp.minimum(segment, MICRO - 1)], 0, keepdims=False
    )
    served = served.transpose(0, 2, 1).reshape(PIECE, WIDTH)
    pieces = []
    for k in range(4):
        route = [
            (j * TILES + 4 * q + (k + j) % 4, place(j, q)) for j in range(MICRO) for q in range(4)
        ]
        pieces.append(lax.ppermute(served, BOTH, route))

    encoded = sinusoid(timesteps[plan], time_weight.shape[1] // 2)
    shifts = jnp.dot(encoded, time_weight[0], precision=lax.Precision.HIGHEST)
    params = jnp.concatenate([norm_gain, norm_bias, jnp.zeros((6, CH), F32), shifts], axis=0)
    high = lax.reduce_precision(params, 8, 7)
    left = params - high
    middle = lax.reduce_precision(left, 8, 7)
    coded = jnp.concatenate([high, middle, left - middle], axis=0).astype(BF)
    columns = [conv_weight[0].T, coded.T, jnp.zeros((CH, LEAD - TAPS - STATS), BF)]
    lead = jnp.concatenate(columns, axis=1)
    columns += [skip_weight[0].T, jnp.zeros((CH, FULL - LEAD - CH), BF)]
    full = jnp.concatenate(columns, axis=1)
    first_up = BLOCKS - DOWN

    def fetch(pair, after):
        own = full if max(pair) >= first_up else lead
        if after is not None:
            own, _ = lax.optimization_barrier((own, after))
        return lax.ppermute(own, "segment", [(pair[0], 0), (pair[1], 1)])

    def swap(value, mask):
        route = [(place(j, q), place(j, q ^ mask)) for j in range(MICRO) for q in range(4)]
        return lax.ppermute(value, BOTH, route)

    def hand_over(block, whole):
        route = [(place(j, q), helper(block, j, q)) for j in range(MICRO) for q in range(4)]
        return lax.ppermute(whole, BOTH, route)

    def spread(group, outs):
        got = []
        for k in range(4):
            for high in range(2):
                route = [
                    (helper(block, j, q), block * TILES + 4 * q + (k + j) % 4)
                    for block in group
                    for j in range(4 * high, 4 * high + 4)
                    for q in range(4)
                ]
                got.append(lax.ppermute(outs[k], BOTH, route))
        return got

    member_at = jnp.arange(CH) // GROUP
    member = (member_at[:, None] == member_at[None, :]).astype(BF)
    weights, cores, fetched = {}, {}, {}

    def swap_cores(index, own):
        both = own, lax.ppermute(own, "segment", [(0, 1), (1, 0)])
        for at, block in enumerate(PAIRS[index]):
            weights[block], cores[block] = both, at

    swap_cores(0, lead)
    for index in (1, 2):
        fetched[index] = fetch(PAIRS[index], None)
    *exchanged, source = first_call(info, pieces)
    wholes, edges_of, passing, received = [], {}, [], []
    for block in range(BLOCKS):
        up_in, up_out = block >= first_up, first_up - 1 <= block < BLOCKS - 1
        near, cross, stats = exchanged
        near_in, cross_in, far = swap(near, 1), swap(cross, 3), swap(stats, 2)
        edges_of[block] = (near_in, cross_in)
        if block >= 2:
            source, near_in, cross_in, far, passing[block - 2] = lax.optimization_barrier(
                (source, near_in, cross_in, far, passing[block - 2])
            )
        last = block == BLOCKS - 1
        whole, exchanged, summed = block_call(
            (cores[block], cores.get(block + 1, 0)),
            info_for(GROUPS[2]) if last else info,
            source,
            (near_in, cross_in, stats, far),
            member,
            weights[block],
            edges_of[BLOCKS - block] if up_in else None,
            wholes[BLOCKS - 2 - block] if up_out else None,
            weights[block + 1] if up_out else None,
            [passing[b] for b in GROUPS[2][:-1]] if last else [],
        )
        wholes.append(whole)
        source = summed if up_out else whole
        if not last:
            passing.append(hand_over(block, whole))
        if block in SPREAD_AFTER:
            group = GROUPS[SPREAD_AFTER[block]]
            outs = split(info_for(group), [passing[b] for b in group])
            received.append(spread(group, outs))
        if block in SWAP_AFTER:
            index = SWAP_AFTER[block]
            own, _ = lax.optimization_barrier((fetched[index], whole))
            swap_cores(index, own)
        if block in FETCH_AFTER:
            index = FETCH_AFTER[block]
            fetched[index] = fetch(PAIRS[index], whole)
    received.append(spread(GROUPS[2], whole))
    group_of = jnp.zeros((), jnp.int32)
    for at, group in enumerate(GROUPS):
        for block in group:
            group_of = jnp.where(segment == block, at, group_of)
    out = collect(jnp.stack([group_of, tile % 4]).astype(jnp.int32), received)
    out = out.reshape(1, MICRO, 3, CH, WIDTH)
    return out.transpose(0, 1, 2, 4, 3)


def solution(mesh):
    placed = (
        P(None, "tile", None, None),
        P(),
        P(),
        P("segment", None, None),
        P("segment", None, None),
        P("segment", None, None),
        P("segment", None),
        P("segment", None),
    )
    return jax.shard_map(
        on_device,
        mesh=mesh,
        in_specs=placed,
        out_specs=P("segment", None, "tile", None, None),
        check_vma=False,
    )
```

time: 1690 us -> 748 us (0.44)
  the two profiles are of different devices: /device:TPU:59 before, /device:TPU:33 now
where the time goes in v1:
time: 748 us; the launch traced here: 737 us
  starting transfers between devices  416 us (56%)
  Pallas kernels  169 us (23%)
  waiting for transfers between devices  79.7 us (11%)
  local copies, waits for them, and re-layouts  64.5 us (9%)
    ppermute x24, starting transfers between devices, spread(): got.append(lax.ppermute(outs[k], BOTH, route))  208 us
    pallas_call x16, Pallas kernels, block_call(): pl.pallas_call(functools.partial(block_body, *cores, up_in, up_out, last)...  160 us
    ppermute x48, starting transfers between devices, swap(): return lax.ppermute(value, BOTH, route)  140 us
    unnamed x203, local copies, waits for them, and re-layouts  52.8 us
    ppermute x48, waiting for transfers between devices, swap(): return lax.ppermute(value, BOTH, route)  38 us
    ppermute x15, starting transfers between devices, hand_over(): return lax.ppermute(whole, BOTH, route)  22.1 us
    ppermute x8, starting transfers between devices, swap_cores(): both = (own, lax.ppermute(own, 'segment', [(0, 1), (1, 0)]))  20.5 us
    ppermute x4, waiting for transfers between devices, on_device(): pieces.append(lax.ppermute(served, BOTH, route))  20.4 us
  transfers between devices with their start and end apart: 106, of which 30 were waited for; matrix products, arithmetic and copies ran while one was open for 1% of the time, Pallas kernels for 22%

profile of v1, /device:TPU:33, one launch (start us, length us, event | category | flops | bytes accessed | tf_op | source)
XLA Modules:
  0.0 736.5 jit_solution(8341937314468370322)
XLA Ops:
  18.9 10.2 %collective-permute-done.3.refs_3_ = bf16[960,128]{1,0:T(8,128)(2,1)S(1)} collective-permute-done((bf16[960,128]{1,0:T(8,128)(2,1)S(1)}, bf16[960,128]{1,0:T(8,128)(2,1)S(1)}, u32[]{:S(2)}, u32[]{:S(2)}) %collective-permute-start.3) | collective-permute-done | bytes 245792 | tf_op jit(solution)/shard_map/ppermute | solution.py:459
  31.7 9.7 %collective-permute-done.refs_0_ = bf16[960,128]{1,0:T(8,128)(2,1)S(1)} collective-permute-done((bf16[960,128]{1,0:T(8,128)(2,1)S(1)}, bf16[960,128]{1,0:T(8,128)(2,1)S(1)}, u32[]{:S(2)}, u32[]{:S(2)}) %collective-permute-start) | collective-permute-done | bytes 245792 | tf_op jit(solution)/shard_map/ppermute | solution.py:459
  46.1 12.7 %collective-permute-start.4 = (bf16[368,128]{1,0:T(8,128)(2,1)S(1)}, bf16[368,128]{1,0:T(8,128)(2,1)S(1)}, u32[]{:S(2)}, u32[]{:S(2)}) collective-permute-start(bf16[368,128]{1,0:T(8,128)(2,1)S(1)} %get-tuple-element.168), channel_id=1, source_target_pairs={{0,1},{1,0},{17,16},{16,17},{2,3},{3,2},{19,18},{18,19},{4,5},{5,4... | collective-permute-start | bytes 282632 | tf_op jit(solution)/shard_map/ppermute | solution.py:482
  62.6 10.2 %res_block.16 = (bf16[3840,128]{1,0:T(8,128)(2,1)S(1)}, bf16[368,128]{1,0:T(8,128)(2,1)S(1)}, bf16[368,128]{1,0:T(8,128)(2,1)S(1)}, bf16[48,128]{1,0:T(8,128)(2,1)S(1)}) custom-call(s32[5]{0:T(128)S(1)} %stack.67.info, bf16[3840,128]{1,0:T(8,128)(2,1)S(1)} %get-tuple-element.167.refs_0_, bf16[368,128]{1,0:T(8,128)(2,1)S(1)} %collective-permute-done.4.refs_1_, ...), custom_call_target="tpu_custom_call" | custom-call | flops 2831155200 | bytes 4194304 | tf_op jit(solution)/shard_map/res_block/pallas_call | solution.py:346
  93.7 10.2 %res_block.17 = (bf16[3840,128]{1,0:T(8,128)(2,1)S(1)}, bf16[368,128]{1,0:T(8,128)(2,1)S(1)}, bf16[368,128]{1,0:T(8,128)(2,1)S(1)}, bf16[48,128]{1,0:T(8,128)(2,1)S(1)}) custom-call(s32[5]{0:T(128)S(1)} %stack.67.info, bf16[3840,128]{1,0:T(8,128)(2,1)S(1)} %get-tuple-element.171.refs_0_.refs_10_, ...), custom_call_target="tpu_custom_call" | custom-call | flops 2831155200 | bytes 4194304 | tf_op jit(solution)/shard_map/res_block/pallas_call | solution.py:346
  179.2 9.7 %res_block.20 = (bf16[3840,128]{1,0:T(8,128)(2,1)}, bf16[368,128]{1,0:T(8,128)(2,1)S(1)}, bf16[368,128]{1,0:T(8,128)(2,1)S(1)}, bf16[48,128]{1,0:T(8,128)(2,1)S(1)}) custom-call(s32[5]{0:T(128)S(1)} %stack.67.info, bf16[3840,128]{1,0:T(8,128)(2,1)} %get-tuple-element.198.refs_0_.refs_8_, bf16[368,128]{1,0:T(8,128)(2,1)S(1)} %collective-permute-done.23.refs_1_.refs_8_, ...), custom_call_target="tpu_custom_call" | custom-call | flops 2831155200 | bytes 4194304 | tf_op jit(solution)/shard_map/res_block/pallas_call | solution.py:346
  210.2 10.2 %res_block.21 = (bf16[3840,128]{1,0:T(8,128)(2,1)S(1)}, bf16[368,128]{1,0:T(8,128)(2,1)S(1)}, bf16[368,128]{1,0:T(8,128)(2,1)S(1)}, bf16[48,128]{1,0:T(8,128)(2,1)S(1)}) custom-call(s32[5]{0:T(128)S(1)} %stack.67.info, bf16[3840,128]{1,0:T(8,128)(2,1)} %get-tuple-element.209.refs_0_, bf16[368,128]{1,0:T(8,128)(2,1)S(1)} %collective-permute-done.29.refs_1_, ...), custom_call_target="tpu_custom_call" | custom-call | flops 2831155200 | bytes 4194304 | tf_op jit(solution)/shard_map/res_block/pallas_call | solution.py:346
  233.1 10.2 %res_block.22 = (bf16[3840,128]{1,0:T(8,128)(2,1)S(1)}, bf16[368,128]{1,0:T(8,128)(2,1)S(1)}, bf16[368,128]{1,0:T(8,128)(2,1)S(1)}, bf16[48,128]{1,0:T(8,128)(2,1)S(1)}) custom-call(s32[5]{0:T(128)S(1)} %stack.67.info, bf16[3840,128]{1,0:T(8,128)(2,1)S(1)} %get-tuple-element.220.refs_0_, bf16[368,128]{1,0:T(8,128)(2,1)S(1)} %collective-permute-done.35.refs_1_, ...), custom_call_target="tpu_custom_call" | custom-call | flops 2831155200 | bytes 4194304 | tf_op jit(solution)/shard_map/res_block/pallas_call | solution.py:346
  284.4 11.0 %collective-permute-start.71 = (bf16[320,3328]{1,0:T(8,128)(2,1)S(1)}, bf16[320,3328]{1,0:T(8,128)(2,1)S(1)}, u32[]{:S(2)}, u32[]{:S(2)}) collective-permute-start(bf16[320,3328]{1,0:T(8,128)(2,1)S(1)} %copy-done.97), channel_id=1, source_target_pairs={{192,0},{208,16},{193,1},{209,17},{194,2},{210,18},{195,3},{211,19... | collective-permute-start | bytes 6389768 | tf_op jit(solution)/shard_map/ppermute | solution.py:478
  313.2 10.2 %res_block.25 = (bf16[3840,128]{1,0:T(8,128)(2,1)S(1)}, bf16[368,128]{1,0:T(8,128)(2,1)S(1)}, bf16[368,128]{1,0:T(8,128)(2,1)S(1)}, bf16[48,128]{1,0:T(8,128)(2,1)S(1)}) custom-call(s32[5]{0:T(128)S(1)} %stack.67.info, bf16[3840,128]{1,0:T(8,128)(2,1)S(1)} %get-tuple-element.251.refs_0_, bf16[368,128]{1,0:T(8,128)(2,1)S(1)} %collective-permute-done.47.refs_1_, ...), custom_call_target="tpu_custom_call" | custom-call | flops 2831155200 | bytes 4194304 | tf_op jit(solution)/shard_map/res_block/pallas_call | solution.py:346
  370.0 10.1 %res_block.27 = (bf16[3840,128]{1,0:T(8,128)(2,1)S(1)}, bf16[368,128]{1,0:T(8,128)(2,1)S(1)}, bf16[368,128]{1,0:T(8,128)(2,1)S(1)}, bf16[48,128]{1,0:T(8,128)(2,1)S(1)}, f32[3840,128]{1,0:T(8,128)S(1)}) custom-call(s32[5]{0:T(128)S(1)} %stack.67.info, bf16[3840,128]{1,0:T(8,128)(2,1)S(1)} %get-tuple-element.271.refs_0_, ...), custom_call_target="tpu_custom_call" | custom-call | flops 2831155200 | bytes 4194304 | tf_op jit(solution)/shard_map/res_block/pallas_call | solution.py:346
  391.2 10.7 %res_block.28 = (bf16[3840,128]{1,0:T(8,128)(2,1)S(1)}, bf16[368,128]{1,0:T(8,128)(2,1)S(1)}, bf16[368,128]{1,0:T(8,128)(2,1)S(1)}, bf16[48,128]{1,0:T(8,128)(2,1)S(1)}, f32[3840,128]{1,0:T(8,128)S(1)}) custom-call(s32[5]{0:T(128)S(1)} %stack.67.info, f32[3840,128]{1,0:T(8,128)S(1)} %get-tuple-element.284.refs_0_, ...), custom_call_target="tpu_custom_call" | custom-call | flops 2831155200 | bytes 4194304 | tf_op jit(solution)/shard_map/res_block/pallas_call | solution.py:346
  415.1 10.8 %res_block.29 = (bf16[3840,128]{1,0:T(8,128)(2,1)}, bf16[368,128]{1,0:T(8,128)(2,1)S(1)}, bf16[368,128]{1,0:T(8,128)(2,1)S(1)}, bf16[48,128]{1,0:T(8,128)(2,1)S(1)}, f32[3840,128]{1,0:T(8,128)S(1)}) custom-call(s32[5]{0:T(128)S(1)} %stack.67.info, f32[3840,128]{1,0:T(8,128)S(1)} %get-tuple-element.298.refs_0_, ...), custom_call_target="tpu_custom_call" | custom-call | flops 2831155200 | bytes 4194304 | tf_op jit(solution)/shard_map/res_block/pallas_call | solution.py:346
  435.9 11.3 %res_block.30 = (bf16[3840,128]{1,0:T(8,128)(2,1)}, bf16[368,128]{1,0:T(8,128)(2,1)}, bf16[368,128]{1,0:T(8,128)(2,1)}, bf16[48,128]{1,0:T(8,128)(2,1)}, f32[3840,128]{1,0:T(8,128)S(1)}) custom-call(s32[5]{0:T(128)S(1)} %stack.67.info, f32[3840,128]{1,0:T(8,128)S(1)} %get-tuple-element.307.refs_0_, bf16[368,128]{1,0:T(8,128)(2,1)S(1)} %collective-permute-done.89.refs_1_, ...), custom_call_target="tpu_custom_call" | custom-call | flops 2831155200 | bytes 4194304 | tf_op jit(solution)/shard_map/res_block/pallas_call | solution.py:346
  458.7 24.6 %collective-permute-start.52 = (bf16[960,128]{1,0:T(8,128)(2,1)S(1)}, bf16[960,128]{1,0:T(8,128)(2,1)S(1)}, u32[]{:S(2)}, u32[]{:S(2)}) collective-permute-start(bf16[960,128]{1,0:T(8,128)(2,1)S(1)} %get-tuple-element.247), channel_id=1, source_target_pairs={{48,32},{49,36},{57,40},{56,44},{50,33},{51,37},{59,41},{58,45},{5... | collective-permute-start | bytes 737288 | tf_op jit(solution)/shard_map/ppermute | solution.py:498
  483.3 12.9 %collective-permute-start.51 = (bf16[960,128]{1,0:T(8,128)(2,1)S(1)}, bf16[960,128]{1,0:T(8,128)(2,1)S(1)}, u32[]{:S(2)}, u32[]{:S(2)}) collective-permute-start(bf16[960,128]{1,0:T(8,128)(2,1)S(1)} %get-tuple-element.247), channel_id=1, source_target_pairs={{32,32},{33,36},{41,40},{40,44},{34,33},{35,37},{43,41},{42,45},{3... | collective-permute-start | bytes 737288 | tf_op jit(solution)/shard_map/ppermute | solution.py:498
  496.2 13.1 %collective-permute-start.54 = (bf16[960,128]{1,0:T(8,128)(2,1)S(1)}, bf16[960,128]{1,0:T(8,128)(2,1)S(1)}, u32[]{:S(2)}, u32[]{:S(2)}) collective-permute-start(bf16[960,128]{1,0:T(8,128)(2,1)S(1)} %get-tuple-element.248), channel_id=1, source_target_pairs={{48,33},{49,37},{57,41},{56,45},{50,34},{51,38},{59,42},{58,46},{5... | collective-permute-start | bytes 737288 | tf_op jit(solution)/shard_map/ppermute | solution.py:498
  510.1 12.9 %collective-permute-start.53 = (bf16[960,128]{1,0:T(8,128)(2,1)S(1)}, bf16[960,128]{1,0:T(8,128)(2,1)S(1)}, u32[]{:S(2)}, u32[]{:S(2)}) collective-permute-start(bf16[960,128]{1,0:T(8,128)(2,1)S(1)} %get-tuple-element.248), channel_id=1, source_target_pairs={{32,33},{33,37},{41,41},{40,45},{34,34},{35,38},{43,42},{42,46},{3... | collective-permute-start | bytes 737288 | tf_op jit(solution)/shard_map/ppermute | solution.py:498
  523.7 13.1 %collective-permute-start.56 = (bf16[960,128]{1,0:T(8,128)(2,1)}, bf16[960,128]{1,0:T(8,128)(2,1)S(1)}, u32[]{:S(2)}, u32[]{:S(2)}) collective-permute-start(bf16[960,128]{1,0:T(8,128)(2,1)} %get-tuple-element.249), channel_id=1, source_target_pairs={{48,34},{49,38},{57,42},{56,46},{50,35},{51,39},{59,43},{58,47},{5... | collective-permute-start | bytes 737288 | tf_op jit(solution)/shard_map/ppermute | solution.py:498
  554.6 11.7 %collective-permute-start.55 = (bf16[960,128]{1,0:T(8,128)(2,1)}, bf16[960,128]{1,0:T(8,128)(2,1)}, u32[]{:S(2)}, u32[]{:S(2)}) collective-permute-start(bf16[960,128]{1,0:T(8,128)(2,1)} %get-tuple-element.249), channel_id=1, source_target_pairs={{32,34},{33,38},{41,42},{40,46},{34,35},{35,39},{43,43},{42,47},{3... | collective-permute-start | bytes 737288 | tf_op jit(solution)/shard_map/ppermute | solution.py:498
  566.2 15.4 %collective-permute-start.58 = (bf16[960,128]{1,0:T(8,128)(2,1)}, bf16[960,128]{1,0:T(8,128)(2,1)}, u32[]{:S(2)}, u32[]{:S(2)}) collective-permute-start(bf16[960,128]{1,0:T(8,128)(2,1)} %get-tuple-element.250), channel_id=1, source_target_pairs={{48,35},{49,39},{57,43},{56,47},{50,32},{51,36},{59,40},{58,44},{5... | collective-permute-start | bytes 737288 | tf_op jit(solution)/shard_map/ppermute | solution.py:498
  581.7 13.3 %collective-permute-start.57 = (bf16[960,128]{1,0:T(8,128)(2,1)}, bf16[960,128]{1,0:T(8,128)(2,1)}, u32[]{:S(2)}, u32[]{:S(2)}) collective-permute-start(bf16[960,128]{1,0:T(8,128)(2,1)} %get-tuple-element.250), channel_id=1, source_target_pairs={{32,35},{33,39},{41,43},{40,47},{34,32},{35,36},{43,40},{42,44},{3... | collective-permute-start | bytes 737288 | tf_op jit(solution)/shard_map/ppermute | solution.py:498
  605.4 10.4 %res_block.31 = (bf16[960,128]{1,0:T(8,128)(2,1)S(1)}, bf16[960,128]{1,0:T(8,128)(2,1)}, bf16[960,128]{1,0:T(8,128)(2,1)}, bf16[960,128]{1,0:T(8,128)(2,1)}) custom-call(s32[5]{0:T(128)S(1)} %stack.71.info, f32[3840,128]{1,0:T(8,128)S(1)} %copy-done.9, bf16[368,128]{1,0:T(8,128)(2,1)} %collective-permute-done.93.refs_1_, ...), custom_call_target="tpu_custom_call" | custom-call | flops 2831155200 | bytes 4194304 | tf_op jit(solution)/shard_map/res_block/pallas_call | solution.py:346
  619.3 26.3 %collective-permute-start.99 = (bf16[960,128]{1,0:T(8,128)(2,1)S(1)}, bf16[960,128]{1,0:T(8,128)(2,1)S(1)}, u32[]{:S(2)}, u32[]{:S(2)}) collective-permute-start(bf16[960,128]{1,0:T(8,128)(2,1)S(1)} %get-tuple-element.325), channel_id=1, source_target_pairs={{144,0},{145,4},{153,8},{152,12},{146,1},{147,5},{155,9},{154,13},... | collective-permute-start | bytes 737288 | tf_op jit(solution)/shard_map/ppermute | solution.py:498
  (436 shorter events, 431.3 us)
Async XLA Ops:
  8.6 54.0 %collective-permute-start.7 = (bf16[320,2944]{1,0:T(8,128)(2,1)}, bf16[320,2944]{1,0:T(8,128)(2,1)}, u32[]{:S(2)}, u32[]{:S(2)}) collective-permute-start(bf16[320,2944]{1,0:T(8,128)(2,1)} %concatenate.19.refs_6_), channel_id=1, source_target_pairs={{0,16},{16,0},{1,17},{17,1},{2,18},{18,2},{3,19},{19,3},{4,20},{20... | collective-permute-start | bytes 5652488 | tf_op jit(solution)/shard_map/ppermute | solution.py:506
  11.2 61.7 %collective-permute-start.15 = (bf16[320,2944]{1,0:T(8,128)(2,1)}, bf16[320,2944]{1,0:T(8,128)(2,1)}, u32[]{:S(2)}, u32[]{:S(2)}) collective-permute-start(bf16[320,2944]{1,0:T(8,128)(2,1)} %concatenate.19.refs_6_), channel_id=1, source_target_pairs={{32,0},{96,16},{33,1},{97,17},{34,2},{98,18},{35,3},{99,19},{36,4}... | collective-permute-start | bytes 5652488 | tf_op jit(solution)/shard_map/ppermute | solution.py:478
  61.3 46.1 %collective-permute-start.21 = (bf16[320,2944]{1,0:T(8,128)(2,1)}, bf16[320,2944]{1,0:T(8,128)(2,1)S(1)}, u32[]{:S(2)}, u32[]{:S(2)}) collective-permute-start(bf16[320,2944]{1,0:T(8,128)(2,1)} %concatenate.19.refs_6_), channel_id=1, source_target_pairs={{48,0},{112,16},{49,1},{113,17},{50,2},{114,18},{51,3},{115,19},{5... | collective-permute-start | bytes 5652488 | tf_op jit(solution)/shard_map/ppermute | solution.py:478
  72.8 43.1 %collective-permute-start.16 = (bf16[320,2944]{1,0:T(8,128)(2,1)}, bf16[320,2944]{1,0:T(8,128)(2,1)S(1)}, u32[]{:S(2)}, u32[]{:S(2)}) collective-permute-start(bf16[320,2944]{1,0:T(8,128)(2,1)} %collective-permute-done.15.refs_6_), channel_id=1, source_target_pairs={{0,16},{16,0},{1,17},{17,1},{2,18},{18,2},{3,19},{19,3},{4,20},{20... | collective-permute-start | bytes 5652488 | tf_op jit(solution)/shard_map/ppermute | solution.py:506
  77.3 50.6 %collective-permute-start.27 = (bf16[320,2944]{1,0:T(8,128)(2,1)}, bf16[320,2944]{1,0:T(8,128)(2,1)S(1)}, u32[]{:S(2)}, u32[]{:S(2)}) collective-permute-start(bf16[320,2944]{1,0:T(8,128)(2,1)} %concatenate.19.refs_6_), channel_id=1, source_target_pairs={{64,0},{128,16},{65,1},{129,17},{66,2},{130,18},{67,3},{131,19},{6... | collective-permute-start | bytes 5652488 | tf_op jit(solution)/shard_map/ppermute | solution.py:478
  127.9 51.3 %collective-permute-start.28 = (bf16[320,2944]{1,0:T(8,128)(2,1)S(1)}, bf16[320,2944]{1,0:T(8,128)(2,1)S(1)}, u32[]{:S(2)}, u32[]{:S(2)}) collective-permute-start(bf16[320,2944]{1,0:T(8,128)(2,1)S(1)} %collective-permute-done.27.refs_6_), channel_id=1, source_target_pairs={{0,16},{16,0},{1,17},{17,1},{2,18},{18,2},{3,19},{19,3},{4,20},{20... | collective-permute-start | bytes 5652488 | tf_op jit(solution)/shard_map/ppermute | solution.py:506
  163.0 47.2 %collective-permute-start.34 = (bf16[320,2944]{1,0:T(8,128)(2,1)}, bf16[320,2944]{1,0:T(8,128)(2,1)}, u32[]{:S(2)}, u32[]{:S(2)}) collective-permute-start(bf16[320,2944]{1,0:T(8,128)(2,1)} %collective-permute-done.33.refs_6_), channel_id=1, source_target_pairs={{0,16},{16,0},{1,17},{17,1},{2,18},{18,2},{3,19},{19,3},{4,20},{20... | collective-permute-start | bytes 5652488 | tf_op jit(solution)/shard_map/ppermute | solution.py:506
  199.9 70.8 %collective-permute-start.63 = (bf16[320,3328]{1,0:T(8,128)(2,1)}, bf16[320,3328]{1,0:T(8,128)(2,1)S(1)}, u32[]{:S(2)}, u32[]{:S(2)}) collective-permute-start(bf16[320,3328]{1,0:T(8,128)(2,1)} %concatenate.20), channel_id=1, source_target_pairs={{160,0},{224,16},{161,1},{225,17},{162,2},{226,18},{163,3},{227,19... | collective-permute-start | bytes 6389768 | tf_op jit(solution)/shard_map/ppermute | solution.py:478
  270.7 64.8 %collective-permute-start.69 = (bf16[320,3328]{1,0:T(8,128)(2,1)S(1)}, bf16[320,3328]{1,0:T(8,128)(2,1)S(1)}, u32[]{:S(2)}, u32[]{:S(2)}) collective-permute-start(bf16[320,3328]{1,0:T(8,128)(2,1)S(1)} %copy-done.97), channel_id=1, source_target_pairs={{176,0},{240,16},{177,1},{241,17},{178,2},{242,18},{179,3},{243,19... | collective-permute-start | bytes 6389768 | tf_op jit(solution)/shard_map/ppermute | solution.py:478
  273.2 64.6 %collective-permute-start.64 = (bf16[320,3328]{1,0:T(8,128)(2,1)S(1)}, bf16[320,3328]{1,0:T(8,128)(2,1)S(1)}, u32[]{:S(2)}, u32[]{:S(2)}) collective-permute-start(bf16[320,3328]{1,0:T(8,128)(2,1)S(1)} %collective-permute-done.63.refs_6_.refs_11_), channel_id=1, source_target_pairs={{0,16},{16,0},{1,17},{17,1},{2,18},{18,2},{3,19},{19,3},{4,20},{20... | collective-permute-start | bytes 6389768 | tf_op jit(solution)/shard_map/ppermute | solution.py:506
  284.4 62.6 %collective-permute-start.71 = (bf16[320,3328]{1,0:T(8,128)(2,1)S(1)}, bf16[320,3328]{1,0:T(8,128)(2,1)S(1)}, u32[]{:S(2)}, u32[]{:S(2)}) collective-permute-start(bf16[320,3328]{1,0:T(8,128)(2,1)S(1)} %copy-done.97), channel_id=1, source_target_pairs={{192,0},{208,16},{193,1},{209,17},{194,2},{210,18},{195,3},{211,19... | collective-permute-start | bytes 6389768 | tf_op jit(solution)/shard_map/ppermute | solution.py:478
  433.5 161.5 %collective-permute-start.96 = (bf16[3840,128]{1,0:T(8,128)(2,1)}, bf16[3840,128]{1,0:T(8,128)(2,1)}, u32[]{:S(2)}, u32[]{:S(2)}) collective-permute-start(bf16[3840,128]{1,0:T(8,128)(2,1)} %get-tuple-element.315), channel_id=1, source_target_pairs={{0,64},{1,65},{17,73},{16,72},{2,66},{3,67},{19,75},{18,74},{4,68}... | collective-permute-start | bytes 2949128 | tf_op jit(solution)/shard_map/ppermute | solution.py:486
  448.5 150.7 %collective-permute-start.97 = (bf16[3840,128]{1,0:T(8,128)(2,1)}, bf16[3840,128]{1,0:T(8,128)(2,1)}, u32[]{:S(2)}, u32[]{:S(2)}) collective-permute-start(bf16[3840,128]{1,0:T(8,128)(2,1)} %get-tuple-element.324), channel_id=1, source_target_pairs={{0,224},{1,225},{17,233},{16,232},{2,226},{3,227},{19,235},{18,234... | collective-permute-start | bytes 2949128 | tf_op jit(solution)/shard_map/ppermute | solution.py:486
  458.7 50.6 %collective-permute-start.52 = (bf16[960,128]{1,0:T(8,128)(2,1)S(1)}, bf16[960,128]{1,0:T(8,128)(2,1)S(1)}, u32[]{:S(2)}, u32[]{:S(2)}) collective-permute-start(bf16[960,128]{1,0:T(8,128)(2,1)S(1)} %get-tuple-element.247), channel_id=1, source_target_pairs={{48,32},{49,36},{57,40},{56,44},{50,33},{51,37},{59,41},{58,45},{5... | collective-permute-start | bytes 737288 | tf_op jit(solution)/shard_map/ppermute | solution.py:498
  540.1 41.5 %collective-permute-start.94 = (bf16[368,128]{1,0:T(8,128)(2,1)}, bf16[368,128]{1,0:T(8,128)(2,1)}, u32[]{:S(2)}, u32[]{:S(2)}) collective-permute-start(bf16[368,128]{1,0:T(8,128)(2,1)} %get-tuple-element.313), channel_id=1, source_target_pairs={{0,16},{1,17},{17,1},{16,0},{2,18},{3,19},{19,3},{18,2},{4,20},{5,... | collective-permute-start | bytes 282632 | tf_op jit(solution)/shard_map/ppermute | solution.py:482
  554.6 41.9 %collective-permute-start.55 = (bf16[960,128]{1,0:T(8,128)(2,1)}, bf16[960,128]{1,0:T(8,128)(2,1)}, u32[]{:S(2)}, u32[]{:S(2)}) collective-permute-start(bf16[960,128]{1,0:T(8,128)(2,1)} %get-tuple-element.249), channel_id=1, source_target_pairs={{32,34},{33,38},{41,42},{40,46},{34,35},{35,39},{43,43},{42,47},{3... | collective-permute-start | bytes 737288 | tf_op jit(solution)/shard_map/ppermute | solution.py:498
  598.5 47.2 %collective-permute-start.86 = (bf16[960,128]{1,0:T(8,128)(2,1)}, bf16[960,128]{1,0:T(8,128)(2,1)S(1)}, u32[]{:S(2)}, u32[]{:S(2)}) collective-permute-start(bf16[960,128]{1,0:T(8,128)(2,1)} %copy-done.92), channel_id=1, source_target_pairs={{144,130},{145,134},{153,138},{152,142},{146,131},{147,135},{155,1... | collective-permute-start | bytes 737288 | tf_op jit(solution)/shard_map/ppermute | solution.py:498
  599.2 54.2 %collective-permute-start.85 = (bf16[960,128]{1,0:T(8,128)(2,1)}, bf16[960,128]{1,0:T(8,128)(2,1)S(1)}, u32[]{:S(2)}, u32[]{:S(2)}) collective-permute-start(bf16[960,128]{1,0:T(8,128)(2,1)} %copy-done.92), channel_id=1, source_target_pairs={{128,130},{129,134},{137,138},{136,142},{130,131},{131,135},{139,1... | collective-permute-start | bytes 737288 | tf_op jit(solution)/shard_map/ppermute | solution.py:498
  616.6 47.1 %collective-permute-start.88 = (bf16[960,128]{1,0:T(8,128)(2,1)S(1)}, bf16[960,128]{1,0:T(8,128)(2,1)S(1)}, u32[]{:S(2)}, u32[]{:S(2)}) collective-permute-start(bf16[960,128]{1,0:T(8,128)(2,1)S(1)} %copy-done.91), channel_id=1, source_target_pairs={{144,131},{145,135},{153,139},{152,143},{146,128},{147,132},{155,1... | collective-permute-start | bytes 737288 | tf_op jit(solution)/shard_map/ppermute | solution.py:498
  617.9 53.0 %collective-permute-start.87 = (bf16[960,128]{1,0:T(8,128)(2,1)S(1)}, bf16[960,128]{1,0:T(8,128)(2,1)S(1)}, u32[]{:S(2)}, u32[]{:S(2)}) collective-permute-start(bf16[960,128]{1,0:T(8,128)(2,1)S(1)} %copy-done.91), channel_id=1, source_target_pairs={{128,131},{129,135},{137,139},{136,143},{130,128},{131,132},{139,1... | collective-permute-start | bytes 737288 | tf_op jit(solution)/shard_map/ppermute | solution.py:498
  619.3 61.1 %collective-permute-start.99 = (bf16[960,128]{1,0:T(8,128)(2,1)S(1)}, bf16[960,128]{1,0:T(8,128)(2,1)S(1)}, u32[]{:S(2)}, u32[]{:S(2)}) collective-permute-start(bf16[960,128]{1,0:T(8,128)(2,1)S(1)} %get-tuple-element.325), channel_id=1, source_target_pairs={{144,0},{145,4},{153,8},{152,12},{146,1},{147,5},{155,9},{154,13},... | collective-permute-start | bytes 737288 | tf_op jit(solution)/shard_map/ppermute | solution.py:498
  646.4 42.6 %collective-permute-start.98 = (bf16[960,128]{1,0:T(8,128)(2,1)S(1)}, bf16[960,128]{1,0:T(8,128)(2,1)S(1)}, u32[]{:S(2)}, u32[]{:S(2)}) collective-permute-start(bf16[960,128]{1,0:T(8,128)(2,1)S(1)} %get-tuple-element.325), channel_id=1, source_target_pairs={{128,0},{129,4},{137,8},{136,12},{130,1},{131,5},{139,9},{138,13},... | collective-permute-start | bytes 737288 | tf_op jit(solution)/shard_map/ppermute | solution.py:498
  654.2 42.3 %collective-permute-start.101 = (bf16[960,128]{1,0:T(8,128)(2,1)}, bf16[960,128]{1,0:T(8,128)(2,1)S(1)}, u32[]{:S(2)}, u32[]{:S(2)}) collective-permute-start(bf16[960,128]{1,0:T(8,128)(2,1)} %get-tuple-element.326), channel_id=1, source_target_pairs={{144,1},{145,5},{153,9},{152,13},{146,2},{147,6},{155,10},{154,14}... | collective-permute-start | bytes 737288 | tf_op jit(solution)/shard_map/ppermute | solution.py:498
  663.6 42.6 %collective-permute-start.100 = (bf16[960,128]{1,0:T(8,128)(2,1)}, bf16[960,128]{1,0:T(8,128)(2,1)S(1)}, u32[]{:S(2)}, u32[]{:S(2)}) collective-permute-start(bf16[960,128]{1,0:T(8,128)(2,1)} %get-tuple-element.326), channel_id=1, source_target_pairs={{128,1},{129,5},{137,9},{136,13},{130,2},{131,6},{139,10},{138,14}... | collective-permute-start | bytes 737288 | tf_op jit(solution)/shard_map/ppermute | solution.py:498
  (183 other events, 2149.3 us)

commit v2 on v1

--- a/solution.py
+++ b/solution.py
@@ -29,9 +29,12 @@
 PAIRS = ((0, 1), (2, 6), (3, 7), (4, 8), (5, 9), (10, 14), (11, 15), (12, 13))
 FETCH_AFTER = {0: 3, 2: 4, 4: 5, 6: 6, 8: 7}
 SWAP_AFTER = {0: 1, 1: 2, 2: 3, 3: 4, 6: 5, 8: 6, 10: 7}
-GROUPS = ((2, 3, 4, 5, 6, 7), (8, 9, 10, 11), (0, 1, 12, 13, 14, 15))
-SPREAD_AFTER = {9: 0, 13: 1}
-COLUMN = {0: 4, 1: 5, 2: 1, 3: 5, 4: 2, 5: 6, 6: 3, 7: 7, 8: 4, 9: 1, 10: 5, 11: 6, 12: 6, 13: 2, 14: 7, 15: 0}
+GROUPS = ((2, 3, 4, 5), (6, 7, 8, 9), (10, 11, 12), (0, 1, 13, 14, 15))
+SPREAD_AFTER = {7: 0, 11: 1, 14: 2}
+SPREAD_BY = {10: 0, 14: 1, 15: 2}
+HELPERS = {0: (4, 6, 0), 1: (4, 6, 1), 13: (5, 7, 0), 14: (5, 7, 1)}
+HELPERS |= {b: (5, 7, b % 2) for b in (2, 3, 6, 7, 10, 11)}
+HELPERS |= {b: (1, 3, b % 2) for b in (4, 5, 8, 9, 12)}
 
 
 def place(slot, quarter):
@@ -42,7 +45,7 @@
 def helper(block, slot, quarter):
     if block == BLOCKS - 1:
         return place(slot, quarter)
-    segment = 2 * COLUMN[block] + slot // 4
+    segment = 2 * HELPERS[block][slot // 4] + HELPERS[block][2]
     return segment * TILES + quarter // 2 * 8 + place(slot, quarter) % 8
 
 
@@ -126,29 +129,31 @@
         near_out, cross_out, stats_out = take(3)
     if up_out:
         (summed_out,) = take(1)
-    xs, ws, cat, result, totals, squares, in_sem, w_sem, out_sem = take(9)
+    xs, result = source, wholes[0]
+    if last:
+        (result,) = take(1)
+    ws, ps, cat, totals, squares, in_sem, w_sem, out_sem = take(8)
     if up_in:
         (sk_in,) = take(1)
     if up_out:
-        ls, sk, sums, l_sem = take(4)
+        ls, sums = lateral, summed_out
+        sk, l_sem = take(2)
 
     @pl.when(info[2] == 1)
     def _():
         core = info[0] // 2
-        x_copy = pltpu.make_async_copy(source, xs, in_sem.at[0])
-        x_copy.start()
         lead, tail = pl.ds(0, LEAD), pl.ds(LEAD, FULL - LEAD)
+        head = pl.ds(LEAD - WIDTH, WIDTH)
         for at in range(2):
 
             @pl.when((core == at_core) == (at == 0))
             def _():
+                pltpu.make_async_copy(weights[at].at[:, head], ps, w_sem.at[2]).start()
                 pltpu.make_async_copy(weights[at].at[:, lead], ws, w_sem.at[0]).start()
                 if up_in:
                     pltpu.make_async_copy(weights[at].at[:, tail], sk_in, w_sem.at[1]).start()
 
         if up_out:
-            lateral_copy = pltpu.make_async_copy(lateral, ls, l_sem.at[0])
-            lateral_copy.start()
             for at in range(2):
 
                 @pl.when((core == next_core) == (at == 0))
@@ -166,8 +171,8 @@
         mean = jnp.sum(jnp.where(even_kind, groups, 0.0), axis=1, keepdims=True) / MEMBERS
         mean_sq = jnp.sum(jnp.where(even_kind, 0.0, groups), axis=1, keepdims=True) / MEMBERS
         variance = jnp.maximum(mean_sq - mean * mean, 0.0)
-        pltpu.make_async_copy(weights[0].at[:, lead], ws, w_sem.at[0]).wait()
-        tailing = ws[:, TAPS : TAPS + 64].astype(F32)
+        pltpu.make_async_copy(weights[0].at[:, head], ps, w_sem.at[2]).wait()
+        tailing = ps[:, 64:128].astype(F32)
         params = tailing[:, 0:16] + tailing[:, 16:32] + tailing[:, 32:48]
         lane = lax.broadcasted_iota(jnp.int32, (CH, 16), 1)
         shift = jnp.sum(jnp.where(lane == info[1] + 8, params, 0.0), axis=1, keepdims=True)
@@ -201,30 +206,36 @@
                 rows + jnp.dot(skip_in, edge[0:CH, :], preferred_element_type=F32)
                 for rows, edge in zip((near_rows, cross_rows), lateral_edges)
             )
-        lift(jnp.where(even, cross_rows, near_rows), 0, info[0] > 0)
-        lift(jnp.where(even, near_rows, cross_rows), ROWS + 1, info[0] < 3)
-        x_copy.wait()
-
         def own_row(r):
-            return pl.ds(pl.multiple_of(r * CH, CH), CH)
-
-        @pl.loop(0, ROWS)
-        def _(r):
-            lift(xs[own_row(r), :].astype(F32), r + 1)
+            return slice(r * CH, (r + 1) * CH)
 
         if up_out:
-            lateral_copy.wait()
             pltpu.make_async_copy(nexts[0].at[:, tail], sk, l_sem.at[1]).wait()
             skip = sk[:, 0:CH]
         totals[...] = jnp.zeros(wide, F32)
         squares[...] = jnp.zeros(wide, F32)
 
-        @pl.loop(0, ROWS // 2)
-        def _(pair):
+        def lift_at(row):
+            if row == 0:
+                lift(jnp.where(even, cross_rows, near_rows), 0, info[0] > 0)
+            elif row == ROWS + 1:
+                lift(jnp.where(even, near_rows, cross_rows), row, info[0] < 3)
+            else:
+                lift(xs[(row - 1) * CH : row * CH, :].astype(F32), row)
+
+        for row in range(2):
+            lift_at(row)
+        lift_at(2)
+        lift_at(3)
+        pltpu.make_async_copy(weights[0].at[:, lead], ws, w_sem.at[0]).wait()
+        for pair in range(ROWS // 2):
+            if pair:
+                lift_at(2 * pair + 2)
+                lift_at(2 * pair + 3)
             convolved = sum(
                 jnp.dot(
                     ws[:, dy * CAT : (dy + 1) * CAT],
-                    cat[:, pl.ds(pl.multiple_of((2 * pair + dy) * WIDTH, WIDTH), 2 * WIDTH)],
+                    cat[:, (2 * pair + dy) * WIDTH : (2 * pair + dy + 2) * WIDTH],
                     preferred_element_type=F32,
                 )
                 for dy in range(3)
@@ -253,9 +264,7 @@
                 for k in range(4)
             ]
         else:
-            finals = [pltpu.make_async_copy(result, wholes[0], out_sem.at[0])]
-        if up_out:
-            finals.append(pltpu.make_async_copy(sums, summed_out, out_sem.at[1]))
+            finals = []
         for copy in finals:
             copy.start()
         if not last:
@@ -311,19 +320,20 @@
 def block_call(cores, info, source, exchanged, member, weights, lateral_edges, lateral, nexts, passing):
     up_in, up_out, last = lateral_edges is not None, lateral is not None, len(passing)
     operands = [source, *exchanged, member, *weights]
-    specs = [ANY] + [VM] * 5 + [ANY] * 2
-    shapes, out_specs = [WHOLE] + EXCHANGED, [ANY] + [VM] * 3
+    specs = [VM] * 6 + [ANY] * 2
+    shapes, out_specs = [WHOLE] + EXCHANGED, [VM] * 4
+    scratch = []
     if last:
         shapes, out_specs = [PART] * 4, [ANY] * 4
-    scratch = [
-        pltpu.VMEM((OWN, WIDTH), F32 if up_in else BF),
+        scratch.append(pltpu.VMEM((OWN, WIDTH), BF))
+    scratch += [
         pltpu.VMEM((CH, LEAD), BF),
+        pltpu.VMEM((CH, WIDTH), BF),
         pltpu.VMEM((CAT, (ROWS + 2) * WIDTH), BF),
-        pltpu.VMEM((OWN, WIDTH), BF),
         pltpu.VMEM((CH, WIDTH), F32),
         pltpu.VMEM((CH, WIDTH), F32),
         pltpu.SemaphoreType.DMA((1,)),
-        pltpu.SemaphoreType.DMA((2,)),
+        pltpu.SemaphoreType.DMA((3,)),
         pltpu.SemaphoreType.DMA((4,)),
     ]
     if up_in:
@@ -332,13 +342,11 @@
         scratch.append(pltpu.VMEM((CH, FULL - LEAD), BF))
     if up_out:
         operands += [lateral, *nexts]
-        specs += [ANY] * 3
+        specs += [VM] + [ANY] * 2
         shapes = shapes + [jax.ShapeDtypeStruct((OWN, WIDTH), F32)]
-        out_specs = out_specs + [ANY]
+        out_specs = out_specs + [VM]
         scratch += [
-            pltpu.VMEM((OWN, WIDTH), BF),
             pltpu.VMEM((CH, FULL - LEAD), BF),
-            pltpu.VMEM((OWN, WIDTH), F32),
             pltpu.SemaphoreType.DMA((2,)),
         ]
     operands += passing
@@ -349,7 +357,7 @@
         in_specs=[SM] + specs,
         out_specs=out_specs,
         scratch_shapes=scratch,
-        compiler_params=pltpu.CompilerParams(vmem_limit_bytes=40 * MIB),
+        compiler_params=pltpu.CompilerParams(vmem_limit_bytes=28 * MIB),
         cost_estimate=pl.CostEstimate(
             flops=2 * OWN * WIDTH * TAPS, bytes_accessed=4 * MIB, transcendentals=OWN * WIDTH
         ),
@@ -436,13 +444,16 @@
     quarter = jnp.where(odd == 1, 1 + core, 3 * core)
     slot = 4 * (tile // 8) + (tile % 8) // 2
     active = (segment < 2).astype(jnp.int32)
-    passed = 4 * core + (tile % 8) // 2
 
     def info_for(group):
-        pick = jnp.full((), -1, jnp.int32)
+        pick, passed = jnp.full((), -1, jnp.int32), (tile % 8) // 2
         for at, block in enumerate(group):
             if block < BLOCKS - 1:
-                pick = jnp.where(segment // 2 == COLUMN[block], at, pick)
+                *columns, its_core = HELPERS[block]
+                for half, column in enumerate(columns):
+                    ours = segment == 2 * column + its_core
+                    pick = jnp.where(ours, at, pick)
+                    passed = jnp.where(ours, passed + 4 * half, passed)
         return jnp.stack([quarter, slot, active, pick, passed]).astype(jnp.int32)
 
     info = info_for(())
@@ -477,9 +488,17 @@
             own, _ = lax.optimization_barrier((own, after))
         return lax.ppermute(own, "segment", [(pair[0], 0), (pair[1], 1)])
 
-    def swap(value, mask):
-        route = [(place(j, q), place(j, q ^ mask)) for j in range(MICRO) for q in range(4)]
-        return lax.ppermute(value, BOTH, route)
+    def exchange(near, cross, stats):
+        other_tile = [(t, t ^ 1) for t in range(TILES)]
+        other_core = [(b, b ^ 1) for b in range(BLOCKS)]
+        both = [
+            (b * TILES + t, (b ^ 1) * TILES + (t ^ 1)) for b in range(BLOCKS) for t in range(TILES)
+        ]
+        return (
+            lax.ppermute(near, "tile", other_tile),
+            lax.ppermute(cross, "segment", other_core),
+            lax.ppermute(stats, BOTH, both),
+        )
 
     def hand_over(block, whole):
         route = [(place(j, q), helper(block, j, q)) for j in range(MICRO) for q in range(4)]
@@ -503,28 +522,31 @@
     weights, cores, fetched = {}, {}, {}
 
     def swap_cores(index, own):
-        both = own, lax.ppermute(own, "segment", [(0, 1), (1, 0)])
+        both = own, lax.ppermute(own, "segment", [(b, b ^ 1) for b in range(BLOCKS)])
         for at, block in enumerate(PAIRS[index]):
             weights[block], cores[block] = both, at
 
     swap_cores(0, lead)
+    *exchanged, source = first_call(info, pieces)
     for index in (1, 2):
-        fetched[index] = fetch(PAIRS[index], None)
-    *exchanged, source = first_call(info, pieces)
+        fetched[index] = fetch(PAIRS[index], pieces[-1])
     wholes, edges_of, passing, received = [], {}, [], []
     for block in range(BLOCKS):
         up_in, up_out = block >= first_up, first_up - 1 <= block < BLOCKS - 1
         near, cross, stats = exchanged
-        near_in, cross_in, far = swap(near, 1), swap(cross, 3), swap(stats, 2)
+        near_in, cross_in, far = exchange(near, cross, stats)
         edges_of[block] = (near_in, cross_in)
         if block >= 2:
             source, near_in, cross_in, far, passing[block - 2] = lax.optimization_barrier(
                 (source, near_in, cross_in, far, passing[block - 2])
             )
+        if block in SPREAD_BY:
+            at = SPREAD_BY[block]
+            source, received[at] = lax.optimization_barrier((source, received[at]))
         last = block == BLOCKS - 1
         whole, exchanged, summed = block_call(
             (cores[block], cores.get(block + 1, 0)),
-            info_for(GROUPS[2]) if last else info,
+            info_for(GROUPS[-1]) if last else info,
             source,
             (near_in, cross_in, stats, far),
             member,
@@ -532,7 +554,7 @@
             edges_of[BLOCKS - block] if up_in else None,
             wholes[BLOCKS - 2 - block] if up_out else None,
             weights[block + 1] if up_out else None,
-            [passing[b] for b in GROUPS[2][:-1]] if last else [],
+            [passing[b] for b in GROUPS[-1][:-1]] if last else [],
         )
         wholes.append(whole)
         source = summed if up_out else whole
@@ -549,7 +571,7 @@
         if block in FETCH_AFTER:
             index = FETCH_AFTER[block]
             fetched[index] = fetch(PAIRS[index], whole)
-    received.append(spread(GROUPS[2], whole))
+    received.append(spread(GROUPS[-1], whole))
     group_of = jnp.zeros((), jnp.int32)
     for at, group in enumerate(GROUPS):
         for block in group:

time: 748 us -> 826 us (1.10)
  the two profiles are of different devices: /device:TPU:33 before, /device:TPU:59 now
where the time goes in v2:
time: 826 us; the launch traced here: 812 us
  starting transfers between devices  557 us (67%)
  waiting for transfers between devices  97.6 us (12%)
  Pallas kernels  78 us (9%)
  local copies, waits for them, and re-layouts  71.5 us (9%)
    ppermute x32, starting transfers between devices, spread(): got.append(lax.ppermute(outs[k], BOTH, route))  374 us
    ppermute x16, starting transfers between devices, exchange(): lax.ppermute(stats, BOTH, both)  111 us
    pallas_call x16, Pallas kernels, block_call(): pl.pallas_call(functools.partial(block_body, *cores, up_in, up_out, last)...  65.7 us
    unnamed x233, local copies, waits for them, and re-layouts  59.8 us
    ppermute x32, waiting for transfers between devices, spread(): got.append(lax.ppermute(outs[k], BOTH, route))  47.3 us
    ppermute x16, waiting for transfers between devices, exchange(): lax.ppermute(stats, BOTH, both)  25.1 us
    ppermute x7, starting transfers between devices, fetch(): return lax.ppermute(own, 'segment', [(pair[0], 0), (pair[1], 1)])  21.9 us
    ppermute x16, waiting for transfers between devices, exchange(): lax.ppermute(near, 'tile', other_tile)  20.7 us
  transfers between devices with their start and end apart: 114, of which 35 were waited for; matrix products, arithmetic and copies ran while one was open for 1% of the time, Pallas kernels for 9%

profile of v2, /device:TPU:59, one launch (start us, length us, event | category | flops | bytes accessed | tf_op | source)
XLA Modules:
  0.0 811.6 jit_solution(17189929995103572506)
XLA Ops:
  65.8 9.6 %res_block.20 = (bf16[3840,128]{1,0:T(8,128)(2,1)}, bf16[368,128]{1,0:T(8,128)(2,1)S(1)}, bf16[368,128]{1,0:T(8,128)(2,1)S(1)}, bf16[48,128]{1,0:T(8,128)(2,1)S(1)}) custom-call(s32[5]{0:T(128)S(1)} %stack.77.info, bf16[3840,128]{1,0:T(8,128)(2,1)} %get-tuple-element.230.refs_0_.refs_8_, bf16[368,128]{1,0:T(8,128)(2,1)S(1)} %collective-permute-done.23.refs_1_.refs_8_, ...), custom_call_target="tpu_custom_call" | custom-call | flops 2831155200 | bytes 4194304 | tf_op jit(solution)/shard_map/res_block/pallas_call | solution.py:354
  87.9 93.1 %collective-permute-start.31 = (bf16[48,128]{1,0:T(8,128)(2,1)S(1)}, bf16[48,128]{1,0:T(8,128)(2,1)S(1)}, u32[]{:S(2)}, u32[]{:S(2)}) collective-permute-start(bf16[48,128]{1,0:T(8,128)(2,1)S(1)} %get-tuple-element.239.refs_3_), channel_id=1, source_target_pairs={{0,17},{1,16},{2,19},{3,18},{4,21},{5,20},{6,23},{7,22},{8,25},{9,... | collective-permute-start | bytes 36872 | tf_op jit(solution)/shard_map/ppermute | solution.py:500
  213.8 13.7 %collective-permute-start.69 = (bf16[320,3328]{1,0:T(8,128)(2,1)}, bf16[320,3328]{1,0:T(8,128)(2,1)S(1)}, u32[]{:S(2)}, u32[]{:S(2)}) collective-permute-start(bf16[320,3328]{1,0:T(8,128)(2,1)} %concatenate.20), channel_id=1, source_target_pairs={{176,0},{240,16},{177,1},{241,17},{178,2},{242,18},{179,3},{243,19... | collective-permute-start | bytes 6389768 | tf_op jit(solution)/shard_map/ppermute | solution.py:489
  234.6 19.2 %collective-permute-start.56 = (bf16[960,128]{1,0:T(8,128)(2,1)S(1)}, bf16[960,128]{1,0:T(8,128)(2,1)S(1)}, u32[]{:S(2)}, u32[]{:S(2)}) collective-permute-start(bf16[960,128]{1,0:T(8,128)(2,1)S(1)} %get-tuple-element.287), channel_id=1, source_target_pairs={{224,32},{225,36},{233,40},{232,44},{226,33},{227,37},{235,41},{23... | collective-permute-start | bytes 737288 | tf_op jit(solution)/shard_map/ppermute | solution.py:517
  271.8 27.6 %collective-permute-start.58 = (bf16[960,128]{1,0:T(8,128)(2,1)S(1)}, bf16[960,128]{1,0:T(8,128)(2,1)S(1)}, u32[]{:S(2)}, u32[]{:S(2)}) collective-permute-start(bf16[960,128]{1,0:T(8,128)(2,1)S(1)} %get-tuple-element.288), channel_id=1, source_target_pairs={{224,33},{225,37},{233,41},{232,45},{226,34},{227,38},{235,42},{23... | collective-permute-start | bytes 737288 | tf_op jit(solution)/shard_map/ppermute | solution.py:517
  306.1 39.6 %collective-permute-start.60 = (bf16[960,128]{1,0:T(8,128)(2,1)S(1)}, bf16[960,128]{1,0:T(8,128)(2,1)S(1)}, u32[]{:S(2)}, u32[]{:S(2)}) collective-permute-start(bf16[960,128]{1,0:T(8,128)(2,1)S(1)} %get-tuple-element.289), channel_id=1, source_target_pairs={{224,34},{225,38},{233,42},{232,46},{226,35},{227,39},{235,43},{23... | collective-permute-start | bytes 737288 | tf_op jit(solution)/shard_map/ppermute | solution.py:517
  345.8 12.9 %collective-permute-done.60.refs_5_ = bf16[960,128]{1,0:T(8,128)(2,1)S(1)} collective-permute-done((bf16[960,128]{1,0:T(8,128)(2,1)S(1)}, bf16[960,128]{1,0:T(8,128)(2,1)S(1)}, u32[]{:S(2)}, u32[]{:S(2)}) %collective-permute-start.60) | collective-permute-done | bytes 245792 | tf_op jit(solution)/shard_map/ppermute | solution.py:517
  369.8 29.0 %collective-permute-start.62 = (bf16[960,128]{1,0:T(8,128)(2,1)S(1)}, bf16[960,128]{1,0:T(8,128)(2,1)S(1)}, u32[]{:S(2)}, u32[]{:S(2)}) collective-permute-start(bf16[960,128]{1,0:T(8,128)(2,1)S(1)} %get-tuple-element.290), channel_id=1, source_target_pairs={{224,35},{225,39},{233,43},{232,47},{226,32},{227,36},{235,40},{23... | collective-permute-start | bytes 737288 | tf_op jit(solution)/shard_map/ppermute | solution.py:517
  455.4 28.4 %collective-permute-start.86 = (bf16[960,128]{1,0:T(8,128)(2,1)S(1)}, bf16[960,128]{1,0:T(8,128)(2,1)S(1)}, u32[]{:S(2)}, u32[]{:S(2)}) collective-permute-start(bf16[960,128]{1,0:T(8,128)(2,1)S(1)} %get-tuple-element.344), channel_id=1, source_target_pairs={{224,96},{225,100},{233,104},{232,108},{226,97},{227,101},{235,105... | collective-permute-start | bytes 737288 | tf_op jit(solution)/shard_map/ppermute | solution.py:517
  484.4 15.5 %collective-permute-start.88 = (bf16[960,128]{1,0:T(8,128)(2,1)S(1)}, bf16[960,128]{1,0:T(8,128)(2,1)S(1)}, u32[]{:S(2)}, u32[]{:S(2)}) collective-permute-start(bf16[960,128]{1,0:T(8,128)(2,1)S(1)} %get-tuple-element.345), channel_id=1, source_target_pairs={{224,97},{225,101},{233,105},{232,109},{226,98},{227,102},{235,106... | collective-permute-start | bytes 737288 | tf_op jit(solution)/shard_map/ppermute | solution.py:517
  508.6 24.2 %collective-permute-start.90 = (bf16[960,128]{1,0:T(8,128)(2,1)S(1)}, bf16[960,128]{1,0:T(8,128)(2,1)S(1)}, u32[]{:S(2)}, u32[]{:S(2)}) collective-permute-start(bf16[960,128]{1,0:T(8,128)(2,1)S(1)} %get-tuple-element.346), channel_id=1, source_target_pairs={{224,98},{225,102},{233,106},{232,110},{226,99},{227,103},{235,107... | collective-permute-start | bytes 737288 | tf_op jit(solution)/shard_map/ppermute | solution.py:517
  533.7 12.2 %collective-permute-start.89 = (bf16[960,128]{1,0:T(8,128)(2,1)S(1)}, bf16[960,128]{1,0:T(8,128)(2,1)S(1)}, u32[]{:S(2)}, u32[]{:S(2)}) collective-permute-start(bf16[960,128]{1,0:T(8,128)(2,1)S(1)} %get-tuple-element.346), channel_id=1, source_target_pairs={{160,98},{161,102},{169,106},{168,110},{162,99},{163,103},{171,107... | collective-permute-start | bytes 737288 | tf_op jit(solution)/shard_map/ppermute | solution.py:517
  546.0 13.1 %collective-permute-start.92 = (bf16[960,128]{1,0:T(8,128)(2,1)S(1)}, bf16[960,128]{1,0:T(8,128)(2,1)S(1)}, u32[]{:S(2)}, u32[]{:S(2)}) collective-permute-start(bf16[960,128]{1,0:T(8,128)(2,1)S(1)} %get-tuple-element.347), channel_id=1, source_target_pairs={{224,99},{225,103},{233,107},{232,111},{226,96},{227,100},{235,104... | collective-permute-start | bytes 737288 | tf_op jit(solution)/shard_map/ppermute | solution.py:517
  559.2 12.3 %collective-permute-start.91 = (bf16[960,128]{1,0:T(8,128)(2,1)S(1)}, bf16[960,128]{1,0:T(8,128)(2,1)S(1)}, u32[]{:S(2)}, u32[]{:S(2)}) collective-permute-start(bf16[960,128]{1,0:T(8,128)(2,1)S(1)} %get-tuple-element.347), channel_id=1, source_target_pairs={{160,99},{161,103},{169,107},{168,111},{162,96},{163,100},{171,104... | collective-permute-start | bytes 737288 | tf_op jit(solution)/shard_map/ppermute | solution.py:517
  592.9 11.1 %collective-permute-start.98 = (bf16[960,128]{1,0:T(8,128)(2,1)S(1)}, bf16[960,128]{1,0:T(8,128)(2,1)S(1)}, u32[]{:S(2)}, u32[]{:S(2)}) collective-permute-start(bf16[960,128]{1,0:T(8,128)(2,1)S(1)} %get-tuple-element.369), channel_id=1, source_target_pairs={{224,160},{225,164},{233,168},{232,172},{226,161},{227,165},{235,1... | collective-permute-start | bytes 737288 | tf_op jit(solution)/shard_map/ppermute | solution.py:517
  657.1 25.9 %collective-permute-start.107 = (bf16[960,128]{1,0:T(8,128)(2,1)S(1)}, bf16[960,128]{1,0:T(8,128)(2,1)S(1)}, u32[]{:S(2)}, u32[]{:S(2)}) collective-permute-start(bf16[960,128]{1,0:T(8,128)(2,1)S(1)} %get-tuple-element.389), channel_id=1, source_target_pairs={{192,0},{193,4},{201,8},{200,12},{194,1},{195,5},{203,9},{202,13},... | collective-permute-start | bytes 737288 | tf_op jit(solution)/shard_map/ppermute | solution.py:517
  683.0 12.2 %collective-permute-start.106 = (bf16[960,128]{1,0:T(8,128)(2,1)S(1)}, bf16[960,128]{1,0:T(8,128)(2,1)S(1)}, u32[]{:S(2)}, u32[]{:S(2)}) collective-permute-start(bf16[960,128]{1,0:T(8,128)(2,1)S(1)} %get-tuple-element.389), channel_id=1, source_target_pairs={{128,0},{129,4},{137,8},{136,12},{130,1},{131,5},{139,9},{138,13},... | collective-permute-start | bytes 737288 | tf_op jit(solution)/shard_map/ppermute | solution.py:517
  695.2 13.1 %collective-permute-start.109 = (bf16[960,128]{1,0:T(8,128)(2,1)}, bf16[960,128]{1,0:T(8,128)(2,1)S(1)}, u32[]{:S(2)}, u32[]{:S(2)}) collective-permute-start(bf16[960,128]{1,0:T(8,128)(2,1)} %get-tuple-element.390), channel_id=1, source_target_pairs={{192,1},{193,5},{201,9},{200,13},{194,2},{195,6},{203,10},{202,14}... | collective-permute-start | bytes 737288 | tf_op jit(solution)/shard_map/ppermute | solution.py:517
  708.3 12.2 %collective-permute-start.108 = (bf16[960,128]{1,0:T(8,128)(2,1)}, bf16[960,128]{1,0:T(8,128)(2,1)S(1)}, u32[]{:S(2)}, u32[]{:S(2)}) collective-permute-start(bf16[960,128]{1,0:T(8,128)(2,1)} %get-tuple-element.390), channel_id=1, source_target_pairs={{128,1},{129,5},{137,9},{136,13},{130,2},{131,6},{139,10},{138,14}... | collective-permute-start | bytes 737288 | tf_op jit(solution)/shard_map/ppermute | solution.py:517
  720.5 13.1 %collective-permute-start.111 = (bf16[960,128]{1,0:T(8,128)(2,1)}, bf16[960,128]{1,0:T(8,128)(2,1)S(1)}, u32[]{:S(2)}, u32[]{:S(2)}) collective-permute-start(bf16[960,128]{1,0:T(8,128)(2,1)} %get-tuple-element.391), channel_id=1, source_target_pairs={{192,2},{193,6},{201,10},{200,14},{194,3},{195,7},{203,11},{202,15... | collective-permute-start | bytes 737288 | tf_op jit(solution)/shard_map/ppermute | solution.py:517
  733.7 12.2 %collective-permute-start.110 = (bf16[960,128]{1,0:T(8,128)(2,1)}, bf16[960,128]{1,0:T(8,128)(2,1)S(1)}, u32[]{:S(2)}, u32[]{:S(2)}) collective-permute-start(bf16[960,128]{1,0:T(8,128)(2,1)} %get-tuple-element.391), channel_id=1, source_target_pairs={{128,2},{129,6},{137,10},{136,14},{130,3},{131,7},{139,11},{138,15... | collective-permute-start | bytes 737288 | tf_op jit(solution)/shard_map/ppermute | solution.py:517
  745.9 13.1 %collective-permute-start.113 = (bf16[960,128]{1,0:T(8,128)(2,1)}, bf16[960,128]{1,0:T(8,128)(2,1)S(1)}, u32[]{:S(2)}, u32[]{:S(2)}) collective-permute-start(bf16[960,128]{1,0:T(8,128)(2,1)} %get-tuple-element.392), channel_id=1, source_target_pairs={{192,3},{193,7},{201,11},{200,15},{194,0},{195,4},{203,8},{202,12}... | collective-permute-start | bytes 737288 | tf_op jit(solution)/shard_map/ppermute | solution.py:517
  759.1 12.2 %collective-permute-start.112 = (bf16[960,128]{1,0:T(8,128)(2,1)}, bf16[960,128]{1,0:T(8,128)(2,1)S(1)}, u32[]{:S(2)}, u32[]{:S(2)}) collective-permute-start(bf16[960,128]{1,0:T(8,128)(2,1)} %get-tuple-element.392), channel_id=1, source_target_pairs={{128,3},{129,7},{137,11},{136,15},{130,0},{131,4},{139,8},{138,12}... | collective-permute-start | bytes 737288 | tf_op jit(solution)/shard_map/ppermute | solution.py:517
  772.3 12.6 %collective-permute-done.112.refs_30_ = bf16[960,128]{1,0:T(8,128)(2,1)S(1)} collective-permute-done((bf16[960,128]{1,0:T(8,128)(2,1)}, bf16[960,128]{1,0:T(8,128)(2,1)S(1)}, u32[]{:S(2)}, u32[]{:S(2)}) %collective-permute-start.112) | collective-permute-done | bytes 245792 | tf_op jit(solution)/shard_map/ppermute | solution.py:517
  (483 shorter events, 319.4 us)
Async XLA Ops:
  57.9 127.7 %collective-permute-start.34 = (bf16[320,2944]{1,0:T(8,128)(2,1)}, bf16[320,2944]{1,0:T(8,128)(2,1)}, u32[]{:S(2)}, u32[]{:S(2)}) collective-permute-start(bf16[320,2944]{1,0:T(8,128)(2,1)} %collective-permute-done.33.refs_6_), channel_id=1, source_target_pairs={{0,16},{16,0},{32,48},{48,32},{64,80},{80,64},{96,112},{112,96},{1... | collective-permute-start | bytes 5652488 | tf_op jit(solution)/shard_map/ppermute | solution.py:525
  62.6 118.4 %collective-permute-start.32 = (bf16[3840,128]{1,0:T(8,128)(2,1)}, bf16[3840,128]{1,0:T(8,128)(2,1)S(1)}, u32[]{:S(2)}, u32[]{:S(2)}) collective-permute-start(bf16[3840,128]{1,0:T(8,128)(2,1)} %get-tuple-element.230.refs_0_.refs_8_), channel_id=1, source_target_pairs={{0,176},{1,177},{17,185},{16,184},{2,178},{3,179},{19,187},{18,186... | collective-permute-start | bytes 2949128 | tf_op jit(solution)/shard_map/ppermute | solution.py:505
  78.0 110.9 %collective-permute-start.38 = (bf16[3840,128]{1,0:T(8,128)(2,1)}, bf16[3840,128]{1,0:T(8,128)(2,1)S(1)}, u32[]{:S(2)}, u32[]{:S(2)}) collective-permute-start(bf16[3840,128]{1,0:T(8,128)(2,1)} %get-tuple-element.240.refs_0_), channel_id=1, source_target_pairs={{0,32},{1,33},{17,41},{16,40},{2,34},{3,35},{19,43},{18,42},{4,36}... | collective-permute-start | bytes 2949128 | tf_op jit(solution)/shard_map/ppermute | solution.py:505
  85.9 127.8 %collective-permute-start.63 = (bf16[320,3328]{1,0:T(8,128)(2,1)}, bf16[320,3328]{1,0:T(8,128)(2,1)}, u32[]{:S(2)}, u32[]{:S(2)}) collective-permute-start(bf16[320,3328]{1,0:T(8,128)(2,1)} %concatenate.20), channel_id=1, source_target_pairs={{160,0},{224,16},{161,1},{225,17},{162,2},{226,18},{163,3},{227,19... | collective-permute-start | bytes 6389768 | tf_op jit(solution)/shard_map/ppermute | solution.py:489
  87.9 94.4 %collective-permute-start.31 = (bf16[48,128]{1,0:T(8,128)(2,1)S(1)}, bf16[48,128]{1,0:T(8,128)(2,1)S(1)}, u32[]{:S(2)}, u32[]{:S(2)}) collective-permute-start(bf16[48,128]{1,0:T(8,128)(2,1)S(1)} %get-tuple-element.239.refs_3_), channel_id=1, source_target_pairs={{0,17},{1,16},{2,19},{3,18},{4,21},{5,20},{6,23},{7,22},{8,25},{9,... | collective-permute-start | bytes 36872 | tf_op jit(solution)/shard_map/ppermute | solution.py:500
  201.3 52.6 %collective-permute-start.46 = (bf16[3840,128]{1,0:T(8,128)(2,1)}, bf16[3840,128]{1,0:T(8,128)(2,1)}, u32[]{:S(2)}, u32[]{:S(2)}) collective-permute-start(bf16[3840,128]{1,0:T(8,128)(2,1)} %get-tuple-element.258.refs_0_), channel_id=1, source_target_pairs={{0,160},{1,161},{17,169},{16,168},{2,162},{3,163},{19,171},{18,170... | collective-permute-start | bytes 2949128 | tf_op jit(solution)/shard_map/ppermute | solution.py:505
  213.8 194.5 %collective-permute-start.69 = (bf16[320,3328]{1,0:T(8,128)(2,1)}, bf16[320,3328]{1,0:T(8,128)(2,1)S(1)}, u32[]{:S(2)}, u32[]{:S(2)}) collective-permute-start(bf16[320,3328]{1,0:T(8,128)(2,1)} %concatenate.20), channel_id=1, source_target_pairs={{176,0},{240,16},{177,1},{241,17},{178,2},{242,18},{179,3},{243,19... | collective-permute-start | bytes 6389768 | tf_op jit(solution)/shard_map/ppermute | solution.py:489
  234.5 175.6 %collective-permute-start.64 = (bf16[320,3328]{1,0:T(8,128)(2,1)}, bf16[320,3328]{1,0:T(8,128)(2,1)S(1)}, u32[]{:S(2)}, u32[]{:S(2)}) collective-permute-start(bf16[320,3328]{1,0:T(8,128)(2,1)} %collective-permute-done.63.refs_6_.refs_11_), channel_id=1, source_target_pairs={{0,16},{16,0},{32,48},{48,32},{64,80},{80,64},{96,112},{112,96},{1... | collective-permute-start | bytes 6389768 | tf_op jit(solution)/shard_map/ppermute | solution.py:525
  271.0 147.1 %collective-permute-start.71 = (bf16[320,3328]{1,0:T(8,128)(2,1)S(1)}, bf16[320,3328]{1,0:T(8,128)(2,1)S(1)}, u32[]{:S(2)}, u32[]{:S(2)}) collective-permute-start(bf16[320,3328]{1,0:T(8,128)(2,1)S(1)} %copy-done.112), channel_id=1, source_target_pairs={{192,0},{208,16},{193,1},{209,17},{194,2},{210,18},{195,3},{211,19... | collective-permute-start | bytes 6389768 | tf_op jit(solution)/shard_map/ppermute | solution.py:489
  305.4 93.4 %collective-permute-start.54 = (bf16[3840,128]{1,0:T(8,128)(2,1)S(1)}, bf16[3840,128]{1,0:T(8,128)(2,1)S(1)}, u32[]{:S(2)}, u32[]{:S(2)}) collective-permute-start(bf16[3840,128]{1,0:T(8,128)(2,1)S(1)} %get-tuple-element.274.refs_0_), channel_id=1, source_target_pairs={{0,32},{1,33},{17,41},{16,40},{2,34},{3,35},{19,43},{18,42},{4,36}... | collective-permute-start | bytes 2949128 | tf_op jit(solution)/shard_map/ppermute | solution.py:505
  306.1 52.6 %collective-permute-start.60 = (bf16[960,128]{1,0:T(8,128)(2,1)S(1)}, bf16[960,128]{1,0:T(8,128)(2,1)S(1)}, u32[]{:S(2)}, u32[]{:S(2)}) collective-permute-start(bf16[960,128]{1,0:T(8,128)(2,1)S(1)} %get-tuple-element.289), channel_id=1, source_target_pairs={{224,34},{225,38},{233,42},{232,46},{226,35},{227,39},{235,43},{23... | collective-permute-start | bytes 737288 | tf_op jit(solution)/shard_map/ppermute | solution.py:517
  436.8 63.2 %collective-permute-start.80 = (bf16[3840,128]{1,0:T(8,128)(2,1)S(1)}, bf16[3840,128]{1,0:T(8,128)(2,1)S(1)}, u32[]{:S(2)}, u32[]{:S(2)}) collective-permute-start(bf16[3840,128]{1,0:T(8,128)(2,1)S(1)} %get-tuple-element.329), channel_id=1, source_target_pairs={{0,176},{1,177},{17,185},{16,184},{2,178},{3,179},{19,187},{18,186... | collective-permute-start | bytes 2949128 | tf_op jit(solution)/shard_map/ppermute | solution.py:505
  449.4 83.4 %collective-permute-start.84 = (bf16[3840,128]{1,0:T(8,128)(2,1)S(1)}, bf16[3840,128]{1,0:T(8,128)(2,1)S(1)}, u32[]{:S(2)}, u32[]{:S(2)}) collective-permute-start(bf16[3840,128]{1,0:T(8,128)(2,1)S(1)} %get-tuple-element.338), channel_id=1, source_target_pairs={{0,32},{1,33},{17,41},{16,40},{2,34},{3,35},{19,43},{18,42},{4,36}... | collective-permute-start | bytes 2949128 | tf_op jit(solution)/shard_map/ppermute | solution.py:505
  455.4 47.3 %collective-permute-start.86 = (bf16[960,128]{1,0:T(8,128)(2,1)S(1)}, bf16[960,128]{1,0:T(8,128)(2,1)S(1)}, u32[]{:S(2)}, u32[]{:S(2)}) collective-permute-start(bf16[960,128]{1,0:T(8,128)(2,1)S(1)} %get-tuple-element.344), channel_id=1, source_target_pairs={{224,96},{225,100},{233,104},{232,108},{226,97},{227,101},{235,105... | collective-permute-start | bytes 737288 | tf_op jit(solution)/shard_map/ppermute | solution.py:517
  503.4 55.7 %collective-permute-start.82 = (bf16[368,128]{1,0:T(8,128)(2,1)S(1)}, bf16[368,128]{1,0:T(8,128)(2,1)S(1)}, u32[]{:S(2)}, u32[]{:S(2)}) collective-permute-start(bf16[368,128]{1,0:T(8,128)(2,1)S(1)} %get-tuple-element.336), channel_id=1, source_target_pairs={{0,16},{16,0},{32,48},{48,32},{64,80},{80,64},{96,112},{112,96},{1... | collective-permute-start | bytes 282632 | tf_op jit(solution)/shard_map/ppermute | solution.py:499
  506.8 64.6 %collective-permute-start.87 = (bf16[960,128]{1,0:T(8,128)(2,1)S(1)}, bf16[960,128]{1,0:T(8,128)(2,1)S(1)}, u32[]{:S(2)}, u32[]{:S(2)}) collective-permute-start(bf16[960,128]{1,0:T(8,128)(2,1)S(1)} %get-tuple-element.345), channel_id=1, source_target_pairs={{160,97},{161,101},{169,105},{168,109},{162,98},{163,102},{171,106... | collective-permute-start | bytes 737288 | tf_op jit(solution)/shard_map/ppermute | solution.py:517
  508.6 65.2 %collective-permute-start.90 = (bf16[960,128]{1,0:T(8,128)(2,1)S(1)}, bf16[960,128]{1,0:T(8,128)(2,1)S(1)}, u32[]{:S(2)}, u32[]{:S(2)}) collective-permute-start(bf16[960,128]{1,0:T(8,128)(2,1)S(1)} %get-tuple-element.346), channel_id=1, source_target_pairs={{224,98},{225,102},{233,106},{232,110},{226,99},{227,103},{235,107... | collective-permute-start | bytes 737288 | tf_op jit(solution)/shard_map/ppermute | solution.py:517
  572.1 65.4 %collective-permute-start.96 = (bf16[3840,128]{1,0:T(8,128)(2,1)}, bf16[3840,128]{1,0:T(8,128)(2,1)}, u32[]{:S(2)}, u32[]{:S(2)}) collective-permute-start(bf16[3840,128]{1,0:T(8,128)(2,1)} %get-tuple-element.364), channel_id=1, source_target_pairs={{0,160},{1,161},{17,169},{16,168},{2,162},{3,163},{19,171},{18,170... | collective-permute-start | bytes 2949128 | tf_op jit(solution)/shard_map/ppermute | solution.py:505
  585.6 61.0 %collective-permute-start.105 = (bf16[3840,128]{1,0:T(8,128)(2,1)}, bf16[3840,128]{1,0:T(8,128)(2,1)}, u32[]{:S(2)}, u32[]{:S(2)}) collective-permute-start(bf16[3840,128]{1,0:T(8,128)(2,1)} %get-tuple-element.388), channel_id=1, source_target_pairs={{0,176},{1,177},{17,185},{16,184},{2,178},{3,179},{19,187},{18,186... | collective-permute-start | bytes 2949128 | tf_op jit(solution)/shard_map/ppermute | solution.py:505
  657.1 76.6 %collective-permute-start.107 = (bf16[960,128]{1,0:T(8,128)(2,1)S(1)}, bf16[960,128]{1,0:T(8,128)(2,1)S(1)}, u32[]{:S(2)}, u32[]{:S(2)}) collective-permute-start(bf16[960,128]{1,0:T(8,128)(2,1)S(1)} %get-tuple-element.389), channel_id=1, source_target_pairs={{192,0},{193,4},{201,8},{200,12},{194,1},{195,5},{203,9},{202,13},... | collective-permute-start | bytes 737288 | tf_op jit(solution)/shard_map/ppermute | solution.py:517
  683.0 63.0 %collective-permute-start.106 = (bf16[960,128]{1,0:T(8,128)(2,1)S(1)}, bf16[960,128]{1,0:T(8,128)(2,1)S(1)}, u32[]{:S(2)}, u32[]{:S(2)}) collective-permute-start(bf16[960,128]{1,0:T(8,128)(2,1)S(1)} %get-tuple-element.389), channel_id=1, source_target_pairs={{128,0},{129,4},{137,8},{136,12},{130,1},{131,5},{139,9},{138,13},... | collective-permute-start | bytes 737288 | tf_op jit(solution)/shard_map/ppermute | solution.py:517
  695.2 63.9 %collective-permute-start.109 = (bf16[960,128]{1,0:T(8,128)(2,1)}, bf16[960,128]{1,0:T(8,128)(2,1)S(1)}, u32[]{:S(2)}, u32[]{:S(2)}) collective-permute-start(bf16[960,128]{1,0:T(8,128)(2,1)} %get-tuple-element.390), channel_id=1, source_target_pairs={{192,1},{193,5},{201,9},{200,13},{194,2},{195,6},{203,10},{202,14}... | collective-permute-start | bytes 737288 | tf_op jit(solution)/shard_map/ppermute | solution.py:517
  708.3 63.1 %collective-permute-start.108 = (bf16[960,128]{1,0:T(8,128)(2,1)}, bf16[960,128]{1,0:T(8,128)(2,1)S(1)}, u32[]{:S(2)}, u32[]{:S(2)}) collective-permute-start(bf16[960,128]{1,0:T(8,128)(2,1)} %get-tuple-element.390), channel_id=1, source_target_pairs={{128,1},{129,5},{137,9},{136,13},{130,2},{131,6},{139,10},{138,14}... | collective-permute-start | bytes 737288 | tf_op jit(solution)/shard_map/ppermute | solution.py:517
  720.5 50.8 %collective-permute-start.111 = (bf16[960,128]{1,0:T(8,128)(2,1)}, bf16[960,128]{1,0:T(8,128)(2,1)S(1)}, u32[]{:S(2)}, u32[]{:S(2)}) collective-permute-start(bf16[960,128]{1,0:T(8,128)(2,1)} %get-tuple-element.391), channel_id=1, source_target_pairs={{192,2},{193,6},{201,10},{200,14},{194,3},{195,7},{203,11},{202,15... | collective-permute-start | bytes 737288 | tf_op jit(solution)/shard_map/ppermute | solution.py:517
  (206 other events, 2498.0 us)

commit v3 on v2

--- a/solution.py
+++ b/solution.py
@@ -26,15 +26,16 @@
 SM = pl.BlockSpec(memory_space=pltpu.SMEM)
 BOTH = ("segment", "tile")
 
-PAIRS = ((0, 1), (2, 6), (3, 7), (4, 8), (5, 9), (10, 14), (11, 15), (12, 13))
-FETCH_AFTER = {0: 3, 2: 4, 4: 5, 6: 6, 8: 7}
-SWAP_AFTER = {0: 1, 1: 2, 2: 3, 3: 4, 6: 5, 8: 6, 10: 7}
-GROUPS = ((2, 3, 4, 5), (6, 7, 8, 9), (10, 11, 12), (0, 1, 13, 14, 15))
-SPREAD_AFTER = {7: 0, 11: 1, 14: 2}
-SPREAD_BY = {10: 0, 14: 1, 15: 2}
-HELPERS = {0: (4, 6, 0), 1: (4, 6, 1), 13: (5, 7, 0), 14: (5, 7, 1)}
-HELPERS |= {b: (5, 7, b % 2) for b in (2, 3, 6, 7, 10, 11)}
-HELPERS |= {b: (1, 3, b % 2) for b in (4, 5, 8, 9, 12)}
+PAIRS = ((0, 1), (2, 6), (3, 7), (4, 8), (5, 9), (10, 14), (11, 15), (12,), (13,))
+ROUTES = ((0, 1), (2, 6), (3, 7), (4, 8), (5, 9), (2, 6), (3, 7), (4, 8), (5, 9))
+FETCH_AFTER = {0: 3, 2: 4, 4: 5, 6: 6, 8: 7, 9: 8}
+SWAP_AFTER = {0: 1, 1: 2, 2: 3, 3: 4, 6: 5, 8: 6, 9: 7, 10: 8}
+COLUMN = {0: 6, 1: 7, 2: 2, 3: 3, 8: 4, 9: 5, 4: 4, 5: 5, 6: 6, 7: 7, 10: 2, 11: 3, 12: 4, 13: 5}
+ROUNDS = ((0, 1, 2, 3, 8, 9), (4, 5, 6, 7, 10, 11), (12, 13))
+ROUND_AFTER = {11: 0, 13: 1, 14: 2}
+ROUND_BY = {13: 0, 15: 2}
+MOVED = {0: 6, 1: 7, 8: 12, 9: 13}
+ACTIVE_ROWS = (0, 1, 8, 9)
 
 
 def place(slot, quarter):
@@ -43,14 +44,12 @@
 
 
 def helper(block, slot, quarter):
-    if block == BLOCKS - 1:
-        return place(slot, quarter)
-    segment = 2 * HELPERS[block][slot // 4] + HELPERS[block][2]
-    return segment * TILES + quarter // 2 * 8 + place(slot, quarter) % 8
+    return (COLUMN[block] + slot // 4 * 8) * TILES + 4 * quarter + slot % 4
 
 
 def chunk_at(turn, k):
-    return pl.multiple_of(lax.rem(k + turn, 4) * PIECE, PIECE)
+    chunk = k ^ lax.rem(turn, 4)
+    return pl.multiple_of(chunk * PIECE, PIECE)
 
 
 def send_sums(info, totals, squares, source, near, cross, stats):
@@ -108,7 +107,7 @@
         final.wait()
 
 
-def block_body(at_core, next_core, up_in, up_out, last, info, *refs):
+def block_body(at_core, next_core, up_in, up_out, cut, last, info, *refs):
     refs = list(refs)
 
     def take(n):
@@ -122,15 +121,13 @@
         lateral_edges = take(2)
     if up_out:
         (lateral,), nexts = take(1), take(2)
-    if last:
-        passing = take(last)
-    wholes = take(4 if last else 1)
+    wholes = take(4 if cut else 1)
     if not last:
         near_out, cross_out, stats_out = take(3)
     if up_out:
         (summed_out,) = take(1)
     xs, result = source, wholes[0]
-    if last:
+    if cut:
         (result,) = take(1)
     ws, ps, cat, totals, squares, in_sem, w_sem, out_sem = take(8)
     if up_in:
@@ -256,44 +253,20 @@
                     totals[...] += following
                     squares[...] += following * following
 
-        if last:
+        finals = []
+        if cut:
             finals = [
                 pltpu.make_async_copy(
                     result.at[pl.ds(chunk_at(info[1], k), PIECE)], wholes[k], out_sem.at[k]
                 )
                 for k in range(4)
             ]
-        else:
-            finals = []
         for copy in finals:
             copy.start()
         if not last:
             send_sums(info, totals[...], squares[...], result, near_out, cross_out, stats_out)
         for copy in finals:
             copy.wait()
-
-    if last:
-        hand_on(info, passing, wholes, result, in_sem, out_sem)
-
-
-def hand_on(info, passing, outs, held, in_sem, out_sem):
-    for at, ref in enumerate(passing):
-
-        @pl.when(info[3] == at)
-        def _():
-            arrive = pltpu.make_async_copy(ref, held, in_sem.at[0])
-            arrive.start()
-            arrive.wait()
-            copies = [
-                pltpu.make_async_copy(
-                    held.at[pl.ds(chunk_at(info[4], k), PIECE)], outs[k], out_sem.at[k]
-                )
-                for k in range(4)
-            ]
-            for copy in copies:
-                copy.start()
-            for copy in copies:
-                copy.wait()
 
 
 EXCHANGED = [
@@ -317,15 +290,17 @@
     )(info, *pieces)
 
 
-def block_call(cores, info, source, exchanged, member, weights, lateral_edges, lateral, nexts, passing):
-    up_in, up_out, last = lateral_edges is not None, lateral is not None, len(passing)
+def block_call(cores, info, source, exchanged, member, weights, lateral_edges, lateral, nexts, cut, last):
+    up_in, up_out = lateral_edges is not None, lateral is not None
     operands = [source, *exchanged, member, *weights]
     specs = [VM] * 6 + [ANY] * 2
     shapes, out_specs = [WHOLE] + EXCHANGED, [VM] * 4
     scratch = []
+    if cut:
+        shapes, out_specs = [PART] * 4 + EXCHANGED, [ANY] * 4 + [VM] * 3
+        scratch.append(pltpu.VMEM((OWN, WIDTH), BF))
     if last:
-        shapes, out_specs = [PART] * 4, [ANY] * 4
-        scratch.append(pltpu.VMEM((OWN, WIDTH), BF))
+        shapes, out_specs = shapes[:4], out_specs[:4]
     scratch += [
         pltpu.VMEM((CH, LEAD), BF),
         pltpu.VMEM((CH, WIDTH), BF),
@@ -349,10 +324,8 @@
             pltpu.VMEM((CH, FULL - LEAD), BF),
             pltpu.SemaphoreType.DMA((2,)),
         ]
-    operands += passing
-    specs += [ANY] * last
     out = pl.pallas_call(
-        functools.partial(block_body, *cores, up_in, up_out, last),
+        functools.partial(block_body, *cores, up_in, up_out, cut, last),
         out_shape=shapes,
         in_specs=[SM] + specs,
         out_specs=out_specs,
@@ -363,13 +336,29 @@
         ),
         name="res_block",
     )(info, *operands)
-    if last:
-        return out, None, None
-    return out[0], out[1:4], out[4] if up_out else None
+    n = 4 if cut else 1
+    return out[:4] if cut else out[0], out[n : n + 3], out[n + 3] if up_out else None
 
 
 def split_body(count, info, *refs):
-    hand_on(info, refs[:count], refs[count : count + 4], *refs[count + 4 :])
+    wholes, outs, (held, in_sem, out_sem) = refs[:count], refs[count : count + 4], refs[count + 4 :]
+    for at, ref in enumerate(wholes):
+
+        @pl.when(info[0] == at)
+        def _():
+            arrive = pltpu.make_async_copy(ref, held, in_sem.at[0])
+            arrive.start()
+            arrive.wait()
+            copies = [
+                pltpu.make_async_copy(
+                    held.at[pl.ds(chunk_at(info[1], k), PIECE)], outs[k], out_sem.at[k]
+                )
+                for k in range(4)
+            ]
+            for copy in copies:
+                copy.start()
+            for copy in copies:
+                copy.wait()
 
 
 def split(info, wholes):
@@ -388,35 +377,46 @@
     )(info, *wholes)
 
 
-def collect_body(groups, info, *refs):
+def collect_body(groups, moved, info, *refs):
     out, held, in_sem, out_sem = refs[-4:]
+
+    def run(copies):
+        for arrive, _ in copies:
+            arrive.start()
+        for arrive, leave in copies:
+            arrive.wait()
+            leave.start()
+        for _, leave in copies:
+            leave.wait()
+
+    def pair(source, n, slot):
+        return (
+            pltpu.make_async_copy(source, held.at[n], in_sem.at[n]),
+            pltpu.make_async_copy(held.at[n], out.at[slot], out_sem.at[n]),
+        )
+
     for at in range(groups):
 
         @pl.when(info[0] == at)
         def _():
             copies = []
-            for k in range(4):
-                for high in range(2):
-                    slot, n = 4 * high + lax.rem(info[1] + 4 - k, 4), 2 * k + high
-                    copies.append(
-                        (
-                            pltpu.make_async_copy(refs[at * 8 + n], held.at[n], in_sem.at[n]),
-                            pltpu.make_async_copy(held.at[n], out.at[slot], out_sem.at[n]),
-                        )
-                    )
-            for arrive, _ in copies:
-                arrive.start()
-            for arrive, leave in copies:
-                arrive.wait()
-                leave.start()
-            for _, leave in copies:
-                leave.wait()
-
-
-def collect(info, received):
-    flat = [piece for group in received for piece in group]
+            for n in range(8):
+                half = info[2] if n < 4 else 1 - info[2]
+                slot = 4 * half + (info[1] ^ (n % 4))
+                copies.append(pair(refs[at * 8 + n], n, slot))
+            run(copies)
+
+    for at in range(moved):
+
+        @pl.when(info[0] == groups + at)
+        def _():
+            run([pair(refs[groups * 8 + at].at[n], n, n) for n in range(8)])
+
+
+def collect(info, received, moved=()):
+    flat = [piece for group in received for piece in group] + list(moved)
     return pl.pallas_call(
-        functools.partial(collect_body, len(received)),
+        functools.partial(collect_body, len(received), len(moved)),
         out_shape=jax.ShapeDtypeStruct((MICRO, PIECE, WIDTH), BF),
         in_specs=[SM] + [ANY] * len(flat),
         out_specs=ANY,
@@ -445,18 +445,14 @@
     slot = 4 * (tile // 8) + (tile % 8) // 2
     active = (segment < 2).astype(jnp.int32)
 
-    def info_for(group):
-        pick, passed = jnp.full((), -1, jnp.int32), (tile % 8) // 2
-        for at, block in enumerate(group):
-            if block < BLOCKS - 1:
-                *columns, its_core = HELPERS[block]
-                for half, column in enumerate(columns):
-                    ours = segment == 2 * column + its_core
-                    pick = jnp.where(ours, at, pick)
-                    passed = jnp.where(ours, passed + 4 * half, passed)
-        return jnp.stack([quarter, slot, active, pick, passed]).astype(jnp.int32)
-
-    info = info_for(())
+    info = jnp.stack([quarter, slot, active]).astype(jnp.int32)
+    inner = tile % 4
+
+    def at_segment(values, other):
+        got = jnp.full((), other, jnp.int32)
+        for its_segment, value in values.items():
+            got = jnp.where(segment == its_segment, value, got)
+        return got
 
     served = lax.dynamic_index_in_dim(
         features, plan[jnp.minimum(segment, MICRO - 1)], 0, keepdims=False
@@ -465,7 +461,7 @@
     pieces = []
     for k in range(4):
         route = [
-            (j * TILES + 4 * q + (k + j) % 4, place(j, q)) for j in range(MICRO) for q in range(4)
+            (j * TILES + 4 * q + (k ^ j % 4), place(j, q)) for j in range(MICRO) for q in range(4)
         ]
         pieces.append(lax.ppermute(served, BOTH, route))
 
@@ -482,11 +478,15 @@
     full = jnp.concatenate(columns, axis=1)
     first_up = BLOCKS - DOWN
 
-    def fetch(pair, after):
-        own = full if max(pair) >= first_up else lead
-        if after is not None:
-            own, _ = lax.optimization_barrier((own, after))
-        return lax.ppermute(own, "segment", [(pair[0], 0), (pair[1], 1)])
+    rows = [b for b in range(BLOCKS) if b not in ACTIVE_ROWS]
+    relay_route = [(b * TILES + t, (b ^ 8) * TILES + t) for b in rows for t in range(TILES)]
+    relayed = lax.ppermute(lax.optimization_barrier((full, pieces[-1]))[0], BOTH, relay_route)
+
+    def fetch(index, after):
+        own = relayed if PAIRS[index][0] >= 10 else lead
+        own, _ = lax.optimization_barrier((own, after))
+        first, second = ROUTES[index]
+        return lax.ppermute(own, "segment", [(first, 0), (second, 1)])
 
     def exchange(near, cross, stats):
         other_tile = [(t, t ^ 1) for t in range(TILES)]
@@ -504,19 +504,38 @@
         route = [(place(j, q), helper(block, j, q)) for j in range(MICRO) for q in range(4)]
         return lax.ppermute(whole, BOTH, route)
 
-    def spread(group, outs):
+    def spread(at):
+        group = ROUNDS[at]
+        values = {COLUMN[b] + far: n for n, b in enumerate(group) for far in (0, 8)}
+        outs = split(
+            jnp.stack([at_segment(values, -1), inner]).astype(jnp.int32),
+            [passing[b] for b in group],
+        )
+        got = [outs[0]]
+        for far in (0, 8):
+            for k in range(4):
+                if k or far:
+                    route = [(b * TILES + t, (b ^ far) * TILES + (t ^ k)) for b in rows for t in range(TILES)]
+                    got.append(lax.ppermute(outs[k], BOTH, route))
+        return got
+
+    def straight(outs):
         got = []
-        for k in range(4):
-            for high in range(2):
+        for high in range(2):
+            for k in range(4):
                 route = [
-                    (helper(block, j, q), block * TILES + 4 * q + (k + j) % 4)
-                    for block in group
+                    (place(j, q), (BLOCKS - 1) * TILES + 4 * q + (k ^ j % 4))
                     for j in range(4 * high, 4 * high + 4)
                     for q in range(4)
                 ]
                 got.append(lax.ppermute(outs[k], BOTH, route))
         return got
 
+    def collect_at(values, received, moved=(), high_half=segment // 8):
+        chosen = jnp.stack([at_segment(values, -1), inner, high_half]).astype(jnp.int32)
+        return collect(chosen, received, moved)
+
+    other_core = [(b, b ^ 1) for b in range(BLOCKS)]
     member_at = jnp.arange(CH) // GROUP
     member = (member_at[:, None] == member_at[None, :]).astype(BF)
     weights, cores, fetched = {}, {}, {}
@@ -529,8 +548,8 @@
     swap_cores(0, lead)
     *exchanged, source = first_call(info, pieces)
     for index in (1, 2):
-        fetched[index] = fetch(PAIRS[index], pieces[-1])
-    wholes, edges_of, passing, received = [], {}, [], []
+        fetched[index] = fetch(index, pieces[-1])
+    wholes, edges_of, passing, received = [], {}, [], {}
     for block in range(BLOCKS):
         up_in, up_out = block >= first_up, first_up - 1 <= block < BLOCKS - 1
         near, cross, stats = exchanged
@@ -540,13 +559,20 @@
             source, near_in, cross_in, far, passing[block - 2] = lax.optimization_barrier(
                 (source, near_in, cross_in, far, passing[block - 2])
             )
-        if block in SPREAD_BY:
-            at = SPREAD_BY[block]
+        if block - 1 in ROUND_AFTER:
+            received[ROUND_AFTER[block - 1]] = spread(ROUND_AFTER[block - 1])
+        if block in ROUND_BY:
+            at = ROUND_BY[block]
             source, received[at] = lax.optimization_barrier((source, received[at]))
-        last = block == BLOCKS - 1
+        if block == 13:
+            values = {its_segment: 0 for its_segment in MOVED.values()}
+            moving = collect_at(values, [received[0]])
+            route = [(source_of * TILES + t, b * TILES + t) for b, source_of in MOVED.items() for t in range(TILES)]
+            moved = lax.ppermute(moving, BOTH, route)
+        cut, last = block >= BLOCKS - 2, block == BLOCKS - 1
         whole, exchanged, summed = block_call(
             (cores[block], cores.get(block + 1, 0)),
-            info_for(GROUPS[-1]) if last else info,
+            info,
             source,
             (near_in, cross_in, stats, far),
             member,
@@ -554,29 +580,31 @@
             edges_of[BLOCKS - block] if up_in else None,
             wholes[BLOCKS - 2 - block] if up_out else None,
             weights[block + 1] if up_out else None,
-            [passing[b] for b in GROUPS[-1][:-1]] if last else [],
+            cut,
+            last,
         )
         wholes.append(whole)
         source = summed if up_out else whole
-        if not last:
+        if cut:
+            received[block] = straight(whole)
+        else:
             passing.append(hand_over(block, whole))
-        if block in SPREAD_AFTER:
-            group = GROUPS[SPREAD_AFTER[block]]
-            outs = split(info_for(group), [passing[b] for b in group])
-            received.append(spread(group, outs))
         if block in SWAP_AFTER:
             index = SWAP_AFTER[block]
             own, _ = lax.optimization_barrier((fetched[index], whole))
             swap_cores(index, own)
         if block in FETCH_AFTER:
             index = FETCH_AFTER[block]
-            fetched[index] = fetch(PAIRS[index], whole)
-    received.append(spread(GROUPS[-1], whole))
-    group_of = jnp.zeros((), jnp.int32)
-    for at, group in enumerate(GROUPS):
-        for block in group:
-            group_of = jnp.where(segment == block, at, group_of)
-    out = collect(jnp.stack([group_of, tile % 4]).astype(jnp.int32), received)
+            fetched[index] = fetch(index, whole)
+    zero = jnp.zeros((), jnp.int32)
+    early = collect_at({BLOCKS - 1: 0}, [received[BLOCKS - 2]], high_half=zero)
+    swapped = lax.ppermute(early, "segment", other_core)
+    values = {BLOCKS - 1: 3, BLOCKS - 2: 4} | {b: 5 for b in MOVED}
+    for at, group in enumerate(ROUNDS):
+        values |= {b: at for b in group if b not in MOVED}
+    half = jnp.where(segment == BLOCKS - 1, 0, segment // 8)
+    lists = [received[0], received[1], received[2], received[BLOCKS - 1]]
+    out = collect_at(values, lists, [swapped, moved], half)
     out = out.reshape(1, MICRO, 3, CH, WIDTH)
     return out.transpose(0, 1, 2, 4, 3)
 

time: 826 us -> 1170 us (1.42)
  waiting for transfers between devices: 97.6 us -> 526 us
  starting transfers between devices: 557 us -> 495 us
  Pallas kernels: 78 us -> 45.2 us
    ppermute x7 -> x27, waiting for transfers between devices: 0.02 us -> 278 us  [the longest x16 254 us: straight(): got.append(lax.ppermute(outs[k], BOTH, route))]
    ppermute x32 -> x21, starting transfers between devices: 374 us -> 136 us  [spread(): got.append(lax.ppermute(outs[k], BOTH, route))]
    ppermute x16, starting transfers between devices: 12.4 us -> 209 us  [exchange(): lax.ppermute(near, 'tile', other_tile)]
    ppermute x15 -> x14, waiting for transfers between devices: 0.04 us -> 120 us  [hand_over(): return lax.ppermute(whole, BOTH, route)]
    ppermute x16, starting transfers between devices: 111 us -> 19.9 us  [exchange(): lax.ppermute(stats, BOTH, both)]
    ppermute x8 -> x9, starting transfers between devices: 6.5 us -> 54.8 us  [swap_cores(): lax.ppermute(own, 'segment', [(b, b ^ 1) for b in range(BLOCKS)])]
    ppermute x32 -> x21, waiting for transfers between devices: 47.3 us -> 79.7 us  [spread(): got.append(lax.ppermute(outs[k], BOTH, route))]
    pallas_call x17 -> x19, Pallas kernels: 70.7 us -> 39.5 us  [the longest x16 30.8 us: block_call(): pl.pallas_call(functools.partial(block_body, *cores, up_in, up_out, cut,...]
  transfers between devices with their start and end apart: 114 -> 123, of which waited for: 35 -> 52; matrix products, arithmetic and copies ran while one was open for 1% -> 1% of each run, Pallas kernels for 9% -> 3%
where the time goes in v3:
time: 1170 us; the launch traced here: 1160 us
  waiting for transfers between devices  526 us (45%)
  starting transfers between devices  495 us (42%)
  local copies, waits for them, and re-layouts  80.8 us (7%)
  Pallas kernels  45.2 us (4%)
    ppermute x16, waiting for transfers between devices, straight(): got.append(lax.ppermute(outs[k], BOTH, route))  254 us
    ppermute x16, starting transfers between devices, exchange(): lax.ppermute(near, 'tile', other_tile)  209 us
    ppermute x21, starting transfers between devices, spread(): got.append(lax.ppermute(outs[k], BOTH, route))  136 us
    ppermute x14, waiting for transfers between devices, hand_over(): return lax.ppermute(whole, BOTH, route)  120 us
    ppermute x21, waiting for transfers between devices, spread(): got.append(lax.ppermute(outs[k], BOTH, route))  79.7 us
    unnamed x301, local copies, waits for them, and re-layouts  70.2 us
    ppermute x9, starting transfers between devices, swap_cores(): lax.ppermute(own, 'segment', [(b, b ^ 1) for b in range(BLOCKS)])  54.8 us
    pallas_call x16, Pallas kernels, block_call(): pl.pallas_call(functools.partial(block_body, *cores, up_in, up_out, cut,...  30.8 us
  transfers between devices with their start and end apart: 123, of which 52 were waited for; matrix products, arithmetic and copies ran while one was open for 1% of the time, Pallas kernels for 3%

profile of v3, /device:TPU:59, one launch (start us, length us, event | category | flops | bytes accessed | tf_op | source)
XLA Modules:
  0.0 1155.2 jit_solution(7423921952601789008)
XLA Ops:
  49.9 50.2 %collective-permute-start.28 = (bf16[320,2944]{1,0:T(8,128)(2,1)}, bf16[320,2944]{1,0:T(8,128)(2,1)}, u32[]{:S(2)}, u32[]{:S(2)}) collective-permute-start(bf16[320,2944]{1,0:T(8,128)(2,1)} %collective-permute-done.27.refs_6_), channel_id=1, source_target_pairs={{0,16},{16,0},{32,48},{48,32},{64,80},{80,64},{96,112},{112,96},{1... | collective-permute-start | bytes 5652488 | tf_op jit(solution)/shard_map/ppermute | solution.py:544
  100.5 79.0 %collective-permute-done.20.refs_1_ = bf16[3840,128]{1,0:T(8,128)(2,1)S(1)} collective-permute-done((bf16[3840,128]{1,0:T(8,128)(2,1)S(1)}, bf16[3840,128]{1,0:T(8,128)(2,1)S(1)}, u32[]{:S(2)}, u32[]{:S(2)}) %collective-permute-start.20) | collective-permute-done | bytes 983072 | tf_op jit(solution)/shard_map/ppermute | solution.py:505
  192.6 12.0 %collective-permute-start.55 = (bf16[320,3328]{1,0:T(8,128)(2,1)}, bf16[320,3328]{1,0:T(8,128)(2,1)S(1)}, u32[]{:S(2)}, u32[]{:S(2)}) collective-permute-start(bf16[320,3328]{1,0:T(8,128)(2,1)} %concatenate.20), channel_id=1, source_target_pairs={{32,160},{33,161},{34,162},{35,163},{36,164},{37,165},{38,166},{39... | collective-permute-start | bytes 6389768 | tf_op jit(solution)/shard_map/ppermute | solution.py:483
  226.7 24.3 %collective-permute-done.55 = bf16[320,3328]{1,0:T(8,128)(2,1)S(1)} collective-permute-done((bf16[320,3328]{1,0:T(8,128)(2,1)}, bf16[320,3328]{1,0:T(8,128)(2,1)S(1)}, u32[]{:S(2)}, u32[]{:S(2)}) %collective-permute-start.55) | collective-permute-done | bytes 2129952 | tf_op jit(solution)/shard_map/ppermute | solution.py:483
  275.8 196.7 %collective-permute-start.47 = (bf16[368,128]{1,0:T(8,128)(2,1)S(1)}, bf16[368,128]{1,0:T(8,128)(2,1)S(1)}, u32[]{:S(2)}, u32[]{:S(2)}) collective-permute-start(bf16[368,128]{1,0:T(8,128)(2,1)S(1)} %get-tuple-element.268), channel_id=1, source_target_pairs={{0,1},{1,0},{2,3},{3,2},{4,5},{5,4},{6,7},{7,6},{8,9},{9,8},{10,11... | collective-permute-start | bytes 282632 | tf_op jit(solution)/shard_map/ppermute | solution.py:498
  476.3 40.6 %collective-permute-done.50.refs_3_ = bf16[3840,128]{1,0:T(8,128)(2,1)S(1)} collective-permute-done((bf16[3840,128]{1,0:T(8,128)(2,1)S(1)}, bf16[3840,128]{1,0:T(8,128)(2,1)S(1)}, u32[]{:S(2)}, u32[]{:S(2)}) %collective-permute-start.50) | collective-permute-done | bytes 983072 | tf_op jit(solution)/shard_map/ppermute | solution.py:505
  571.8 7.8 res_block.28
  583.7 65.9 %collective-permute-start.81 = (bf16[960,128]{1,0:T(8,128)(2,1)S(1)}, bf16[960,128]{1,0:T(8,128)(2,1)S(1)}, u32[]{:S(2)}, u32[]{:S(2)}) collective-permute-start(bf16[960,128]{1,0:T(8,128)(2,1)S(1)} %get-tuple-element.322), channel_id=1, source_target_pairs={{32,162},{33,163},{34,160},{35,161},{36,166},{37,167},{38,164},{39... | collective-permute-start | bytes 737288 | tf_op jit(solution)/shard_map/ppermute | solution.py:519
  661.4 14.9 %collective-permute-done.81.refs_6_ = bf16[960,128]{1,0:T(8,128)(2,1)S(1)} collective-permute-done((bf16[960,128]{1,0:T(8,128)(2,1)S(1)}, bf16[960,128]{1,0:T(8,128)(2,1)S(1)}, u32[]{:S(2)}, u32[]{:S(2)}) %collective-permute-start.81) | collective-permute-done | bytes 245792 | tf_op jit(solution)/shard_map/ppermute | solution.py:519
  676.4 5.3 collective-permute-done.77.refs_2_
  681.6 5.3 collective-permute-done.82.refs_7_
  686.9 5.3 collective-permute-done.78.refs_3_
  699.5 9.5 res_block.30
  724.1 186.7 %collective-permute-done.117.refs_4_ = bf16[960,128]{1,0:T(8,128)(2,1)} collective-permute-done((bf16[960,128]{1,0:T(8,128)(2,1)}, bf16[960,128]{1,0:T(8,128)(2,1)}, u32[]{:S(2)}, u32[]{:S(2)}) %collective-permute-start.117) | collective-permute-done | bytes 245792 | tf_op jit(solution)/shard_map/ppermute | solution.py:531
  912.0 38.0 %collective-permute-done.113.refs_0_ = bf16[960,128]{1,0:T(8,128)(2,1)} collective-permute-done((bf16[960,128]{1,0:T(8,128)(2,1)}, bf16[960,128]{1,0:T(8,128)(2,1)}, u32[]{:S(2)}, u32[]{:S(2)}) %collective-permute-start.113) | collective-permute-done | bytes 245792 | tf_op jit(solution)/shard_map/ppermute | solution.py:531
  970.8 14.4 %collective-permute-start.102 = (bf16[960,128]{1,0:T(8,128)(2,1)S(1)}, bf16[960,128]{1,0:T(8,128)(2,1)S(1)}, u32[]{:S(2)}, u32[]{:S(2)}) collective-permute-start(bf16[960,128]{1,0:T(8,128)(2,1)S(1)} %get-tuple-element.364), channel_id=1, source_target_pairs={{32,161},{33,160},{34,163},{35,162},{36,165},{37,164},{38,167},{39... | collective-permute-start | bytes 737288 | tf_op jit(solution)/shard_map/ppermute | solution.py:519
  999.5 10.7 collective-permute-done.103.refs_22_
  1017.3 5.0 collective-permute-start.86
  1023.0 8.0 collective-permute-done.104.refs_23_
  1050.6 12.0 %collective-permute-done.88.refs_14_ = bf16[960,128]{1,0:T(8,128)(2,1)S(1)} collective-permute-done((bf16[960,128]{1,0:T(8,128)(2,1)S(1)}, bf16[960,128]{1,0:T(8,128)(2,1)S(1)}, u32[]{:S(2)}, u32[]{:S(2)}) %collective-permute-start.88) | collective-permute-done | bytes 245792 | tf_op jit(solution)/shard_map/ppermute | solution.py:519
  1072.3 6.7 collective-permute-done.89.refs_15_
  1081.0 5.7 collective-permute-done.85.refs_11_
  1094.2 8.5 collective-permute-done.110.refs_29_
  1109.0 9.0 collective-permute-done.107.refs_26_
  (572 shorter events, 328.9 us)
Async XLA Ops:
  43.9 140.0 %collective-permute-start.22 = (bf16[320,2944]{1,0:T(8,128)(2,1)S(1)}, bf16[320,2944]{1,0:T(8,128)(2,1)S(1)}, u32[]{:S(2)}, u32[]{:S(2)}) collective-permute-start(bf16[320,2944]{1,0:T(8,128)(2,1)S(1)} %collective-permute-done.21.refs_6_), channel_id=1, source_target_pairs={{0,16},{16,0},{32,48},{48,32},{64,80},{80,64},{96,112},{112,96},{1... | collective-permute-start | bytes 5652488 | tf_op jit(solution)/shard_map/ppermute | solution.py:544
  46.6 138.6 %collective-permute-start.33 = (bf16[320,2944]{1,0:T(8,128)(2,1)}, bf16[320,2944]{1,0:T(8,128)(2,1)}, u32[]{:S(2)}, u32[]{:S(2)}) collective-permute-start(bf16[320,2944]{1,0:T(8,128)(2,1)} %concatenate.19.refs_6_), channel_id=1, source_target_pairs={{80,0},{144,16},{81,1},{145,17},{82,2},{146,18},{83,3},{147,19},{8... | collective-permute-start | bytes 5652488 | tf_op jit(solution)/shard_map/ppermute | solution.py:489
  48.6 130.9 %collective-permute-start.20 = (bf16[3840,128]{1,0:T(8,128)(2,1)S(1)}, bf16[3840,128]{1,0:T(8,128)(2,1)S(1)}, u32[]{:S(2)}, u32[]{:S(2)}) collective-permute-start(bf16[3840,128]{1,0:T(8,128)(2,1)S(1)} %get-tuple-element.208.refs_0_.refs_10_), channel_id=1, source_target_pairs={{0,112},{1,116},{17,120},{16,124},{2,113},{3,117},{19,121},{18,125... | collective-permute-start | bytes 2949128 | tf_op jit(solution)/shard_map/ppermute | solution.py:505
  49.9 165.0 %collective-permute-start.28 = (bf16[320,2944]{1,0:T(8,128)(2,1)}, bf16[320,2944]{1,0:T(8,128)(2,1)}, u32[]{:S(2)}, u32[]{:S(2)}) collective-permute-start(bf16[320,2944]{1,0:T(8,128)(2,1)} %collective-permute-done.27.refs_6_), channel_id=1, source_target_pairs={{0,16},{16,0},{32,48},{48,32},{64,80},{80,64},{96,112},{112,96},{1... | collective-permute-start | bytes 5652488 | tf_op jit(solution)/shard_map/ppermute | solution.py:544
  100.1 80.4 %collective-permute-start.19 = (bf16[48,128]{1,0:T(8,128)(2,1)S(1)}, bf16[48,128]{1,0:T(8,128)(2,1)S(1)}, u32[]{:S(2)}, u32[]{:S(2)}) collective-permute-start(bf16[48,128]{1,0:T(8,128)(2,1)S(1)} %get-tuple-element.217.refs_3_), channel_id=1, source_target_pairs={{0,17},{1,16},{2,19},{3,18},{4,21},{5,20},{6,23},{7,22},{8,25},{9,... | collective-permute-start | bytes 36872 | tf_op jit(solution)/shard_map/ppermute | solution.py:500
  192.6 58.4 %collective-permute-start.55 = (bf16[320,3328]{1,0:T(8,128)(2,1)}, bf16[320,3328]{1,0:T(8,128)(2,1)S(1)}, u32[]{:S(2)}, u32[]{:S(2)}) collective-permute-start(bf16[320,3328]{1,0:T(8,128)(2,1)} %concatenate.20), channel_id=1, source_target_pairs={{32,160},{33,161},{34,162},{35,163},{36,164},{37,165},{38,166},{39... | collective-permute-start | bytes 6389768 | tf_op jit(solution)/shard_map/ppermute | solution.py:483
  267.8 256.0 %collective-permute-start.62 = (bf16[320,3328]{1,0:T(8,128)(2,1)S(1)}, bf16[320,3328]{1,0:T(8,128)(2,1)S(1)}, u32[]{:S(2)}, u32[]{:S(2)}) collective-permute-start(bf16[320,3328]{1,0:T(8,128)(2,1)S(1)} %collective-permute-done.55), channel_id=1, source_target_pairs={{48,0},{112,16},{49,1},{113,17},{50,2},{114,18},{51,3},{115,19},{5... | collective-permute-start | bytes 6389768 | tf_op jit(solution)/shard_map/ppermute | solution.py:489
  268.6 248.3 %collective-permute-start.50 = (bf16[3840,128]{1,0:T(8,128)(2,1)S(1)}, bf16[3840,128]{1,0:T(8,128)(2,1)S(1)}, u32[]{:S(2)}, u32[]{:S(2)}) collective-permute-start(bf16[3840,128]{1,0:T(8,128)(2,1)S(1)} %get-tuple-element.263.refs_0_), channel_id=1, source_target_pairs={{0,112},{1,116},{17,120},{16,124},{2,113},{3,117},{19,121},{18,125... | collective-permute-start | bytes 2949128 | tf_op jit(solution)/shard_map/ppermute | solution.py:505
  270.9 253.0 %collective-permute-start.64 = (bf16[320,3328]{1,0:T(8,128)(2,1)S(1)}, bf16[320,3328]{1,0:T(8,128)(2,1)S(1)}, u32[]{:S(2)}, u32[]{:S(2)}) collective-permute-start(bf16[320,3328]{1,0:T(8,128)(2,1)S(1)} %collective-permute-done.55), channel_id=1, source_target_pairs={{64,0},{128,16},{65,1},{129,17},{66,2},{130,18},{67,3},{131,19},{6... | collective-permute-start | bytes 6389768 | tf_op jit(solution)/shard_map/ppermute | solution.py:489
  271.7 200.8 %collective-permute-start.49 = (bf16[48,128]{1,0:T(8,128)(2,1)S(1)}, bf16[48,128]{1,0:T(8,128)(2,1)S(1)}, u32[]{:S(2)}, u32[]{:S(2)}) collective-permute-start(bf16[48,128]{1,0:T(8,128)(2,1)S(1)} %get-tuple-element.270.refs_3_), channel_id=1, source_target_pairs={{0,17},{1,16},{2,19},{3,18},{4,21},{5,20},{6,23},{7,22},{8,25},{9,... | collective-permute-start | bytes 36872 | tf_op jit(solution)/shard_map/ppermute | solution.py:500
  275.8 199.6 %collective-permute-start.47 = (bf16[368,128]{1,0:T(8,128)(2,1)S(1)}, bf16[368,128]{1,0:T(8,128)(2,1)S(1)}, u32[]{:S(2)}, u32[]{:S(2)}) collective-permute-start(bf16[368,128]{1,0:T(8,128)(2,1)S(1)} %get-tuple-element.268), channel_id=1, source_target_pairs={{0,1},{1,0},{2,3},{3,2},{4,5},{5,4},{6,7},{7,6},{8,9},{9,8},{10,11... | collective-permute-start | bytes 282632 | tf_op jit(solution)/shard_map/ppermute | solution.py:498
  475.4 52.4 %collective-permute-start.57 = (bf16[320,3328]{1,0:T(8,128)(2,1)S(1)}, bf16[320,3328]{1,0:T(8,128)(2,1)S(1)}, u32[]{:S(2)}, u32[]{:S(2)}) collective-permute-start(bf16[320,3328]{1,0:T(8,128)(2,1)S(1)} %collective-permute-done.56.refs_6_.refs_11_), channel_id=1, source_target_pairs={{0,16},{16,0},{32,48},{48,32},{64,80},{80,64},{96,112},{112,96},{1... | collective-permute-start | bytes 6389768 | tf_op jit(solution)/shard_map/ppermute | solution.py:544
  548.2 108.6 %collective-permute-start.75 = (bf16[3840,128]{1,0:T(8,128)(2,1)}, bf16[3840,128]{1,0:T(8,128)(2,1)}, u32[]{:S(2)}, u32[]{:S(2)}) collective-permute-start(bf16[3840,128]{1,0:T(8,128)(2,1)} %get-tuple-element.312), channel_id=1, source_target_pairs={{0,48},{1,52},{17,56},{16,60},{2,49},{3,53},{19,57},{18,61},{4,50}... | collective-permute-start | bytes 2949128 | tf_op jit(solution)/shard_map/ppermute | solution.py:505
  563.5 86.1 %collective-permute-start.76 = (bf16[960,128]{1,0:T(8,128)(2,1)S(1)}, bf16[960,128]{1,0:T(8,128)(2,1)S(1)}, u32[]{:S(2)}, u32[]{:S(2)}) collective-permute-start(bf16[960,128]{1,0:T(8,128)(2,1)S(1)} %get-tuple-element.321), channel_id=1, source_target_pairs={{32,33},{33,32},{34,35},{35,34},{36,37},{37,36},{38,39},{39,38},{4... | collective-permute-start | bytes 737288 | tf_op jit(solution)/shard_map/ppermute | solution.py:519
  579.6 79.4 %collective-permute-start.72 = (bf16[368,128]{1,0:T(8,128)(2,1)S(1)}, bf16[368,128]{1,0:T(8,128)(2,1)S(1)}, u32[]{:S(2)}, u32[]{:S(2)}) collective-permute-start(bf16[368,128]{1,0:T(8,128)(2,1)S(1)} %get-tuple-element.309), channel_id=1, source_target_pairs={{0,1},{1,0},{2,3},{3,2},{4,5},{5,4},{6,7},{7,6},{8,9},{9,8},{10,11... | collective-permute-start | bytes 282632 | tf_op jit(solution)/shard_map/ppermute | solution.py:498
  581.9 70.9 %collective-permute-start.74 = (bf16[48,128]{1,0:T(8,128)(2,1)S(1)}, bf16[48,128]{1,0:T(8,128)(2,1)S(1)}, u32[]{:S(2)}, u32[]{:S(2)}) collective-permute-start(bf16[48,128]{1,0:T(8,128)(2,1)S(1)} %get-tuple-element.311.refs_3_), channel_id=1, source_target_pairs={{0,17},{1,16},{2,19},{3,18},{4,21},{5,20},{6,23},{7,22},{8,25},{9,... | collective-permute-start | bytes 36872 | tf_op jit(solution)/shard_map/ppermute | solution.py:500
  583.7 92.7 %collective-permute-start.81 = (bf16[960,128]{1,0:T(8,128)(2,1)S(1)}, bf16[960,128]{1,0:T(8,128)(2,1)S(1)}, u32[]{:S(2)}, u32[]{:S(2)}) collective-permute-start(bf16[960,128]{1,0:T(8,128)(2,1)S(1)} %get-tuple-element.322), channel_id=1, source_target_pairs={{32,162},{33,163},{34,160},{35,161},{36,166},{37,167},{38,164},{39... | collective-permute-start | bytes 737288 | tf_op jit(solution)/shard_map/ppermute | solution.py:519
  710.4 200.4 %collective-permute-start.117 = (bf16[960,128]{1,0:T(8,128)(2,1)}, bf16[960,128]{1,0:T(8,128)(2,1)}, u32[]{:S(2)}, u32[]{:S(2)}) collective-permute-start(bf16[960,128]{1,0:T(8,128)(2,1)} %get-tuple-element.383), channel_id=1, source_target_pairs={{8,240},{9,244},{25,248},{24,252},{10,241},{11,245},{27,249},{26,2... | collective-permute-start | bytes 737288 | tf_op jit(solution)/shard_map/ppermute | solution.py:531
  711.6 238.4 %collective-permute-start.113 = (bf16[960,128]{1,0:T(8,128)(2,1)}, bf16[960,128]{1,0:T(8,128)(2,1)}, u32[]{:S(2)}, u32[]{:S(2)}) collective-permute-start(bf16[960,128]{1,0:T(8,128)(2,1)} %get-tuple-element.383), channel_id=1, source_target_pairs={{0,240},{1,244},{17,248},{16,252},{2,241},{3,245},{19,249},{18,253... | collective-permute-start | bytes 737288 | tf_op jit(solution)/shard_map/ppermute | solution.py:531
  712.9 238.4 %collective-permute-start.118 = (bf16[960,128]{1,0:T(8,128)(2,1)}, bf16[960,128]{1,0:T(8,128)(2,1)}, u32[]{:S(2)}, u32[]{:S(2)}) collective-permute-start(bf16[960,128]{1,0:T(8,128)(2,1)} %get-tuple-element.384), channel_id=1, source_target_pairs={{8,241},{9,245},{25,249},{24,253},{10,240},{11,244},{27,248},{26,2... | collective-permute-start | bytes 737288 | tf_op jit(solution)/shard_map/ppermute | solution.py:531
  721.4 234.5 %collective-permute-start.114 = (bf16[960,128]{1,0:T(8,128)(2,1)}, bf16[960,128]{1,0:T(8,128)(2,1)}, u32[]{:S(2)}, u32[]{:S(2)}) collective-permute-start(bf16[960,128]{1,0:T(8,128)(2,1)} %get-tuple-element.384), channel_id=1, source_target_pairs={{0,241},{1,245},{17,249},{16,253},{2,240},{3,244},{19,248},{18,252... | collective-permute-start | bytes 737288 | tf_op jit(solution)/shard_map/ppermute | solution.py:531
  722.8 236.1 %collective-permute-start.119 = (bf16[960,128]{1,0:T(8,128)(2,1)}, bf16[960,128]{1,0:T(8,128)(2,1)}, u32[]{:S(2)}, u32[]{:S(2)}) collective-permute-start(bf16[960,128]{1,0:T(8,128)(2,1)} %copy-done.137), channel_id=1, source_target_pairs={{8,242},{9,246},{25,250},{24,254},{10,243},{11,247},{27,251},{26,2... | collective-permute-start | bytes 737288 | tf_op jit(solution)/shard_map/ppermute | solution.py:531
  958.9 164.4 %collective-permute-start.122 = (bf16[8,960,128]{2,1,0:T(8,128)(2,1)}, bf16[8,960,128]{2,1,0:T(8,128)(2,1)}, u32[]{:S(2)}, u32[]{:S(2)}) collective-permute-start(bf16[8,960,128]{2,1,0:T(8,128)(2,1)} %collect.4), channel_id=1, source_target_pairs={{96,0},{97,1},{98,2},{99,3},{100,4},{101,5},{102,6},{103,7},{104,8... | collective-permute-start | bytes 5898248 | tf_op jit(solution)/shard_map/ppermute | solution.py:571
  970.7 152.6 %collective-permute-start.121 = (bf16[8,960,128]{2,1,0:T(8,128)(2,1)}, bf16[8,960,128]{2,1,0:T(8,128)(2,1)}, u32[]{:S(2)}, u32[]{:S(2)}) collective-permute-start(bf16[8,960,128]{2,1,0:T(8,128)(2,1)} %collect.3), channel_id=1, source_target_pairs={{0,16},{16,0},{32,48},{48,32},{64,80},{80,64},{96,112},{112,96},{1... | collective-permute-start | bytes 5898248 | tf_op jit(solution)/shard_map/ppermute | solution.py:601
  (249 other events, 3508.4 us)

commit v4 on v2

--- a/solution.py
+++ b/solution.py
@@ -29,12 +29,6 @@
 PAIRS = ((0, 1), (2, 6), (3, 7), (4, 8), (5, 9), (10, 14), (11, 15), (12, 13))
 FETCH_AFTER = {0: 3, 2: 4, 4: 5, 6: 6, 8: 7}
 SWAP_AFTER = {0: 1, 1: 2, 2: 3, 3: 4, 6: 5, 8: 6, 10: 7}
-GROUPS = ((2, 3, 4, 5), (6, 7, 8, 9), (10, 11, 12), (0, 1, 13, 14, 15))
-SPREAD_AFTER = {7: 0, 11: 1, 14: 2}
-SPREAD_BY = {10: 0, 14: 1, 15: 2}
-HELPERS = {0: (4, 6, 0), 1: (4, 6, 1), 13: (5, 7, 0), 14: (5, 7, 1)}
-HELPERS |= {b: (5, 7, b % 2) for b in (2, 3, 6, 7, 10, 11)}
-HELPERS |= {b: (1, 3, b % 2) for b in (4, 5, 8, 9, 12)}
 
 
 def place(slot, quarter):
@@ -43,14 +37,12 @@
 
 
 def helper(block, slot, quarter):
-    if block == BLOCKS - 1:
-        return place(slot, quarter)
-    segment = 2 * HELPERS[block][slot // 4] + HELPERS[block][2]
-    return segment * TILES + quarter // 2 * 8 + place(slot, quarter) % 8
+    return (block % 8 + slot // 4 * 8) * TILES + 4 * quarter + slot % 4
 
 
 def chunk_at(turn, k):
-    return pl.multiple_of(lax.rem(k + turn, 4) * PIECE, PIECE)
+    chunk = k ^ lax.rem(turn, 4)
+    return pl.multiple_of(chunk * PIECE, PIECE)
 
 
 def send_sums(info, totals, squares, source, near, cross, stats):
@@ -122,17 +114,13 @@
         lateral_edges = take(2)
     if up_out:
         (lateral,), nexts = take(1), take(2)
-    if last:
-        passing = take(last)
-    wholes = take(4 if last else 1)
+    (result,) = take(1)
     if not last:
         near_out, cross_out, stats_out = take(3)
     if up_out:
         (summed_out,) = take(1)
-    xs, result = source, wholes[0]
-    if last:
-        (result,) = take(1)
-    ws, ps, cat, totals, squares, in_sem, w_sem, out_sem = take(8)
+    xs = source
+    ws, ps, cat, totals, squares, w_sem = take(6)
     if up_in:
         (sk_in,) = take(1)
     if up_out:
@@ -256,44 +244,8 @@
                     totals[...] += following
                     squares[...] += following * following
 
-        if last:
-            finals = [
-                pltpu.make_async_copy(
-                    result.at[pl.ds(chunk_at(info[1], k), PIECE)], wholes[k], out_sem.at[k]
-                )
-                for k in range(4)
-            ]
-        else:
-            finals = []
-        for copy in finals:
-            copy.start()
         if not last:
             send_sums(info, totals[...], squares[...], result, near_out, cross_out, stats_out)
-        for copy in finals:
-            copy.wait()
-
-    if last:
-        hand_on(info, passing, wholes, result, in_sem, out_sem)
-
-
-def hand_on(info, passing, outs, held, in_sem, out_sem):
-    for at, ref in enumerate(passing):
-
-        @pl.when(info[3] == at)
-        def _():
-            arrive = pltpu.make_async_copy(ref, held, in_sem.at[0])
-            arrive.start()
-            arrive.wait()
-            copies = [
-                pltpu.make_async_copy(
-                    held.at[pl.ds(chunk_at(info[4], k), PIECE)], outs[k], out_sem.at[k]
-                )
-                for k in range(4)
-            ]
-            for copy in copies:
-                copy.start()
-            for copy in copies:
-                copy.wait()
 
 
 EXCHANGED = [
@@ -302,7 +254,6 @@
     jax.ShapeDtypeStruct((STATS, WIDTH), BF),
 ]
 WHOLE = jax.ShapeDtypeStruct((OWN, WIDTH), BF)
-PART = jax.ShapeDtypeStruct((PIECE, WIDTH), BF)
 
 
 def first_call(info, pieces):
@@ -317,24 +268,20 @@
     )(info, *pieces)
 
 
-def block_call(cores, info, source, exchanged, member, weights, lateral_edges, lateral, nexts, passing):
-    up_in, up_out, last = lateral_edges is not None, lateral is not None, len(passing)
+def block_call(cores, info, source, exchanged, member, weights, lateral_edges, lateral, nexts, last):
+    up_in, up_out = lateral_edges is not None, lateral is not None
     operands = [source, *exchanged, member, *weights]
     specs = [VM] * 6 + [ANY] * 2
     shapes, out_specs = [WHOLE] + EXCHANGED, [VM] * 4
-    scratch = []
     if last:
-        shapes, out_specs = [PART] * 4, [ANY] * 4
-        scratch.append(pltpu.VMEM((OWN, WIDTH), BF))
-    scratch += [
+        shapes, out_specs = shapes[:1], out_specs[:1]
+    scratch = [
         pltpu.VMEM((CH, LEAD), BF),
         pltpu.VMEM((CH, WIDTH), BF),
         pltpu.VMEM((CAT, (ROWS + 2) * WIDTH), BF),
         pltpu.VMEM((CH, WIDTH), F32),
         pltpu.VMEM((CH, WIDTH), F32),
-        pltpu.SemaphoreType.DMA((1,)),
         pltpu.SemaphoreType.DMA((3,)),
-        pltpu.SemaphoreType.DMA((4,)),
     ]
     if up_in:
         operands += list(lateral_edges)
@@ -349,8 +296,6 @@
             pltpu.VMEM((CH, FULL - LEAD), BF),
             pltpu.SemaphoreType.DMA((2,)),
         ]
-    operands += passing
-    specs += [ANY] * last
     out = pl.pallas_call(
         functools.partial(block_body, *cores, up_in, up_out, last),
         out_shape=shapes,
@@ -363,47 +308,22 @@
         ),
         name="res_block",
     )(info, *operands)
-    if last:
-        return out, None, None
     return out[0], out[1:4], out[4] if up_out else None
 
 
-def split_body(count, info, *refs):
-    hand_on(info, refs[:count], refs[count : count + 4], *refs[count + 4 :])
-
-
-def split(info, wholes):
-    return pl.pallas_call(
-        functools.partial(split_body, len(wholes)),
-        out_shape=[PART] * 4,
-        in_specs=[SM] + [ANY] * len(wholes),
-        out_specs=[ANY] * 4,
-        scratch_shapes=[
-            pltpu.VMEM((OWN, WIDTH), BF),
-            pltpu.SemaphoreType.DMA((1,)),
-            pltpu.SemaphoreType.DMA((4,)),
-        ],
-        compiler_params=pltpu.CompilerParams(vmem_limit_bytes=16 * MIB),
-        name="split",
-    )(info, *wholes)
-
-
-def collect_body(groups, info, *refs):
-    out, held, in_sem, out_sem = refs[-4:]
-    for at in range(groups):
+def pick_body(info, *refs):
+    wholes, out, held, in_sem, out_sem = refs[:BLOCKS], *refs[BLOCKS:]
+    for at in range(8):
 
         @pl.when(info[0] == at)
         def _():
-            copies = []
-            for k in range(4):
-                for high in range(2):
-                    slot, n = 4 * high + lax.rem(info[1] + 4 - k, 4), 2 * k + high
-                    copies.append(
-                        (
-                            pltpu.make_async_copy(refs[at * 8 + n], held.at[n], in_sem.at[n]),
-                            pltpu.make_async_copy(held.at[n], out.at[slot], out_sem.at[n]),
-                        )
-                    )
+            copies = [
+                (
+                    pltpu.make_async_copy(wholes[at + 8 * n], held.at[n], in_sem.at[n]),
+                    pltpu.make_async_copy(held.at[n], out.at[n], out_sem.at[n]),
+                )
+                for n in range(2)
+            ]
             for arrive, _ in copies:
                 arrive.start()
             for arrive, leave in copies:
@@ -413,21 +333,20 @@
                 leave.wait()
 
 
-def collect(info, received):
-    flat = [piece for group in received for piece in group]
+def pick(info, wholes):
     return pl.pallas_call(
-        functools.partial(collect_body, len(received)),
-        out_shape=jax.ShapeDtypeStruct((MICRO, PIECE, WIDTH), BF),
-        in_specs=[SM] + [ANY] * len(flat),
+        pick_body,
+        out_shape=jax.ShapeDtypeStruct((2, OWN, WIDTH), BF),
+        in_specs=[SM] + [ANY] * BLOCKS,
         out_specs=ANY,
         scratch_shapes=[
-            pltpu.VMEM((MICRO, PIECE, WIDTH), BF),
-            pltpu.SemaphoreType.DMA((8,)),
-            pltpu.SemaphoreType.DMA((8,)),
+            pltpu.VMEM((2, OWN, WIDTH), BF),
+            pltpu.SemaphoreType.DMA((2,)),
+            pltpu.SemaphoreType.DMA((2,)),
         ],
         compiler_params=pltpu.CompilerParams(vmem_limit_bytes=16 * MIB),
-        name="collect",
-    )(info, *flat)
+        name="pick",
+    )(info, *wholes)
 
 
 def sinusoid(steps, half_width):
@@ -445,18 +364,7 @@
     slot = 4 * (tile // 8) + (tile % 8) // 2
     active = (segment < 2).astype(jnp.int32)
 
-    def info_for(group):
-        pick, passed = jnp.full((), -1, jnp.int32), (tile % 8) // 2
-        for at, block in enumerate(group):
-            if block < BLOCKS - 1:
-                *columns, its_core = HELPERS[block]
-                for half, column in enumerate(columns):
-                    ours = segment == 2 * column + its_core
-                    pick = jnp.where(ours, at, pick)
-                    passed = jnp.where(ours, passed + 4 * half, passed)
-        return jnp.stack([quarter, slot, active, pick, passed]).astype(jnp.int32)
-
-    info = info_for(())
+    info = jnp.stack([quarter, slot, active]).astype(jnp.int32)
 
     served = lax.dynamic_index_in_dim(
         features, plan[jnp.minimum(segment, MICRO - 1)], 0, keepdims=False
@@ -465,7 +373,7 @@
     pieces = []
     for k in range(4):
         route = [
-            (j * TILES + 4 * q + (k + j) % 4, place(j, q)) for j in range(MICRO) for q in range(4)
+            (j * TILES + 4 * q + (k ^ j % 4), place(j, q)) for j in range(MICRO) for q in range(4)
         ]
         pieces.append(lax.ppermute(served, BOTH, route))
 
@@ -482,11 +390,13 @@
     full = jnp.concatenate(columns, axis=1)
     first_up = BLOCKS - DOWN
 
-    def fetch(pair, after):
-        own = full if max(pair) >= first_up else lead
-        if after is not None:
-            own, _ = lax.optimization_barrier((own, after))
-        return lax.ppermute(own, "segment", [(pair[0], 0), (pair[1], 1)])
+    lead, full = lax.optimization_barrier((lead, full))
+
+    def fetch(index, after):
+        own = full if max(PAIRS[index]) >= first_up else lead
+        own, _ = lax.optimization_barrier((own, after))
+        first, second = PAIRS[index]
+        return lax.ppermute(own, "segment", [(first, 0), (second, 1)])
 
     def exchange(near, cross, stats):
         other_tile = [(t, t ^ 1) for t in range(TILES)]
@@ -504,19 +414,6 @@
         route = [(place(j, q), helper(block, j, q)) for j in range(MICRO) for q in range(4)]
         return lax.ppermute(whole, BOTH, route)
 
-    def spread(group, outs):
-        got = []
-        for k in range(4):
-            for high in range(2):
-                route = [
-                    (helper(block, j, q), block * TILES + 4 * q + (k + j) % 4)
-                    for block in group
-                    for j in range(4 * high, 4 * high + 4)
-                    for q in range(4)
-                ]
-                got.append(lax.ppermute(outs[k], BOTH, route))
-        return got
-
     member_at = jnp.arange(CH) // GROUP
     member = (member_at[:, None] == member_at[None, :]).astype(BF)
     weights, cores, fetched = {}, {}, {}
@@ -529,8 +426,8 @@
     swap_cores(0, lead)
     *exchanged, source = first_call(info, pieces)
     for index in (1, 2):
-        fetched[index] = fetch(PAIRS[index], pieces[-1])
-    wholes, edges_of, passing, received = [], {}, [], []
+        fetched[index] = fetch(index, pieces[-1])
+    wholes, edges_of, passing = [], {}, []
     for block in range(BLOCKS):
         up_in, up_out = block >= first_up, first_up - 1 <= block < BLOCKS - 1
         near, cross, stats = exchanged
@@ -540,13 +437,9 @@
             source, near_in, cross_in, far, passing[block - 2] = lax.optimization_barrier(
                 (source, near_in, cross_in, far, passing[block - 2])
             )
-        if block in SPREAD_BY:
-            at = SPREAD_BY[block]
-            source, received[at] = lax.optimization_barrier((source, received[at]))
-        last = block == BLOCKS - 1
         whole, exchanged, summed = block_call(
             (cores[block], cores.get(block + 1, 0)),
-            info_for(GROUPS[-1]) if last else info,
+            info,
             source,
             (near_in, cross_in, stats, far),
             member,
@@ -554,29 +447,27 @@
             edges_of[BLOCKS - block] if up_in else None,
             wholes[BLOCKS - 2 - block] if up_out else None,
             weights[block + 1] if up_out else None,
-            [passing[b] for b in GROUPS[-1][:-1]] if last else [],
+            block == BLOCKS - 1,
         )
         wholes.append(whole)
         source = summed if up_out else whole
-        if not last:
-            passing.append(hand_over(block, whole))
-        if block in SPREAD_AFTER:
-            group = GROUPS[SPREAD_AFTER[block]]
-            outs = split(info_for(group), [passing[b] for b in group])
-            received.append(spread(group, outs))
+        passing.append(hand_over(block, whole))
         if block in SWAP_AFTER:
             index = SWAP_AFTER[block]
             own, _ = lax.optimization_barrier((fetched[index], whole))
             swap_cores(index, own)
         if block in FETCH_AFTER:
             index = FETCH_AFTER[block]
-            fetched[index] = fetch(PAIRS[index], whole)
-    received.append(spread(GROUPS[-1], whole))
-    group_of = jnp.zeros((), jnp.int32)
-    for at, group in enumerate(GROUPS):
-        for block in group:
-            group_of = jnp.where(segment == block, at, group_of)
-    out = collect(jnp.stack([group_of, tile % 4]).astype(jnp.int32), received)
+            fetched[index] = fetch(index, whole)
+    held = pick((segment % 8).astype(jnp.int32)[None], passing)
+    peers = [
+        [(s + 8 * far) * TILES + 4 * q + i for far in range(2) for i in range(4)]
+        for s in range(8)
+        for q in range(4)
+    ]
+    out = lax.all_to_all(
+        held.reshape(MICRO, PIECE, WIDTH), BOTH, 0, 0, axis_index_groups=peers, tiled=True
+    )
     out = out.reshape(1, MICRO, 3, CH, WIDTH)
     return out.transpose(0, 1, 2, 4, 3)
 

time: 826 us -> 1120 us (1.36)
  waiting for transfers between devices: 97.6 us -> 466 us
  starting transfers between devices: 557 us -> 459 us
  blocking collectives: 0 us -> 88.7 us
  local copies, waits for them, and re-layouts: 71.5 us -> 30.7 us
  Pallas kernels: 78 us -> 53.4 us
    ppermute x15 -> x16, waiting for transfers between devices: 0.04 us -> 413 us  [hand_over(): return lax.ppermute(whole, BOTH, route)]
    ppermute x39 -> x7, starting transfers between devices: 396 us -> 61 us  [fetch(): return lax.ppermute(own, 'segment', [(first, 0), (second, 1)])]
    ppermute x16, starting transfers between devices: 12.4 us -> 217 us  [exchange(): lax.ppermute(near, 'tile', other_tile)]
    all_to_all x0 -> x1, blocking collectives: none -> 88.7 us  [on_device(): lax.all_to_all(held.reshape(MICRO, PIECE, WIDTH), BOTH, 0, 0, axis_index_...]
    ppermute x39 -> x7, waiting for transfers between devices: 47.4 us -> 0.02 us  [fetch(): return lax.ppermute(own, 'segment', [(first, 0), (second, 1)])]
    unnamed x233 -> x60, local copies, waits for them, and re-layouts: 59.8 us -> 20.3 us
    ppermute x16, starting transfers between devices: 111 us -> 147 us  [exchange(): lax.ppermute(stats, BOTH, both)]
    pallas_call x16, Pallas kernels: 65.7 us -> 51 us  [block_call(): pl.pallas_call(functools.partial(block_body, *cores, up_in, up_out, last)...]
  transfers between devices with their start and end apart: 114 -> 83, of which waited for: 35 -> 30; matrix products, arithmetic and copies ran while one was open for 1% -> 0% of each run, Pallas kernels for 9% -> 5%
where the time goes in v4:
time: 1120 us; the launch traced here: 1100 us
  waiting for transfers between devices  466 us (42%)
  starting transfers between devices  459 us (41%)
  blocking collectives  88.7 us (8%)
  Pallas kernels  53.4 us (5%)
  local copies, waits for them, and re-layouts  30.7 us (3%)
    ppermute x16, waiting for transfers between devices, hand_over(): return lax.ppermute(whole, BOTH, route)  413 us
    ppermute x16, starting transfers between devices, exchange(): lax.ppermute(near, 'tile', other_tile)  217 us
    ppermute x16, starting transfers between devices, exchange(): lax.ppermute(stats, BOTH, both)  147 us
    all_to_all x1, blocking collectives, on_device(): lax.all_to_all(held.reshape(MICRO, PIECE, WIDTH), BOTH, 0, 0, axis_index_...  88.7 us
    ppermute x7, starting transfers between devices, fetch(): return lax.ppermute(own, 'segment', [(first, 0), (second, 1)])  61 us
    pallas_call x16, Pallas kernels, block_call(): pl.pallas_call(functools.partial(block_body, *cores, up_in, up_out, last)...  51 us
    ppermute x16, waiting for transfers between devices, exchange(): lax.ppermute(stats, BOTH, both)  32.5 us
  transfers between devices with their start and end apart: 83, of which 30 were waited for; matrix products, arithmetic and copies ran while one was open for 0% of the time, Pallas kernels for 5%

profile of v4, /device:TPU:59, one launch (start us, length us, event | category | flops | bytes accessed | tf_op | source)
XLA Modules:
  0.0 1104.7 jit_solution(7855657968986276170)
XLA Ops:
  5.8 3.8 concatenate.19.refs_6_
  9.7 4.5 concatenate.20
  33.7 3.2 collective-permute-done.8.refs_1_.refs_8_
  65.0 6.9 res_block.20
  73.4 136.8 %collective-permute-start.31 = (bf16[48,128]{1,0:T(8,128)(2,1)S(1)}, bf16[48,128]{1,0:T(8,128)(2,1)S(1)}, u32[]{:S(2)}, u32[]{:S(2)}) collective-permute-start(bf16[48,128]{1,0:T(8,128)(2,1)S(1)} %get-tuple-element.202.refs_3_), channel_id=1, source_target_pairs={{0,17},{1,16},{2,19},{3,18},{4,21},{5,20},{6,23},{7,22},{8,25},{9,... | collective-permute-start | bytes 36872 | tf_op jit(solution)/shard_map/ppermute | solution.py:410
  218.4 2.8 collective-permute-done.37.refs_4_
  221.2 7.2 res_block.22
  237.9 56.2 %collective-permute-start.61 = (bf16[320,3328]{1,0:T(8,128)(2,1)}, bf16[320,3328]{1,0:T(8,128)(2,1)S(1)}, u32[]{:S(2)}, u32[]{:S(2)}) collective-permute-start(bf16[320,3328]{1,0:T(8,128)(2,1)} %concatenate.20), channel_id=1, source_target_pairs={{176,0},{240,16},{177,1},{241,17},{178,2},{242,18},{179,3},{243,19... | collective-permute-start | bytes 6389768 | tf_op jit(solution)/shard_map/ppermute | solution.py:399
  294.3 7.5 res_block.24
  304.3 2.9 collective-permute-done.49.refs_4_
  307.2 204.5 %collective-permute-start.47 = (bf16[368,128]{1,0:T(8,128)(2,1)S(1)}, bf16[368,128]{1,0:T(8,128)(2,1)S(1)}, u32[]{:S(2)}, u32[]{:S(2)}) collective-permute-start(bf16[368,128]{1,0:T(8,128)(2,1)S(1)} %get-tuple-element.238), channel_id=1, source_target_pairs={{0,1},{1,0},{2,3},{3,2},{4,5},{5,4},{6,7},{7,6},{8,9},{9,8},{10,11... | collective-permute-start | bytes 282632 | tf_op jit(solution)/shard_map/ppermute | solution.py:408
  513.7 2.9 collective-permute-start.48
  518.3 18.8 %collective-permute-done.50.refs_7_ = bf16[3840,128]{1,0:T(8,128)(2,1)S(1)} collective-permute-done((bf16[3840,128]{1,0:T(8,128)(2,1)S(1)}, bf16[3840,128]{1,0:T(8,128)(2,1)S(1)}, u32[]{:S(2)}, u32[]{:S(2)}) %collective-permute-start.50) | collective-permute-done | bytes 983072 | tf_op jit(solution)/shard_map/ppermute | solution.py:415
  538.1 3.1 collective-permute-done.53.refs_4_
  541.6 3.0 collective-permute-done.51.refs_1_
  544.6 7.7 res_block.26
  555.5 3.2 collective-permute-done.59.refs_4_
  564.6 2.9 collective-permute-done.67.refs_4_
  567.4 7.6 res_block.28
  578.1 2.8 collective-permute-done.71.refs_4_
  585.2 3.0 collective-permute-done.75.refs_4_
  589.2 7.1 res_block.30
  604.2 394.3 %collective-permute-done.82.refs_15_ = bf16[3840,128]{1,0:T(8,128)(2,1)} collective-permute-done((bf16[3840,128]{1,0:T(8,128)(2,1)}, bf16[3840,128]{1,0:T(8,128)(2,1)}, u32[]{:S(2)}, u32[]{:S(2)}) %collective-permute-start.82) | collective-permute-done | bytes 983072 | tf_op jit(solution)/shard_map/ppermute | solution.py:415
  1013.5 88.7 %all_to_all.5 = bf16[8,960,128]{2,1,0:T(8,128)(2,1)S(1)} all-to-all(bf16[8,960,128]{2,1,0:T(8,128)(2,1)S(1)} %bitcast.24), channel_id=1, replica_groups={{0,1,2,3,128,129,130,131},{4,5,6,7,132,133,134,135},{8,9,10,11,136,137,..., dimensions={0} | all-to-all | bytes 3932160 | tf_op jit(solution)/shard_map/all_to_all | solution.py:468
  (242 shorter events, 120.2 us)
Async XLA Ops:
  24.9 18.8 %collective-permute-start.21 = (bf16[320,2944]{1,0:T(8,128)(2,1)}, bf16[320,2944]{1,0:T(8,128)(2,1)S(1)}, u32[]{:S(2)}, u32[]{:S(2)}) collective-permute-start(bf16[320,2944]{1,0:T(8,128)(2,1)} %concatenate.19.refs_6_), channel_id=1, source_target_pairs={{48,0},{112,16},{49,1},{113,17},{50,2},{114,18},{51,3},{115,19},{5... | collective-permute-start | bytes 5652488 | tf_op jit(solution)/shard_map/ppermute | solution.py:399
  26.8 20.9 %collective-permute-start.16 = (bf16[320,2944]{1,0:T(8,128)(2,1)S(1)}, bf16[320,2944]{1,0:T(8,128)(2,1)S(1)}, u32[]{:S(2)}, u32[]{:S(2)}) collective-permute-start(bf16[320,2944]{1,0:T(8,128)(2,1)S(1)} %collective-permute-done.15.refs_6_), channel_id=1, source_target_pairs={{0,16},{16,0},{32,48},{48,32},{64,80},{80,64},{96,112},{112,96},{1... | collective-permute-start | bytes 5652488 | tf_op jit(solution)/shard_map/ppermute | solution.py:422
  27.8 19.9 %collective-permute-start.14 = (bf16[3840,128]{1,0:T(8,128)(2,1)S(1)}, bf16[3840,128]{1,0:T(8,128)(2,1)S(1)}, u32[]{:S(2)}, u32[]{:S(2)}) collective-permute-start(bf16[3840,128]{1,0:T(8,128)(2,1)S(1)} %get-tuple-element.163.refs_0_.refs_10_), channel_id=1, source_target_pairs={{0,0},{1,4},{17,8},{16,12},{2,1},{3,5},{19,9},{18,13},{4,2},{5,6},... | collective-permute-start | bytes 2949128 | tf_op jit(solution)/shard_map/ppermute | solution.py:415
  28.5 21.3 %collective-permute-start.27 = (bf16[320,2944]{1,0:T(8,128)(2,1)}, bf16[320,2944]{1,0:T(8,128)(2,1)S(1)}, u32[]{:S(2)}, u32[]{:S(2)}) collective-permute-start(bf16[320,2944]{1,0:T(8,128)(2,1)} %concatenate.19.refs_6_), channel_id=1, source_target_pairs={{64,0},{128,16},{65,1},{129,17},{66,2},{130,18},{67,3},{131,19},{6... | collective-permute-start | bytes 5652488 | tf_op jit(solution)/shard_map/ppermute | solution.py:399
  57.4 156.9 %collective-permute-start.34 = (bf16[320,2944]{1,0:T(8,128)(2,1)S(1)}, bf16[320,2944]{1,0:T(8,128)(2,1)S(1)}, u32[]{:S(2)}, u32[]{:S(2)}) collective-permute-start(bf16[320,2944]{1,0:T(8,128)(2,1)S(1)} %collective-permute-done.33.refs_6_), channel_id=1, source_target_pairs={{0,16},{16,0},{32,48},{48,32},{64,80},{80,64},{96,112},{112,96},{1... | collective-permute-start | bytes 5652488 | tf_op jit(solution)/shard_map/ppermute | solution.py:422
  61.7 148.5 %collective-permute-start.32 = (bf16[3840,128]{1,0:T(8,128)(2,1)S(1)}, bf16[3840,128]{1,0:T(8,128)(2,1)S(1)}, u32[]{:S(2)}, u32[]{:S(2)}) collective-permute-start(bf16[3840,128]{1,0:T(8,128)(2,1)S(1)} %get-tuple-element.193.refs_0_.refs_8_), channel_id=1, source_target_pairs={{0,48},{1,52},{17,56},{16,60},{2,49},{3,53},{19,57},{18,61},{4,50}... | collective-permute-start | bytes 2949128 | tf_op jit(solution)/shard_map/ppermute | solution.py:415
  71.9 146.1 %collective-permute-start.38 = (bf16[3840,128]{1,0:T(8,128)(2,1)S(1)}, bf16[3840,128]{1,0:T(8,128)(2,1)S(1)}, u32[]{:S(2)}, u32[]{:S(2)}) collective-permute-start(bf16[3840,128]{1,0:T(8,128)(2,1)S(1)} %get-tuple-element.204.refs_0_), channel_id=1, source_target_pairs={{0,64},{1,68},{17,72},{16,76},{2,65},{3,69},{19,73},{18,77},{4,66}... | collective-permute-start | bytes 2949128 | tf_op jit(solution)/shard_map/ppermute | solution.py:415
  72.6 165.3 %collective-permute-start.55 = (bf16[320,3328]{1,0:T(8,128)(2,1)}, bf16[320,3328]{1,0:T(8,128)(2,1)S(1)}, u32[]{:S(2)}, u32[]{:S(2)}) collective-permute-start(bf16[320,3328]{1,0:T(8,128)(2,1)} %concatenate.20), channel_id=1, source_target_pairs={{160,0},{224,16},{161,1},{225,17},{162,2},{226,18},{163,3},{227,19... | collective-permute-start | bytes 6389768 | tf_op jit(solution)/shard_map/ppermute | solution.py:399
  73.4 138.5 %collective-permute-start.31 = (bf16[48,128]{1,0:T(8,128)(2,1)S(1)}, bf16[48,128]{1,0:T(8,128)(2,1)S(1)}, u32[]{:S(2)}, u32[]{:S(2)}) collective-permute-start(bf16[48,128]{1,0:T(8,128)(2,1)S(1)} %get-tuple-element.202.refs_3_), channel_id=1, source_target_pairs={{0,17},{1,16},{2,19},{3,18},{4,21},{5,20},{6,23},{7,22},{8,25},{9,... | collective-permute-start | bytes 36872 | tf_op jit(solution)/shard_map/ppermute | solution.py:410
  217.3 17.3 %collective-permute-start.42 = (bf16[3840,128]{1,0:T(8,128)(2,1)S(1)}, bf16[3840,128]{1,0:T(8,128)(2,1)S(1)}, u32[]{:S(2)}, u32[]{:S(2)}) collective-permute-start(bf16[3840,128]{1,0:T(8,128)(2,1)S(1)} %get-tuple-element.215.refs_0_), channel_id=1, source_target_pairs={{0,80},{1,84},{17,88},{16,92},{2,81},{3,85},{19,89},{18,93},{4,82}... | collective-permute-start | bytes 2949128 | tf_op jit(solution)/shard_map/ppermute | solution.py:415
  228.4 65.8 %collective-permute-start.46 = (bf16[3840,128]{1,0:T(8,128)(2,1)S(1)}, bf16[3840,128]{1,0:T(8,128)(2,1)S(1)}, u32[]{:S(2)}, u32[]{:S(2)}) collective-permute-start(bf16[3840,128]{1,0:T(8,128)(2,1)S(1)} %get-tuple-element.224.refs_0_), channel_id=1, source_target_pairs={{0,96},{1,100},{17,104},{16,108},{2,97},{3,101},{19,105},{18,109},... | collective-permute-start | bytes 2949128 | tf_op jit(solution)/shard_map/ppermute | solution.py:415
  235.5 58.8 %collective-permute-start.43 = (bf16[368,128]{1,0:T(8,128)(2,1)S(1)}, bf16[368,128]{1,0:T(8,128)(2,1)S(1)}, u32[]{:S(2)}, u32[]{:S(2)}) collective-permute-start(bf16[368,128]{1,0:T(8,128)(2,1)S(1)} %get-tuple-element.229), channel_id=1, source_target_pairs={{0,1},{1,0},{2,3},{3,2},{4,5},{5,4},{6,7},{7,6},{8,9},{9,8},{10,11... | collective-permute-start | bytes 282632 | tf_op jit(solution)/shard_map/ppermute | solution.py:408
  236.5 57.7 %collective-permute-start.44 = (bf16[368,128]{1,0:T(8,128)(2,1)S(1)}, bf16[368,128]{1,0:T(8,128)(2,1)S(1)}, u32[]{:S(2)}, u32[]{:S(2)}) collective-permute-start(bf16[368,128]{1,0:T(8,128)(2,1)S(1)} %get-tuple-element.230), channel_id=1, source_target_pairs={{0,16},{16,0},{32,48},{48,32},{64,80},{80,64},{96,112},{112,96},{1... | collective-permute-start | bytes 282632 | tf_op jit(solution)/shard_map/ppermute | solution.py:409
  237.5 56.6 %collective-permute-start.45 = (bf16[48,128]{1,0:T(8,128)(2,1)S(1)}, bf16[48,128]{1,0:T(8,128)(2,1)S(1)}, u32[]{:S(2)}, u32[]{:S(2)}) collective-permute-start(bf16[48,128]{1,0:T(8,128)(2,1)S(1)} %get-tuple-element.231.refs_3_), channel_id=1, source_target_pairs={{0,17},{1,16},{2,19},{3,18},{4,21},{5,20},{6,23},{7,22},{8,25},{9,... | collective-permute-start | bytes 36872 | tf_op jit(solution)/shard_map/ppermute | solution.py:410
  237.9 306.7 %collective-permute-start.61 = (bf16[320,3328]{1,0:T(8,128)(2,1)}, bf16[320,3328]{1,0:T(8,128)(2,1)S(1)}, u32[]{:S(2)}, u32[]{:S(2)}) collective-permute-start(bf16[320,3328]{1,0:T(8,128)(2,1)} %concatenate.20), channel_id=1, source_target_pairs={{176,0},{240,16},{177,1},{241,17},{178,2},{242,18},{179,3},{243,19... | collective-permute-start | bytes 6389768 | tf_op jit(solution)/shard_map/ppermute | solution.py:399
  294.2 250.5 %collective-permute-start.56 = (bf16[320,3328]{1,0:T(8,128)(2,1)S(1)}, bf16[320,3328]{1,0:T(8,128)(2,1)S(1)}, u32[]{:S(2)}, u32[]{:S(2)}) collective-permute-start(bf16[320,3328]{1,0:T(8,128)(2,1)S(1)} %collective-permute-done.55.refs_6_.refs_11_), channel_id=1, source_target_pairs={{0,16},{16,0},{32,48},{48,32},{64,80},{80,64},{96,112},{112,96},{1... | collective-permute-start | bytes 6389768 | tf_op jit(solution)/shard_map/ppermute | solution.py:422
  301.8 250.5 %collective-permute-start.63 = (bf16[320,3328]{1,0:T(8,128)(2,1)}, bf16[320,3328]{1,0:T(8,128)(2,1)S(1)}, u32[]{:S(2)}, u32[]{:S(2)}) collective-permute-start(bf16[320,3328]{1,0:T(8,128)(2,1)} %concatenate.20), channel_id=1, source_target_pairs={{192,0},{208,16},{193,1},{209,17},{194,2},{210,18},{195,3},{211,19... | collective-permute-start | bytes 6389768 | tf_op jit(solution)/shard_map/ppermute | solution.py:399
  302.6 234.5 %collective-permute-start.50 = (bf16[3840,128]{1,0:T(8,128)(2,1)S(1)}, bf16[3840,128]{1,0:T(8,128)(2,1)S(1)}, u32[]{:S(2)}, u32[]{:S(2)}) collective-permute-start(bf16[3840,128]{1,0:T(8,128)(2,1)S(1)} %get-tuple-element.233.refs_0_), channel_id=1, source_target_pairs={{0,112},{1,116},{17,120},{16,124},{2,113},{3,117},{19,121},{18,125... | collective-permute-start | bytes 2949128 | tf_op jit(solution)/shard_map/ppermute | solution.py:415
  307.2 206.5 %collective-permute-start.47 = (bf16[368,128]{1,0:T(8,128)(2,1)S(1)}, bf16[368,128]{1,0:T(8,128)(2,1)S(1)}, u32[]{:S(2)}, u32[]{:S(2)}) collective-permute-start(bf16[368,128]{1,0:T(8,128)(2,1)S(1)} %get-tuple-element.238), channel_id=1, source_target_pairs={{0,1},{1,0},{2,3},{3,2},{4,5},{5,4},{6,7},{7,6},{8,9},{9,8},{10,11... | collective-permute-start | bytes 282632 | tf_op jit(solution)/shard_map/ppermute | solution.py:408
  517.6 23.6 %collective-permute-start.54 = (bf16[3840,128]{1,0:T(8,128)(2,1)S(1)}, bf16[3840,128]{1,0:T(8,128)(2,1)S(1)}, u32[]{:S(2)}, u32[]{:S(2)}) collective-permute-start(bf16[3840,128]{1,0:T(8,128)(2,1)S(1)} %get-tuple-element.242.refs_0_), channel_id=1, source_target_pairs={{0,0},{1,4},{17,8},{16,12},{2,1},{3,5},{19,9},{18,13},{4,2},{5,6},... | collective-permute-start | bytes 2949128 | tf_op jit(solution)/shard_map/ppermute | solution.py:415
  544.6 16.2 %collective-permute-start.62 = (bf16[320,3328]{1,0:T(8,128)(2,1)S(1)}, bf16[320,3328]{1,0:T(8,128)(2,1)S(1)}, u32[]{:S(2)}, u32[]{:S(2)}) collective-permute-start(bf16[320,3328]{1,0:T(8,128)(2,1)S(1)} %collective-permute-done.61.refs_6_.refs_11_), channel_id=1, source_target_pairs={{0,16},{16,0},{32,48},{48,32},{64,80},{80,64},{96,112},{112,96},{1... | collective-permute-start | bytes 6389768 | tf_op jit(solution)/shard_map/ppermute | solution.py:422
  561.8 19.2 %collective-permute-start.72 = (bf16[3840,128]{1,0:T(8,128)(2,1)S(1)}, bf16[3840,128]{1,0:T(8,128)(2,1)S(1)}, u32[]{:S(2)}, u32[]{:S(2)}) collective-permute-start(bf16[3840,128]{1,0:T(8,128)(2,1)S(1)} %get-tuple-element.284), channel_id=1, source_target_pairs={{0,48},{1,52},{17,56},{16,60},{2,49},{3,53},{19,57},{18,61},{4,50}... | collective-permute-start | bytes 2949128 | tf_op jit(solution)/shard_map/ppermute | solution.py:415
  582.5 18.8 %collective-permute-start.80 = (bf16[3840,128]{1,0:T(8,128)(2,1)S(1)}, bf16[3840,128]{1,0:T(8,128)(2,1)S(1)}, u32[]{:S(2)}, u32[]{:S(2)}) collective-permute-start(bf16[3840,128]{1,0:T(8,128)(2,1)S(1)} %get-tuple-element.304), channel_id=1, source_target_pairs={{0,80},{1,84},{17,88},{16,92},{2,81},{3,85},{19,89},{18,93},{4,82}... | collective-permute-start | bytes 2949128 | tf_op jit(solution)/shard_map/ppermute | solution.py:415
  602.9 395.6 %collective-permute-start.82 = (bf16[3840,128]{1,0:T(8,128)(2,1)}, bf16[3840,128]{1,0:T(8,128)(2,1)}, u32[]{:S(2)}, u32[]{:S(2)}) collective-permute-start(bf16[3840,128]{1,0:T(8,128)(2,1)} %res_block.31), channel_id=1, source_target_pairs={{0,112},{1,116},{17,120},{16,124},{2,113},{3,117},{19,121},{18,125... | collective-permute-start | bytes 2949128 | tf_op jit(solution)/shard_map/ppermute | solution.py:415
  (88 other events, 636.2 us)

commit v5 on v4

--- a/solution.py
+++ b/solution.py
@@ -17,8 +17,6 @@
 OWN = ROWS * CH
 MEMBERS = float(48 * WIDTH * GROUP)
 MIB = 1024 * 1024
-LEAD = 2944
-FULL = LEAD + 384
 STATS = 48
 BF, F32 = jnp.bfloat16, jnp.float32
 ANY = pl.BlockSpec(memory_space=pl.ANY)
@@ -31,13 +29,17 @@
 SWAP_AFTER = {0: 1, 1: 2, 2: 3, 3: 4, 6: 5, 8: 6, 10: 7}
 
 
+MOVE_AFTER = {4: 0, 5: 1, 12: 8, 13: 9}
+
+
 def place(slot, quarter):
     tile = (slot // 4) * 8 + 2 * (slot % 4) + (quarter in (1, 2))
     return (quarter // 2) * TILES + tile
 
 
 def helper(block, slot, quarter):
-    return (block % 8 + slot // 4 * 8) * TILES + 4 * quarter + slot % 4
+    column = block % 8 if block % 8 > 1 else 6 + block % 8
+    return (column + slot // 4 * 8) * TILES + 4 * quarter + slot % 4
 
 
 def chunk_at(turn, k):
@@ -100,7 +102,7 @@
         final.wait()
 
 
-def block_body(at_core, next_core, up_in, up_out, last, info, *refs):
+def block_body(block, at_core, up_in, up_out, last, info, *refs):
     refs = list(refs)
 
     def take(n):
@@ -108,12 +110,14 @@
         del refs[:n]
         return got
 
-    source, near, cross, own_stats, far_stats, member = take(6)
+    source, near, cross, own_stats, far_stats, member, params_all = take(7)
     weights = take(2)
+    if up_in or up_out:
+        (skips,) = take(1)
     if up_in:
         lateral_edges = take(2)
     if up_out:
-        (lateral,), nexts = take(1), take(2)
+        (lateral,) = take(1)
     (result,) = take(1)
     if not last:
         near_out, cross_out, stats_out = take(3)
@@ -130,23 +134,20 @@
     @pl.when(info[2] == 1)
     def _():
         core = info[0] // 2
-        lead, tail = pl.ds(0, LEAD), pl.ds(LEAD, FULL - LEAD)
-        head = pl.ds(LEAD - WIDTH, WIDTH)
+        params_copy = pltpu.make_async_copy(params_all.at[block], ps, w_sem.at[2])
+        params_copy.start()
         for at in range(2):
 
             @pl.when((core == at_core) == (at == 0))
             def _():
-                pltpu.make_async_copy(weights[at].at[:, head], ps, w_sem.at[2]).start()
-                pltpu.make_async_copy(weights[at].at[:, lead], ws, w_sem.at[0]).start()
-                if up_in:
-                    pltpu.make_async_copy(weights[at].at[:, tail], sk_in, w_sem.at[1]).start()
-
+                pltpu.make_async_copy(weights[at], ws, w_sem.at[0]).start()
+
+        if up_in:
+            in_copy = pltpu.make_async_copy(skips.at[block], sk_in, w_sem.at[1])
+            in_copy.start()
         if up_out:
-            for at in range(2):
-
-                @pl.when((core == next_core) == (at == 0))
-                def _():
-                    pltpu.make_async_copy(nexts[at].at[:, tail], sk, l_sem.at[1]).start()
+            out_copy = pltpu.make_async_copy(skips.at[block + 1], sk, l_sem.at[0])
+            out_copy.start()
 
         coded = [jnp.concatenate([ref[a + 16 * i : a + 16 * i + 16, :] for i in range(3)], axis=1)
                  for ref, a in ((own_stats, 0), (far_stats, 0), (near, CH), (cross, CH))]
@@ -159,9 +160,8 @@
         mean = jnp.sum(jnp.where(even_kind, groups, 0.0), axis=1, keepdims=True) / MEMBERS
         mean_sq = jnp.sum(jnp.where(even_kind, 0.0, groups), axis=1, keepdims=True) / MEMBERS
         variance = jnp.maximum(mean_sq - mean * mean, 0.0)
-        pltpu.make_async_copy(weights[0].at[:, head], ps, w_sem.at[2]).wait()
-        tailing = ps[:, 64:128].astype(F32)
-        params = tailing[:, 0:16] + tailing[:, 16:32] + tailing[:, 32:48]
+        params_copy.wait()
+        params = jnp.transpose(ps[...])
         lane = lax.broadcasted_iota(jnp.int32, (CH, 16), 1)
         shift = jnp.sum(jnp.where(lane == info[1] + 8, params, 0.0), axis=1, keepdims=True)
         wide = (CH, WIDTH)
@@ -188,8 +188,8 @@
         even = lax.rem(info[0], 2) == 0
         near_rows, cross_rows = near[0:CH, :].astype(F32), cross[0:CH, :].astype(F32)
         if up_in:
-            pltpu.make_async_copy(weights[0].at[:, tail], sk_in, w_sem.at[1]).wait()
-            skip_in = sk_in[:, 0:CH]
+            in_copy.wait()
+            skip_in = sk_in[...]
             near_rows, cross_rows = (
                 rows + jnp.dot(skip_in, edge[0:CH, :], preferred_element_type=F32)
                 for rows, edge in zip((near_rows, cross_rows), lateral_edges)
@@ -198,8 +198,8 @@
             return slice(r * CH, (r + 1) * CH)
 
         if up_out:
-            pltpu.make_async_copy(nexts[0].at[:, tail], sk, l_sem.at[1]).wait()
-            skip = sk[:, 0:CH]
+            out_copy.wait()
+            skip = sk[...]
         totals[...] = jnp.zeros(wide, F32)
         squares[...] = jnp.zeros(wide, F32)
 
@@ -215,7 +215,7 @@
             lift_at(row)
         lift_at(2)
         lift_at(3)
-        pltpu.make_async_copy(weights[0].at[:, lead], ws, w_sem.at[0]).wait()
+        pltpu.make_async_copy(weights[0], ws, w_sem.at[0]).wait()
         for pair in range(ROWS // 2):
             if pair:
                 lift_at(2 * pair + 2)
@@ -268,36 +268,37 @@
     )(info, *pieces)
 
 
-def block_call(cores, info, source, exchanged, member, weights, lateral_edges, lateral, nexts, last):
+def block_call(block, at_core, info, source, exchanged, member, params, weights, skips, lateral_edges, lateral):
     up_in, up_out = lateral_edges is not None, lateral is not None
-    operands = [source, *exchanged, member, *weights]
-    specs = [VM] * 6 + [ANY] * 2
+    last = block == BLOCKS - 1
+    operands = [source, *exchanged, member, params, *weights]
+    specs = [VM] * 6 + [ANY] * 3
     shapes, out_specs = [WHOLE] + EXCHANGED, [VM] * 4
     if last:
         shapes, out_specs = shapes[:1], out_specs[:1]
     scratch = [
-        pltpu.VMEM((CH, LEAD), BF),
-        pltpu.VMEM((CH, WIDTH), BF),
+        pltpu.VMEM((CH, TAPS), BF),
+        pltpu.VMEM((16, CH), F32),
         pltpu.VMEM((CAT, (ROWS + 2) * WIDTH), BF),
         pltpu.VMEM((CH, WIDTH), F32),
         pltpu.VMEM((CH, WIDTH), F32),
         pltpu.SemaphoreType.DMA((3,)),
     ]
+    if up_in or up_out:
+        operands.append(skips)
+        specs.append(ANY)
     if up_in:
         operands += list(lateral_edges)
         specs += [VM] * 2
-        scratch.append(pltpu.VMEM((CH, FULL - LEAD), BF))
+        scratch.append(pltpu.VMEM((CH, CH), BF))
     if up_out:
-        operands += [lateral, *nexts]
-        specs += [VM] + [ANY] * 2
+        operands.append(lateral)
+        specs.append(VM)
         shapes = shapes + [jax.ShapeDtypeStruct((OWN, WIDTH), F32)]
         out_specs = out_specs + [VM]
-        scratch += [
-            pltpu.VMEM((CH, FULL - LEAD), BF),
-            pltpu.SemaphoreType.DMA((2,)),
-        ]
+        scratch += [pltpu.VMEM((CH, CH), BF), pltpu.SemaphoreType.DMA((1,))]
     out = pl.pallas_call(
-        functools.partial(block_body, *cores, up_in, up_out, last),
+        functools.partial(block_body, block, at_core, up_in, up_out, last),
         out_shape=shapes,
         in_specs=[SM] + specs,
         out_specs=out_specs,
@@ -380,21 +381,13 @@
     encoded = sinusoid(timesteps[plan], time_weight.shape[1] // 2)
     shifts = jnp.dot(encoded, time_weight[0], precision=lax.Precision.HIGHEST)
     params = jnp.concatenate([norm_gain, norm_bias, jnp.zeros((6, CH), F32), shifts], axis=0)
-    high = lax.reduce_precision(params, 8, 7)
-    left = params - high
-    middle = lax.reduce_precision(left, 8, 7)
-    coded = jnp.concatenate([high, middle, left - middle], axis=0).astype(BF)
-    columns = [conv_weight[0].T, coded.T, jnp.zeros((CH, LEAD - TAPS - STATS), BF)]
-    lead = jnp.concatenate(columns, axis=1)
-    columns += [skip_weight[0].T, jnp.zeros((CH, FULL - LEAD - CH), BF)]
-    full = jnp.concatenate(columns, axis=1)
+    params = lax.all_gather(params, "segment")
+    skips = lax.all_gather(skip_weight[0].T, "segment")
+    lead = conv_weight[0].T
     first_up = BLOCKS - DOWN
 
-    lead, full = lax.optimization_barrier((lead, full))
-
     def fetch(index, after):
-        own = full if max(PAIRS[index]) >= first_up else lead
-        own, _ = lax.optimization_barrier((own, after))
+        own, _ = lax.optimization_barrier((lead, after))
         first, second = PAIRS[index]
         return lax.ppermute(own, "segment", [(first, 0), (second, 1)])
 
@@ -425,33 +418,46 @@
 
     swap_cores(0, lead)
     *exchanged, source = first_call(info, pieces)
-    for index in (1, 2):
-        fetched[index] = fetch(index, pieces[-1])
+    fetched[1] = fetch(1, pieces)
+    fetched[2] = fetch(2, source)
     wholes, edges_of, passing = [], {}, []
     for block in range(BLOCKS):
         up_in, up_out = block >= first_up, first_up - 1 <= block < BLOCKS - 1
         near, cross, stats = exchanged
         near_in, cross_in, far = exchange(near, cross, stats)
         edges_of[block] = (near_in, cross_in)
-        if block >= 2:
-            source, near_in, cross_in, far, passing[block - 2] = lax.optimization_barrier(
-                (source, near_in, cross_in, far, passing[block - 2])
+        if block >= 1:
+            sent, _ = lax.optimization_barrier((wholes[-1], (near_in, cross_in, far)))
+            passing.append(hand_over(block - 1, sent))
+        if block >= 3:
+            source, near_in, cross_in, far, passing[block - 3] = lax.optimization_barrier(
+                (source, near_in, cross_in, far, passing[block - 3])
             )
+        for after, moving in MOVE_AFTER.items():
+            if block == after + 3:
+                source, passing[moving] = lax.optimization_barrier((source, passing[moving]))
         whole, exchanged, summed = block_call(
-            (cores[block], cores.get(block + 1, 0)),
+            block,
+            cores[block],
             info,
             source,
             (near_in, cross_in, stats, far),
             member,
+            params,
             weights[block],
+            skips,
             edges_of[BLOCKS - block] if up_in else None,
             wholes[BLOCKS - 2 - block] if up_out else None,
-            weights[block + 1] if up_out else None,
-            block == BLOCKS - 1,
         )
         wholes.append(whole)
         source = summed if up_out else whole
-        passing.append(hand_over(block, whole))
+        if block in MOVE_AFTER:
+            moving = MOVE_AFTER[block]
+            column = helper(moving, 0, 0) // TILES
+            moved, _ = lax.optimization_barrier((passing[moving], whole))
+            passing[moving] = lax.ppermute(
+                moved, "segment", [(column + far, moving % 8 + far) for far in (0, 8)]
+            )
         if block in SWAP_AFTER:
             index = SWAP_AFTER[block]
             own, _ = lax.optimization_barrier((fetched[index], whole))
@@ -459,6 +465,7 @@
         if block in FETCH_AFTER:
             index = FETCH_AFTER[block]
             fetched[index] = fetch(index, whole)
+    passing.append(hand_over(BLOCKS - 1, wholes[-1]))
     held = pick((segment % 8).astype(jnp.int32)[None], passing)
     peers = [
         [(s + 8 * far) * TILES + 4 * q + i for far in range(2) for i in range(4)]

time: 1120 us -> 1110 us (level)
  the two profiles are of different devices: /device:TPU:59 before, /device:TPU:29 now
where the time goes in v5:
time: 1110 us; the launch traced here: 1100 us
  starting transfers between devices  498 us (45%)
  blocking collectives  362 us (33%)
  waiting for transfers between devices  139 us (13%)
  Pallas kernels  48.3 us (4%)
  local copies, waits for them, and re-layouts  29.2 us (3%)
  between operations  16.7 us (2%)
    all_to_all x1, blocking collectives, on_device(): lax.all_to_all(held.reshape(MICRO, PIECE, WIDTH), BOTH, 0, 0, axis_index_...  336 us
    ppermute x16, starting transfers between devices, exchange(): lax.ppermute(cross, 'segment', other_core)  298 us
    ppermute x16, starting transfers between devices, exchange(): lax.ppermute(stats, BOTH, both)  100 us
    pallas_call x16, Pallas kernels, block_call(): pl.pallas_call(functools.partial(block_body, block, at_core, up_in, up_ou...  45.9 us
    ppermute x16, starting transfers between devices, exchange(): lax.ppermute(near, 'tile', other_tile)  40.1 us
    ppermute x16, waiting for transfers between devices, exchange(): lax.ppermute(stats, BOTH, both)  34.5 us
    ppermute x16, waiting for transfers between devices, hand_over(): return lax.ppermute(whole, BOTH, route)  33.5 us
    unnamed x134, local copies, waits for them, and re-layouts  26.5 us
  transfers between devices with their start and end apart: 88, of which 37 were waited for; matrix products, arithmetic and copies ran while one was open for 0% of the time, Pallas kernels for 4%

profile of v5, /device:TPU:29, one launch (start us, length us, event | category | flops | bytes accessed | tf_op | source)
XLA Modules:
  0.0 1096.0 jit_solution(15685510305839984512)
XLA Ops:
  9.9 7.2 collective-permute-start.3
  21.1 13.1 %collective-permute-done.3.refs_3_ = bf16[960,128]{1,0:T(8,128)(2,1)S(1)} collective-permute-done((bf16[960,128]{1,0:T(8,128)(2,1)S(1)}, bf16[960,128]{1,0:T(8,128)(2,1)S(1)}, u32[]{:S(2)}, u32[]{:S(2)}) %collective-permute-start.3) | collective-permute-done | bytes 245792 | tf_op jit(solution)/shard_map/ppermute | solution.py:379
  41.4 7.2 collective-permute-start.6
  48.6 3.9 collective-permute-start.4
  52.5 25.5 %all-gather = f32[256,320]{1,0:T(8,128)S(1)} all-gather(f32[16,320]{1,0:T(8,128)S(1)} %pad_maximum_fusion), channel_id=2, replica_groups=mesh['segment'=16,'tile'=16] {'segment'}, dimensions={0}, use_global_device_ids=true | all-gather | bytes 348160 | tf_op jit(solution)/shard_map/all_gather | solution.py:384
  78.0 3.5 collective-permute-start.20
  92.0 8.3 res_block.17
  102.6 20.0 %collective-permute-done.20.refs_7_ = bf16[320,2880]{1,0:T(8,128)(2,1)S(1)} collective-permute-done((bf16[320,2880]{1,0:T(8,128)(2,1)}, bf16[320,2880]{1,0:T(8,128)(2,1)S(1)}, u32[]{:S(2)}, u32[]{:S(2)}) %collective-permute-start.20) | collective-permute-done | bytes 1843232 | tf_op jit(solution)/shard_map/ppermute | solution.py:392
  134.8 18.6 %collective-permute-start.17 = (bf16[368,128]{1,0:T(8,128)(2,1)S(1)}, bf16[368,128]{1,0:T(8,128)(2,1)S(1)}, u32[]{:S(2)}, u32[]{:S(2)}) collective-permute-start(bf16[368,128]{1,0:T(8,128)(2,1)S(1)} %get-tuple-element.193), channel_id=1, source_target_pairs={{0,16},{16,0},{32,48},{48,32},{64,80},{80,64},{96,112},{112,96},{1... | collective-permute-start | bytes 282632 | tf_op jit(solution)/shard_map/ppermute | solution.py:402
  154.4 7.7 res_block.19
  177.2 9.3 collective-permute-done.25
  193.0 22.7 %collective-permute-start.28 = (bf16[368,128]{1,0:T(8,128)(2,1)S(1)}, bf16[368,128]{1,0:T(8,128)(2,1)S(1)}, u32[]{:S(2)}, u32[]{:S(2)}) collective-permute-start(bf16[368,128]{1,0:T(8,128)(2,1)S(1)} %get-tuple-element.214), channel_id=1, source_target_pairs={{0,1},{1,0},{2,3},{3,2},{4,5},{5,4},{6,7},{7,6},{8,9},{9,8},{10,11... | collective-permute-start | bytes 282632 | tf_op jit(solution)/shard_map/ppermute | solution.py:401
  222.6 37.9 %collective-permute-start.36 = (bf16[48,128]{1,0:T(8,128)(2,1)S(1)}, bf16[48,128]{1,0:T(8,128)(2,1)S(1)}, u32[]{:S(2)}, u32[]{:S(2)}) collective-permute-start(bf16[48,128]{1,0:T(8,128)(2,1)S(1)} %get-tuple-element.227.refs_3_), channel_id=1, source_target_pairs={{0,17},{1,16},{2,19},{3,18},{4,21},{5,20},{6,23},{7,22},{8,25},{9,... | collective-permute-start | bytes 36872 | tf_op jit(solution)/shard_map/ppermute | solution.py:403
  269.3 9.2 collective-permute-start.47
  283.0 3.6 collective-permute-done.38.refs_1_
  309.0 268.8 %collective-permute-start.49 = (bf16[368,128]{1,0:T(8,128)(2,1)S(1)}, bf16[368,128]{1,0:T(8,128)(2,1)S(1)}, u32[]{:S(2)}, u32[]{:S(2)}) collective-permute-start(bf16[368,128]{1,0:T(8,128)(2,1)S(1)} %get-tuple-element.265), channel_id=1, source_target_pairs={{0,16},{16,0},{32,48},{48,32},{64,80},{80,64},{96,112},{112,96},{1... | collective-permute-start | bytes 282632 | tf_op jit(solution)/shard_map/ppermute | solution.py:402
  582.5 3.2 collective-permute-done.54.refs_4_
  586.2 3.5 collective-permute-done.53.refs_2_
  614.7 48.0 %collective-permute-start.66 = (bf16[48,128]{1,0:T(8,128)(2,1)S(1)}, bf16[48,128]{1,0:T(8,128)(2,1)S(1)}, u32[]{:S(2)}, u32[]{:S(2)}) collective-permute-start(bf16[48,128]{1,0:T(8,128)(2,1)S(1)} %get-tuple-element.299.refs_3_), channel_id=1, source_target_pairs={{0,17},{1,16},{2,19},{3,18},{4,21},{5,20},{6,23},{7,22},{8,25},{9,... | collective-permute-start | bytes 36872 | tf_op jit(solution)/shard_map/ppermute | solution.py:403
  667.0 7.3 res_block.28
  688.9 7.1 res_block.30
  709.7 4.0 collective-permute-done.83.refs_9_
  713.7 24.2 %collective-permute-done.86.refs_15_ = bf16[3840,128]{1,0:T(8,128)(2,1)} collective-permute-done((bf16[3840,128]{1,0:T(8,128)(2,1)}, bf16[3840,128]{1,0:T(8,128)(2,1)}, u32[]{:S(2)}, u32[]{:S(2)}) %collective-permute-start.86) | collective-permute-done | bytes 983072 | tf_op jit(solution)/shard_map/ppermute | solution.py:408
  750.6 336.0 %all_to_all.5 = bf16[8,960,128]{2,1,0:T(8,128)(2,1)S(1)} all-to-all(bf16[8,960,128]{2,1,0:T(8,128)(2,1)S(1)} %bitcast.46), channel_id=1, replica_groups={{0,1,2,3,128,129,130,131},{4,5,6,7,132,133,134,135},{8,9,10,11,136,137,..., dimensions={0} | all-to-all | bytes 3932160 | tf_op jit(solution)/shard_map/all_to_all | solution.py:475
  (322 shorter events, 179.3 us)
Async XLA Ops:
  6.5 601.6 %all-gather.4.cloned.1.call-start = ((), (), s32[]{:S(2)}) async-start(), calls=%async_computation.1 | async-start | bytes 4177920 | tf_op jit(solution)/shard_map/all_gather | solution.py:385
  19.1 62.5 %collective-permute-start.7 = (bf16[320,2880]{1,0:T(8,128)(2,1)}, bf16[320,2880]{1,0:T(8,128)(2,1)S(1)}, u32[]{:S(2)}, u32[]{:S(2)}) collective-permute-start(bf16[320,2880]{1,0:T(8,128)(2,1)} %bitcast.13.refs_7_), channel_id=1, source_target_pairs={{0,16},{16,0},{32,48},{48,32},{64,80},{80,64},{96,112},{112,96},{1... | collective-permute-start | bytes 5529608 | tf_op jit(solution)/shard_map/ppermute | solution.py:415
  34.2 50.7 %collective-permute-start.14 = (bf16[320,2880]{1,0:T(8,128)(2,1)}, bf16[320,2880]{1,0:T(8,128)(2,1)}, u32[]{:S(2)}, u32[]{:S(2)}) collective-permute-start(bf16[320,2880]{1,0:T(8,128)(2,1)} %bitcast.13.refs_7_), channel_id=1, source_target_pairs={{32,0},{96,16},{33,1},{97,17},{34,2},{98,18},{35,3},{99,19},{36,4}... | collective-permute-start | bytes 5529608 | tf_op jit(solution)/shard_map/ppermute | solution.py:392
  41.4 36.6 %collective-permute-start.6 = (bf16[48,128]{1,0:T(8,128)(2,1)S(1)}, bf16[48,128]{1,0:T(8,128)(2,1)S(1)}, u32[]{:S(2)}, u32[]{:S(2)}) collective-permute-start(bf16[48,128]{1,0:T(8,128)(2,1)S(1)} %get-tuple-element.180.refs_3_), channel_id=1, source_target_pairs={{0,17},{1,16},{2,19},{3,18},{4,21},{5,20},{6,23},{7,22},{8,25},{9,... | collective-permute-start | bytes 36872 | tf_op jit(solution)/shard_map/ppermute | solution.py:403
  78.0 44.6 %collective-permute-start.20 = (bf16[320,2880]{1,0:T(8,128)(2,1)}, bf16[320,2880]{1,0:T(8,128)(2,1)S(1)}, u32[]{:S(2)}, u32[]{:S(2)}) collective-permute-start(bf16[320,2880]{1,0:T(8,128)(2,1)} %bitcast.13.refs_7_), channel_id=1, source_target_pairs={{48,0},{112,16},{49,1},{113,17},{50,2},{114,18},{51,3},{115,19},{5... | collective-permute-start | bytes 5529608 | tf_op jit(solution)/shard_map/ppermute | solution.py:392
  84.9 40.8 %collective-permute-start.15 = (bf16[320,2880]{1,0:T(8,128)(2,1)}, bf16[320,2880]{1,0:T(8,128)(2,1)S(1)}, u32[]{:S(2)}, u32[]{:S(2)}) collective-permute-start(bf16[320,2880]{1,0:T(8,128)(2,1)} %collective-permute-done.14.refs_7_), channel_id=1, source_target_pairs={{0,16},{16,0},{32,48},{48,32},{64,80},{80,64},{96,112},{112,96},{1... | collective-permute-start | bytes 5529608 | tf_op jit(solution)/shard_map/ppermute | solution.py:415
  85.0 45.4 %collective-permute-start.26 = (bf16[320,2880]{1,0:T(8,128)(2,1)}, bf16[320,2880]{1,0:T(8,128)(2,1)}, u32[]{:S(2)}, u32[]{:S(2)}) collective-permute-start(bf16[320,2880]{1,0:T(8,128)(2,1)} %bitcast.13.refs_7_), channel_id=1, source_target_pairs={{64,0},{128,16},{65,1},{129,17},{66,2},{130,18},{67,3},{131,19},{6... | collective-permute-start | bytes 5529608 | tf_op jit(solution)/shard_map/ppermute | solution.py:392
  130.4 56.7 %collective-permute-start.27 = (bf16[320,2880]{1,0:T(8,128)(2,1)}, bf16[320,2880]{1,0:T(8,128)(2,1)}, u32[]{:S(2)}, u32[]{:S(2)}) collective-permute-start(bf16[320,2880]{1,0:T(8,128)(2,1)} %collective-permute-done.26.refs_7_), channel_id=1, source_target_pairs={{0,16},{16,0},{32,48},{48,32},{64,80},{80,64},{96,112},{112,96},{1... | collective-permute-start | bytes 5529608 | tf_op jit(solution)/shard_map/ppermute | solution.py:415
  163.1 58.7 %collective-permute-start.33 = (bf16[320,2880]{1,0:T(8,128)(2,1)}, bf16[320,2880]{1,0:T(8,128)(2,1)}, u32[]{:S(2)}, u32[]{:S(2)}) collective-permute-start(bf16[320,2880]{1,0:T(8,128)(2,1)} %collective-permute-done.32.refs_7_), channel_id=1, source_target_pairs={{0,16},{16,0},{32,48},{48,32},{64,80},{80,64},{96,112},{112,96},{1... | collective-permute-start | bytes 5529608 | tf_op jit(solution)/shard_map/ppermute | solution.py:415
  166.9 54.1 %collective-permute-start.31 = (bf16[3840,128]{1,0:T(8,128)(2,1)}, bf16[3840,128]{1,0:T(8,128)(2,1)S(1)}, u32[]{:S(2)}, u32[]{:S(2)}) collective-permute-start(bf16[3840,128]{1,0:T(8,128)(2,1)} %copy-done.20), channel_id=1, source_target_pairs={{0,32},{1,36},{17,40},{16,44},{2,33},{3,37},{19,41},{18,45},{4,34}... | collective-permute-start | bytes 2949128 | tf_op jit(solution)/shard_map/ppermute | solution.py:408
  186.5 82.8 %collective-permute-start.37 = (bf16[3840,128]{1,0:T(8,128)(2,1)}, bf16[3840,128]{1,0:T(8,128)(2,1)S(1)}, u32[]{:S(2)}, u32[]{:S(2)}) collective-permute-start(bf16[3840,128]{1,0:T(8,128)(2,1)} %copy-done.32), channel_id=1, source_target_pairs={{0,48},{1,52},{17,56},{16,60},{2,49},{3,53},{19,57},{18,61},{4,50}... | collective-permute-start | bytes 2949128 | tf_op jit(solution)/shard_map/ppermute | solution.py:408
  189.0 103.7 %collective-permute-start.56 = (bf16[320,2880]{1,0:T(8,128)(2,1)}, bf16[320,2880]{1,0:T(8,128)(2,1)S(1)}, u32[]{:S(2)}, u32[]{:S(2)}) collective-permute-start(bf16[320,2880]{1,0:T(8,128)(2,1)} %bitcast.13.refs_7_), channel_id=1, source_target_pairs={{160,0},{224,16},{161,1},{225,17},{162,2},{226,18},{163,3},{227,19... | collective-permute-start | bytes 5529608 | tf_op jit(solution)/shard_map/ppermute | solution.py:392
  220.3 58.8 %collective-permute-start.41 = (bf16[3840,128]{1,0:T(8,128)(2,1)S(1)}, bf16[3840,128]{1,0:T(8,128)(2,1)S(1)}, u32[]{:S(2)}, u32[]{:S(2)}) collective-permute-start(bf16[3840,128]{1,0:T(8,128)(2,1)S(1)} %get-tuple-element.237.refs_0_), channel_id=1, source_target_pairs={{0,64},{1,68},{17,72},{16,76},{2,65},{3,69},{19,73},{18,77},{4,66}... | collective-permute-start | bytes 2949128 | tf_op jit(solution)/shard_map/ppermute | solution.py:408
  221.1 69.3 %collective-permute-start.42 = (bf16[3840,128]{1,0:T(8,128)(2,1)S(1)}, bf16[3840,128]{1,0:T(8,128)(2,1)S(1)}, u32[]{:S(2)}, u32[]{:S(2)}) collective-permute-start(bf16[3840,128]{1,0:T(8,128)(2,1)S(1)} %copy-done.65), channel_id=1, source_target_pairs={{96,0},{224,128},{97,1},{225,129},{98,2},{226,130},{99,3},{227,131... | collective-permute-start | bytes 2949128 | tf_op jit(solution)/shard_map/ppermute | solution.py:458
  222.6 39.3 %collective-permute-start.36 = (bf16[48,128]{1,0:T(8,128)(2,1)S(1)}, bf16[48,128]{1,0:T(8,128)(2,1)S(1)}, u32[]{:S(2)}, u32[]{:S(2)}) collective-permute-start(bf16[48,128]{1,0:T(8,128)(2,1)S(1)} %get-tuple-element.227.refs_3_), channel_id=1, source_target_pairs={{0,17},{1,16},{2,19},{3,18},{4,21},{5,20},{6,23},{7,22},{8,25},{9,... | collective-permute-start | bytes 36872 | tf_op jit(solution)/shard_map/ppermute | solution.py:403
  288.3 293.8 %collective-permute-start.62 = (bf16[320,2880]{1,0:T(8,128)(2,1)}, bf16[320,2880]{1,0:T(8,128)(2,1)}, u32[]{:S(2)}, u32[]{:S(2)}) collective-permute-start(bf16[320,2880]{1,0:T(8,128)(2,1)} %bitcast.13.refs_7_), channel_id=1, source_target_pairs={{176,0},{240,16},{177,1},{241,17},{178,2},{242,18},{179,3},{243,19... | collective-permute-start | bytes 5529608 | tf_op jit(solution)/shard_map/ppermute | solution.py:392
  296.8 292.8 %collective-permute-start.57 = (bf16[320,2880]{1,0:T(8,128)(2,1)S(1)}, bf16[320,2880]{1,0:T(8,128)(2,1)S(1)}, u32[]{:S(2)}, u32[]{:S(2)}) collective-permute-start(bf16[320,2880]{1,0:T(8,128)(2,1)S(1)} %collective-permute-done.56.refs_7_), channel_id=1, source_target_pairs={{0,16},{16,0},{32,48},{48,32},{64,80},{80,64},{96,112},{112,96},{1... | collective-permute-start | bytes 5529608 | tf_op jit(solution)/shard_map/ppermute | solution.py:415
  299.9 292.8 %collective-permute-start.68 = (bf16[320,2880]{1,0:T(8,128)(2,1)}, bf16[320,2880]{1,0:T(8,128)(2,1)S(1)}, u32[]{:S(2)}, u32[]{:S(2)}) collective-permute-start(bf16[320,2880]{1,0:T(8,128)(2,1)} %bitcast.13.refs_7_), channel_id=1, source_target_pairs={{192,0},{208,16},{193,1},{209,17},{194,2},{210,18},{195,3},{211,19... | collective-permute-start | bytes 5529608 | tf_op jit(solution)/shard_map/ppermute | solution.py:392
  304.0 285.6 %collective-permute-start.55 = (bf16[3840,128]{1,0:T(8,128)(2,1)S(1)}, bf16[3840,128]{1,0:T(8,128)(2,1)S(1)}, u32[]{:S(2)}, u32[]{:S(2)}) collective-permute-start(bf16[3840,128]{1,0:T(8,128)(2,1)S(1)} %get-tuple-element.277.refs_0_), channel_id=1, source_target_pairs={{0,112},{1,116},{17,120},{16,124},{2,113},{3,117},{19,121},{18,125... | collective-permute-start | bytes 2949128 | tf_op jit(solution)/shard_map/ppermute | solution.py:408
  309.0 269.7 %collective-permute-start.49 = (bf16[368,128]{1,0:T(8,128)(2,1)S(1)}, bf16[368,128]{1,0:T(8,128)(2,1)S(1)}, u32[]{:S(2)}, u32[]{:S(2)}) collective-permute-start(bf16[368,128]{1,0:T(8,128)(2,1)S(1)} %get-tuple-element.265), channel_id=1, source_target_pairs={{0,16},{16,0},{32,48},{48,32},{64,80},{80,64},{96,112},{112,96},{1... | collective-permute-start | bytes 282632 | tf_op jit(solution)/shard_map/ppermute | solution.py:402
  592.6 74.3 %collective-permute-start.69 = (bf16[320,2880]{1,0:T(8,128)(2,1)S(1)}, bf16[320,2880]{1,0:T(8,128)(2,1)}, u32[]{:S(2)}, u32[]{:S(2)}) collective-permute-start(bf16[320,2880]{1,0:T(8,128)(2,1)S(1)} %collective-permute-done.68.refs_7_), channel_id=1, source_target_pairs={{0,16},{16,0},{32,48},{48,32},{64,80},{80,64},{96,112},{112,96},{1... | collective-permute-start | bytes 5529608 | tf_op jit(solution)/shard_map/ppermute | solution.py:415
  594.7 72.2 %collective-permute-start.67 = (bf16[3840,128]{1,0:T(8,128)(2,1)}, bf16[3840,128]{1,0:T(8,128)(2,1)}, u32[]{:S(2)}, u32[]{:S(2)}) collective-permute-start(bf16[3840,128]{1,0:T(8,128)(2,1)} %get-tuple-element.300.refs_0_), channel_id=1, source_target_pairs={{0,112},{1,116},{17,120},{16,124},{2,113},{3,117},{19,121},{18,125... | collective-permute-start | bytes 2949128 | tf_op jit(solution)/shard_map/ppermute | solution.py:408
  606.5 74.6 %collective-permute-start.73 = (bf16[3840,128]{1,0:T(8,128)(2,1)}, bf16[3840,128]{1,0:T(8,128)(2,1)}, u32[]{:S(2)}, u32[]{:S(2)}) collective-permute-start(bf16[3840,128]{1,0:T(8,128)(2,1)} %get-tuple-element.311.refs_0_), channel_id=1, source_target_pairs={{0,32},{1,36},{17,40},{16,44},{2,33},{3,37},{19,41},{18,45},{4,34}... | collective-permute-start | bytes 2949128 | tf_op jit(solution)/shard_map/ppermute | solution.py:408
  614.7 49.4 %collective-permute-start.66 = (bf16[48,128]{1,0:T(8,128)(2,1)S(1)}, bf16[48,128]{1,0:T(8,128)(2,1)S(1)}, u32[]{:S(2)}, u32[]{:S(2)}) collective-permute-start(bf16[48,128]{1,0:T(8,128)(2,1)S(1)} %get-tuple-element.299.refs_3_), channel_id=1, source_target_pairs={{0,17},{1,16},{2,19},{3,18},{4,21},{5,20},{6,23},{7,22},{8,25},{9,... | collective-permute-start | bytes 36872 | tf_op jit(solution)/shard_map/ppermute | solution.py:403
  (130 other events, 2074.6 us)
Sparse Core Ops, SparseCore 0:
  167.0 84.9 all-gather.3

commit v6 on v5

--- a/solution.py
+++ b/solution.py
@@ -29,17 +29,14 @@
 SWAP_AFTER = {0: 1, 1: 2, 2: 3, 3: 4, 6: 5, 8: 6, 10: 7}
 
 
-MOVE_AFTER = {4: 0, 5: 1, 12: 8, 13: 9}
-
-
 def place(slot, quarter):
     tile = (slot // 4) * 8 + 2 * (slot % 4) + (quarter in (1, 2))
     return (quarter // 2) * TILES + tile
 
 
 def helper(block, slot, quarter):
-    column = block % 8 if block % 8 > 1 else 6 + block % 8
-    return (column + slot // 4 * 8) * TILES + 4 * quarter + slot % 4
+    segment = block % 8 + slot // 4 * 8
+    return segment * TILES + quarter // 2 * 8 + place(slot, quarter) % 8
 
 
 def chunk_at(turn, k):
@@ -318,32 +315,33 @@
 
         @pl.when(info[0] == at)
         def _():
-            copies = [
-                (
-                    pltpu.make_async_copy(wholes[at + 8 * n], held.at[n], in_sem.at[n]),
-                    pltpu.make_async_copy(held.at[n], out.at[n], out_sem.at[n]),
-                )
+            arrivals = [
+                pltpu.make_async_copy(wholes[at + 8 * n], held.at[n], in_sem.at[n])
                 for n in range(2)
             ]
-            for arrive, _ in copies:
+            leaves = [
+                pltpu.make_async_copy(held.at[n // 2], out.at[n], out_sem.at[n]) for n in range(4)
+            ]
+            for arrive in arrivals:
                 arrive.start()
-            for arrive, leave in copies:
-                arrive.wait()
+            for n, leave in enumerate(leaves):
+                if n % 2 == 0:
+                    arrivals[n // 2].wait()
                 leave.start()
-            for _, leave in copies:
+            for leave in leaves:
                 leave.wait()
 
 
 def pick(info, wholes):
     return pl.pallas_call(
         pick_body,
-        out_shape=jax.ShapeDtypeStruct((2, OWN, WIDTH), BF),
+        out_shape=jax.ShapeDtypeStruct((4, OWN, WIDTH), BF),
         in_specs=[SM] + [ANY] * BLOCKS,
         out_specs=ANY,
         scratch_shapes=[
             pltpu.VMEM((2, OWN, WIDTH), BF),
             pltpu.SemaphoreType.DMA((2,)),
-            pltpu.SemaphoreType.DMA((2,)),
+            pltpu.SemaphoreType.DMA((4,)),
         ],
         compiler_params=pltpu.CompilerParams(vmem_limit_bytes=16 * MIB),
         name="pick",
@@ -417,6 +415,7 @@
             weights[block], cores[block] = both, at
 
     swap_cores(0, lead)
+    pieces, params = lax.optimization_barrier((pieces, params))
     *exchanged, source = first_call(info, pieces)
     fetched[1] = fetch(1, pieces)
     fetched[2] = fetch(2, source)
@@ -433,9 +432,6 @@
             source, near_in, cross_in, far, passing[block - 3] = lax.optimization_barrier(
                 (source, near_in, cross_in, far, passing[block - 3])
             )
-        for after, moving in MOVE_AFTER.items():
-            if block == after + 3:
-                source, passing[moving] = lax.optimization_barrier((source, passing[moving]))
         whole, exchanged, summed = block_call(
             block,
             cores[block],
@@ -451,13 +447,6 @@
         )
         wholes.append(whole)
         source = summed if up_out else whole
-        if block in MOVE_AFTER:
-            moving = MOVE_AFTER[block]
-            column = helper(moving, 0, 0) // TILES
-            moved, _ = lax.optimization_barrier((passing[moving], whole))
-            passing[moving] = lax.ppermute(
-                moved, "segment", [(column + far, moving % 8 + far) for far in (0, 8)]
-            )
         if block in SWAP_AFTER:
             index = SWAP_AFTER[block]
             own, _ = lax.optimization_barrier((fetched[index], whole))
@@ -468,12 +457,16 @@
     passing.append(hand_over(BLOCKS - 1, wholes[-1]))
     held = pick((segment % 8).astype(jnp.int32)[None], passing)
     peers = [
-        [(s + 8 * far) * TILES + 4 * q + i for far in range(2) for i in range(4)]
+        [(s + 8 * far) * TILES + 8 * side + z for far in range(2) for z in range(8)]
         for s in range(8)
-        for q in range(4)
+        for side in range(2)
     ]
-    out = lax.all_to_all(
-        held.reshape(MICRO, PIECE, WIDTH), BOTH, 0, 0, axis_index_groups=peers, tiled=True
+    got = lax.all_to_all(
+        held.reshape(2 * MICRO, PIECE, WIDTH), BOTH, 0, 0, axis_index_groups=peers, tiled=True
+    )
+    parity = (tile % 8) // 4 ^ tile // 8
+    out = lax.dynamic_index_in_dim(
+        got.reshape(MICRO, 2, PIECE, WIDTH), parity, 1, keepdims=False
     )
     out = out.reshape(1, MICRO, 3, CH, WIDTH)
     return out.transpose(0, 1, 2, 4, 3)

time: 1110 us -> 518 us (0.47)
  the two profiles are of different devices: /device:TPU:29 before, /device:TPU:38 now
where the time goes in v6:
time: 518 us; the launch traced here: 509 us
  waiting for transfers between devices  218 us (42%)
  starting transfers between devices  179 us (35%)
  blocking collectives  35.7 us (7%)
  Pallas kernels  30.8 us (6%)
  local copies, waits for them, and re-layouts  25.5 us (5%)
  between operations  16.4 us (3%)
    all_to_all x1, waiting for transfers between devices, on_device(): lax.all_to_all(held.reshape(2 * MICRO, PIECE, WIDTH), BOTH, 0, 0, axis_in...  89.7 us
    ppermute x16, waiting for transfers between devices, hand_over(): return lax.ppermute(whole, BOTH, route)  64.2 us
    all_to_all x1, starting transfers between devices, on_device(): lax.all_to_all(held.reshape(2 * MICRO, PIECE, WIDTH), BOTH, 0, 0, axis_in...  58.7 us
    ppermute x7, starting transfers between devices, fetch(): return lax.ppermute(own, 'segment', [(first, 0), (second, 1)])  41.2 us
    all_gather x1, blocking collectives, on_device(): params = lax.all_gather(params, 'segment')  35.7 us
    ppermute x16, waiting for transfers between devices, exchange(): lax.ppermute(stats, BOTH, both)  28.8 us
    pallas_call x16, Pallas kernels, block_call(): pl.pallas_call(functools.partial(block_body, block, at_core, up_in, up_ou...  28.2 us
    ppermute x16, waiting for transfers between devices, exchange(): lax.ppermute(near, 'tile', other_tile)  27.5 us
  transfers between devices with their start and end apart: 85, of which 35 were waited for; matrix products, arithmetic and copies ran while one was open for 1% of the time, Pallas kernels for 6%

profile of v6, /device:TPU:38, one launch (start us, length us, event | category | flops | bytes accessed | tf_op | source)
XLA Modules:
  0.0 508.8 jit_solution(7319232171825114687)
XLA Ops:
  17.1 35.7 %all-gather = f32[256,320]{1,0:T(8,128)S(1)} all-gather(f32[16,320]{1,0:T(8,128)S(1)} %pad_maximum_fusion), channel_id=2, replica_groups=mesh['segment'=16,'tile'=16] {'segment'}, dimensions={0}, use_global_device_ids=true | all-gather | bytes 348160 | tf_op jit(solution)/shard_map/all_gather | solution.py:382
  61.6 31.9 %collective-permute-start.26 = (bf16[320,2880]{1,0:T(8,128)(2,1)}, bf16[320,2880]{1,0:T(8,128)(2,1)}, u32[]{:S(2)}, u32[]{:S(2)}) collective-permute-start(bf16[320,2880]{1,0:T(8,128)(2,1)} %bitcast.13.refs_7_), channel_id=1, source_target_pairs={{64,0},{128,16},{65,1},{129,17},{66,2},{130,18},{67,3},{131,19},{6... | collective-permute-start | bytes 5529608 | tf_op jit(solution)/shard_map/ppermute | solution.py:390
  93.5 3.1 collective-permute-done.10.refs_4_
  110.4 3.4 collective-permute-done.26.refs_7_
  113.8 15.0 %collective-permute-start.27 = (bf16[320,2880]{1,0:T(8,128)(2,1)}, bf16[320,2880]{1,0:T(8,128)(2,1)}, u32[]{:S(2)}, u32[]{:S(2)}) collective-permute-start(bf16[320,2880]{1,0:T(8,128)(2,1)} %collective-permute-done.26.refs_7_), channel_id=1, source_target_pairs={{0,16},{16,0},{32,48},{48,32},{64,80},{80,64},{96,112},{112,96},{1... | collective-permute-start | bytes 5529608 | tf_op jit(solution)/shard_map/ppermute | solution.py:413
  130.5 8.5 %collective-permute-done.19.refs_0_ = bf16[3840,128]{1,0:T(8,128)(2,1)S(1)} collective-permute-done((bf16[3840,128]{1,0:T(8,128)(2,1)S(1)}, bf16[3840,128]{1,0:T(8,128)(2,1)S(1)}, u32[]{:S(2)}, u32[]{:S(2)}) %collective-permute-start.19) | collective-permute-done | bytes 983072 | tf_op jit(solution)/shard_map/ppermute | solution.py:406
  141.6 3.0 collective-permute-done.16.refs_1_.refs_10_
  153.7 6.4 %collective-permute-start.23 = (bf16[368,128]{1,0:T(8,128)(2,1)S(1)}, bf16[368,128]{1,0:T(8,128)(2,1)S(1)}, u32[]{:S(2)}, u32[]{:S(2)}) collective-permute-start(bf16[368,128]{1,0:T(8,128)(2,1)S(1)} %get-tuple-element.205), channel_id=1, source_target_pairs={{0,16},{16,0},{32,48},{48,32},{64,80},{80,64},{96,112},{112,96},{1... | collective-permute-start | bytes 282632 | tf_op jit(solution)/shard_map/ppermute | solution.py:400
  164.1 2.5 collective-permute-start.30
  169.7 3.0 collective-permute-done.28.refs_1_
  193.4 3.0 collective-permute-done.44.refs_4_
  200.8 2.6 collective-permute-done.48.refs_4_
  206.0 4.0 collective-permute-done.46.refs_1_
  214.0 2.5 collective-permute-done.52.refs_4_
  217.7 4.2 collective-permute-done.50.refs_1_
  221.9 2.9 res_block.26
  227.8 3.1 collective-permute-done.58.refs_4_
  231.7 3.9 collective-permute-done.56.refs_1_
  238.4 55.7 %collective-permute-done.59.refs_8_ = bf16[3840,128]{1,0:T(8,128)(2,1)S(1)} collective-permute-done((bf16[3840,128]{1,0:T(8,128)(2,1)S(1)}, bf16[3840,128]{1,0:T(8,128)(2,1)S(1)}, u32[]{:S(2)}, u32[]{:S(2)}) %collective-permute-start.59) | collective-permute-done | bytes 983072 | tf_op jit(solution)/shard_map/ppermute | solution.py:406
  302.5 2.4 collective-permute-done.62.refs_1_
  319.3 7.5 %res_block.30 = (bf16[3840,128]{1,0:T(8,128)(2,1)}, bf16[368,128]{1,0:T(8,128)(2,1)S(1)}, bf16[368,128]{1,0:T(8,128)(2,1)S(1)}, bf16[48,128]{1,0:T(8,128)(2,1)S(1)}, f32[3840,128]{1,0:T(8,128)S(1)}) custom-call(s32[3]{0:T(128)S(1)} %pad_add_fusion.info, f32[3840,128]{1,0:T(8,128)S(1)} %get-tuple-element.320.refs_0_, ...), custom_call_target="tpu_custom_call" | custom-call | flops 2831155200 | bytes 4194304 | tf_op jit(solution)/shard_map/res_block/pallas_call | solution.py:297
  350.1 58.7 %all-to-all-start = ((bf16[16,960,128]{2,1,0:T(8,128)(2,1)}), bf16[16,960,128]{2,1,0:T(8,128)(2,1)}, u32[]{:S(2)}, u32[]{:S(2)}) async-start(bf16[16,960,128]{2,1,0:T(8,128)(2,1)} %bitcast.33), calls=%async_computation | async-start | bytes 7864320 | tf_op jit(solution)/shard_map/all_to_all | solution.py:464
  408.9 89.7 %all-to-all-done = bf16[16,960,128]{2,1,0:T(8,128)(2,1)} async-done(((bf16[16,960,128]{2,1,0:T(8,128)(2,1)}), bf16[16,960,128]{2,1,0:T(8,128)(2,1)}, u32[]{:S(2)}, u32[]{:S(2)}) %all-to-all-start) | async-done | bytes 3932192 | tf_op jit(solution)/shard_map/all_to_all | solution.py:464
  498.6 3.1 constant_dynamic-slice_fusion
  (265 shorter events, 136.6 us)
Async XLA Ops:
  6.5 288.6 %all-gather.4.cloned.1.call-start = ((), (), s32[]{:S(2)}) async-start(), calls=%async_computation.1 | async-start | bytes 4177920 | tf_op jit(solution)/shard_map/all_gather | solution.py:383
  9.9 43.0 %collective-permute-start.3 = (bf16[960,128]{1,0:T(8,128)(2,1)S(1)}, bf16[960,128]{1,0:T(8,128)(2,1)S(1)}, u32[]{:S(2)}, u32[]{:S(2)}) collective-permute-start(bf16[960,128]{1,0:T(8,128)(2,1)S(1)} %bitcast.51), channel_id=1, source_target_pairs={{3,0},{7,1},{11,17},{15,16},{18,2},{22,3},{26,19},{30,18},{33,4},{... | collective-permute-start | bytes 737288 | tf_op jit(solution)/shard_map/ppermute | solution.py:377
  10.6 42.3 %collective-permute-start.2 = (bf16[960,128]{1,0:T(8,128)(2,1)S(1)}, bf16[960,128]{1,0:T(8,128)(2,1)S(1)}, u32[]{:S(2)}, u32[]{:S(2)}) collective-permute-start(bf16[960,128]{1,0:T(8,128)(2,1)S(1)} %bitcast.52), channel_id=1, source_target_pairs={{2,0},{6,1},{10,17},{14,16},{19,2},{23,3},{27,19},{31,18},{32,4},{... | collective-permute-start | bytes 737288 | tf_op jit(solution)/shard_map/ppermute | solution.py:377
  11.3 41.6 %collective-permute-start.1 = (bf16[960,128]{1,0:T(8,128)(2,1)S(1)}, bf16[960,128]{1,0:T(8,128)(2,1)S(1)}, u32[]{:S(2)}, u32[]{:S(2)}) collective-permute-start(bf16[960,128]{1,0:T(8,128)(2,1)S(1)} %bitcast.53), channel_id=1, source_target_pairs={{1,0},{5,1},{9,17},{13,16},{16,2},{20,3},{24,19},{28,18},{35,4},{3... | collective-permute-start | bytes 737288 | tf_op jit(solution)/shard_map/ppermute | solution.py:377
  12.0 40.9 %collective-permute-start = (bf16[960,128]{1,0:T(8,128)(2,1)S(1)}, bf16[960,128]{1,0:T(8,128)(2,1)S(1)}, u32[]{:S(2)}, u32[]{:S(2)}) collective-permute-start(bf16[960,128]{1,0:T(8,128)(2,1)S(1)} %bitcast.54), channel_id=1, source_target_pairs={{0,0},{4,1},{8,17},{12,16},{17,2},{21,3},{25,19},{29,18},{34,4},{3... | collective-permute-start | bytes 737288 | tf_op jit(solution)/shard_map/ppermute | solution.py:377
  12.6 48.2 %collective-permute-start.7 = (bf16[320,2880]{1,0:T(8,128)(2,1)}, bf16[320,2880]{1,0:T(8,128)(2,1)}, u32[]{:S(2)}, u32[]{:S(2)}) collective-permute-start(bf16[320,2880]{1,0:T(8,128)(2,1)} %bitcast.13.refs_7_), channel_id=1, source_target_pairs={{0,16},{16,0},{32,48},{48,32},{64,80},{80,64},{96,112},{112,96},{1... | collective-permute-start | bytes 5529608 | tf_op jit(solution)/shard_map/ppermute | solution.py:413
  58.7 42.0 %collective-permute-start.20 = (bf16[320,2880]{1,0:T(8,128)(2,1)}, bf16[320,2880]{1,0:T(8,128)(2,1)S(1)}, u32[]{:S(2)}, u32[]{:S(2)}) collective-permute-start(bf16[320,2880]{1,0:T(8,128)(2,1)} %bitcast.13.refs_7_), channel_id=1, source_target_pairs={{48,0},{112,16},{49,1},{113,17},{50,2},{114,18},{51,3},{115,19},{5... | collective-permute-start | bytes 5529608 | tf_op jit(solution)/shard_map/ppermute | solution.py:390
  61.5 43.8 %collective-permute-start.15 = (bf16[320,2880]{1,0:T(8,128)(2,1)}, bf16[320,2880]{1,0:T(8,128)(2,1)S(1)}, u32[]{:S(2)}, u32[]{:S(2)}) collective-permute-start(bf16[320,2880]{1,0:T(8,128)(2,1)} %collective-permute-done.14.refs_7_), channel_id=1, source_target_pairs={{0,16},{16,0},{32,48},{48,32},{64,80},{80,64},{96,112},{112,96},{1... | collective-permute-start | bytes 5529608 | tf_op jit(solution)/shard_map/ppermute | solution.py:413
  61.6 52.2 %collective-permute-start.26 = (bf16[320,2880]{1,0:T(8,128)(2,1)}, bf16[320,2880]{1,0:T(8,128)(2,1)}, u32[]{:S(2)}, u32[]{:S(2)}) collective-permute-start(bf16[320,2880]{1,0:T(8,128)(2,1)} %bitcast.13.refs_7_), channel_id=1, source_target_pairs={{64,0},{128,16},{65,1},{129,17},{66,2},{130,18},{67,3},{131,19},{6... | collective-permute-start | bytes 5529608 | tf_op jit(solution)/shard_map/ppermute | solution.py:390
  104.1 42.1 %collective-permute-start.21 = (bf16[320,2880]{1,0:T(8,128)(2,1)S(1)}, bf16[320,2880]{1,0:T(8,128)(2,1)S(1)}, u32[]{:S(2)}, u32[]{:S(2)}) collective-permute-start(bf16[320,2880]{1,0:T(8,128)(2,1)S(1)} %collective-permute-done.20.refs_7_), channel_id=1, source_target_pairs={{0,16},{16,0},{32,48},{48,32},{64,80},{80,64},{96,112},{112,96},{1... | collective-permute-start | bytes 5529608 | tf_op jit(solution)/shard_map/ppermute | solution.py:413
  107.2 40.6 %collective-permute-start.32 = (bf16[320,2880]{1,0:T(8,128)(2,1)}, bf16[320,2880]{1,0:T(8,128)(2,1)}, u32[]{:S(2)}, u32[]{:S(2)}) collective-permute-start(bf16[320,2880]{1,0:T(8,128)(2,1)} %bitcast.13.refs_7_), channel_id=1, source_target_pairs={{80,0},{144,16},{81,1},{145,17},{82,2},{146,18},{83,3},{147,19},{8... | collective-permute-start | bytes 5529608 | tf_op jit(solution)/shard_map/ppermute | solution.py:390
  109.1 29.9 %collective-permute-start.19 = (bf16[3840,128]{1,0:T(8,128)(2,1)S(1)}, bf16[3840,128]{1,0:T(8,128)(2,1)S(1)}, u32[]{:S(2)}, u32[]{:S(2)}) collective-permute-start(bf16[3840,128]{1,0:T(8,128)(2,1)S(1)} %get-tuple-element.195.refs_0_.refs_12_), channel_id=1, source_target_pairs={{0,0},{1,1},{17,9},{16,8},{2,2},{3,3},{19,11},{18,10},{4,4},{5,5},... | collective-permute-start | bytes 2949128 | tf_op jit(solution)/shard_map/ppermute | solution.py:406
  113.8 47.3 %collective-permute-start.27 = (bf16[320,2880]{1,0:T(8,128)(2,1)}, bf16[320,2880]{1,0:T(8,128)(2,1)}, u32[]{:S(2)}, u32[]{:S(2)}) collective-permute-start(bf16[320,2880]{1,0:T(8,128)(2,1)} %collective-permute-done.26.refs_7_), channel_id=1, source_target_pairs={{0,16},{16,0},{32,48},{48,32},{64,80},{80,64},{96,112},{112,96},{1... | collective-permute-start | bytes 5529608 | tf_op jit(solution)/shard_map/ppermute | solution.py:413
  147.8 27.6 %collective-permute-start.33 = (bf16[320,2880]{1,0:T(8,128)(2,1)}, bf16[320,2880]{1,0:T(8,128)(2,1)}, u32[]{:S(2)}, u32[]{:S(2)}) collective-permute-start(bf16[320,2880]{1,0:T(8,128)(2,1)} %collective-permute-done.32.refs_7_), channel_id=1, source_target_pairs={{0,16},{16,0},{32,48},{48,32},{64,80},{80,64},{96,112},{112,96},{1... | collective-permute-start | bytes 5529608 | tf_op jit(solution)/shard_map/ppermute | solution.py:413
  149.8 25.7 %collective-permute-start.31 = (bf16[3840,128]{1,0:T(8,128)(2,1)S(1)}, bf16[3840,128]{1,0:T(8,128)(2,1)S(1)}, u32[]{:S(2)}, u32[]{:S(2)}) collective-permute-start(bf16[3840,128]{1,0:T(8,128)(2,1)S(1)} %get-tuple-element.219.refs_0_.refs_12_), channel_id=1, source_target_pairs={{0,32},{1,33},{17,41},{16,40},{2,34},{3,35},{19,43},{18,42},{4,36}... | collective-permute-start | bytes 2949128 | tf_op jit(solution)/shard_map/ppermute | solution.py:406
  162.6 29.8 %collective-permute-start.54 = (bf16[320,2880]{1,0:T(8,128)(2,1)}, bf16[320,2880]{1,0:T(8,128)(2,1)S(1)}, u32[]{:S(2)}, u32[]{:S(2)}) collective-permute-start(bf16[320,2880]{1,0:T(8,128)(2,1)} %bitcast.13.refs_7_), channel_id=1, source_target_pairs={{160,0},{224,16},{161,1},{225,17},{162,2},{226,18},{163,3},{227,19... | collective-permute-start | bytes 5529608 | tf_op jit(solution)/shard_map/ppermute | solution.py:390
  196.4 25.5 %collective-permute-start.55 = (bf16[320,2880]{1,0:T(8,128)(2,1)S(1)}, bf16[320,2880]{1,0:T(8,128)(2,1)S(1)}, u32[]{:S(2)}, u32[]{:S(2)}) collective-permute-start(bf16[320,2880]{1,0:T(8,128)(2,1)S(1)} %collective-permute-done.54.refs_7_), channel_id=1, source_target_pairs={{0,16},{16,0},{32,48},{48,32},{64,80},{80,64},{96,112},{112,96},{1... | collective-permute-start | bytes 5529608 | tf_op jit(solution)/shard_map/ppermute | solution.py:413
  197.6 27.2 %collective-permute-start.66 = (bf16[320,2880]{1,0:T(8,128)(2,1)}, bf16[320,2880]{1,0:T(8,128)(2,1)}, u32[]{:S(2)}, u32[]{:S(2)}) collective-permute-start(bf16[320,2880]{1,0:T(8,128)(2,1)} %bitcast.13.refs_7_), channel_id=1, source_target_pairs={{192,0},{208,16},{193,1},{209,17},{194,2},{210,18},{195,3},{211,19... | collective-permute-start | bytes 5529608 | tf_op jit(solution)/shard_map/ppermute | solution.py:390
  212.9 82.2 %collective-permute-start.61 = (bf16[320,2880]{1,0:T(8,128)(2,1)}, bf16[320,2880]{1,0:T(8,128)(2,1)}, u32[]{:S(2)}, u32[]{:S(2)}) collective-permute-start(bf16[320,2880]{1,0:T(8,128)(2,1)} %collective-permute-done.60.refs_7_), channel_id=1, source_target_pairs={{0,16},{16,0},{32,48},{48,32},{64,80},{80,64},{96,112},{112,96},{1... | collective-permute-start | bytes 5529608 | tf_op jit(solution)/shard_map/ppermute | solution.py:413
  224.8 80.9 %collective-permute-start.67 = (bf16[320,2880]{1,0:T(8,128)(2,1)}, bf16[320,2880]{1,0:T(8,128)(2,1)}, u32[]{:S(2)}, u32[]{:S(2)}) collective-permute-start(bf16[320,2880]{1,0:T(8,128)(2,1)} %collective-permute-done.66.refs_7_), channel_id=1, source_target_pairs={{0,16},{16,0},{32,48},{48,32},{64,80},{80,64},{96,112},{112,96},{1... | collective-permute-start | bytes 5529608 | tf_op jit(solution)/shard_map/ppermute | solution.py:413
  224.9 69.2 %collective-permute-start.59 = (bf16[3840,128]{1,0:T(8,128)(2,1)S(1)}, bf16[3840,128]{1,0:T(8,128)(2,1)S(1)}, u32[]{:S(2)}, u32[]{:S(2)}) collective-permute-start(bf16[3840,128]{1,0:T(8,128)(2,1)S(1)} %get-tuple-element.283.refs_0_), channel_id=1, source_target_pairs={{0,0},{1,1},{17,9},{16,8},{2,2},{3,3},{19,11},{18,10},{4,4},{5,5},... | collective-permute-start | bytes 2949128 | tf_op jit(solution)/shard_map/ppermute | solution.py:406
  226.2 79.5 %collective-permute-start.65 = (bf16[3840,128]{1,0:T(8,128)(2,1)}, bf16[3840,128]{1,0:T(8,128)(2,1)}, u32[]{:S(2)}, u32[]{:S(2)}) collective-permute-start(bf16[3840,128]{1,0:T(8,128)(2,1)} %get-tuple-element.295.refs_0_), channel_id=1, source_target_pairs={{0,16},{1,17},{17,25},{16,24},{2,18},{3,19},{19,27},{18,26},{4,20}... | collective-permute-start | bytes 2949128 | tf_op jit(solution)/shard_map/ppermute | solution.py:406
  236.8 75.0 %collective-permute-start.71 = (bf16[3840,128]{1,0:T(8,128)(2,1)}, bf16[3840,128]{1,0:T(8,128)(2,1)}, u32[]{:S(2)}, u32[]{:S(2)}) collective-permute-start(bf16[3840,128]{1,0:T(8,128)(2,1)} %get-tuple-element.307.refs_0_), channel_id=1, source_target_pairs={{0,32},{1,33},{17,41},{16,40},{2,34},{3,35},{19,43},{18,42},{4,36}... | collective-permute-start | bytes 2949128 | tf_op jit(solution)/shard_map/ppermute | solution.py:406
  350.1 148.4 %all-to-all-start = ((bf16[16,960,128]{2,1,0:T(8,128)(2,1)}), bf16[16,960,128]{2,1,0:T(8,128)(2,1)}, u32[]{:S(2)}, u32[]{:S(2)}) async-start(bf16[16,960,128]{2,1,0:T(8,128)(2,1)} %bitcast.33), calls=%async_computation | async-start | bytes 7864320 | tf_op jit(solution)/shard_map/all_to_all | solution.py:464
  (102 other events, 620.7 us)
Sparse Core Ops, SparseCore 0:
  149.9 69.0 all-gather.3

commit v7 on v6

--- a/solution.py
+++ b/solution.py
@@ -17,6 +17,8 @@
 OWN = ROWS * CH
 MEMBERS = float(48 * WIDTH * GROUP)
 MIB = 1024 * 1024
+LEAD = 2944
+HALF = 1536
 STATS = 48
 BF, F32 = jnp.bfloat16, jnp.float32
 ANY = pl.BlockSpec(memory_space=pl.ANY)
@@ -24,9 +26,11 @@
 SM = pl.BlockSpec(memory_space=pltpu.SMEM)
 BOTH = ("segment", "tile")
 
-PAIRS = ((0, 1), (2, 6), (3, 7), (4, 8), (5, 9), (10, 14), (11, 15), (12, 13))
-FETCH_AFTER = {0: 3, 2: 4, 4: 5, 6: 6, 8: 7}
-SWAP_AFTER = {0: 1, 1: 2, 2: 3, 3: 4, 6: 5, 8: 6, 10: 7}
+PAIRS = ((0, 1), (2, 6), (3, 7), (4, 8), (5, 9), (10, 14), (11, 12), (13, 15))
+FETCH_AFTER = {(2, 0): 0, (2, 1): 1, (3, 0): 1, (3, 1): 2, (4, 0): 2, (4, 1): 3}
+FETCH_AFTER |= {(5, 0): 5, (5, 1): 6, (6, 0): 7, (6, 1): 8, (7, 0): 9, (7, 1): 10}
+SWAP_AFTER = {(1, 0): 0, (1, 1): 1, (2, 0): 1, (2, 1): 2, (3, 0): 2, (3, 1): 3, (4, 0): 3, (4, 1): 4}
+SWAP_AFTER |= {(5, 0): 6, (5, 1): 7, (6, 0): 8, (6, 1): 9, (7, 0): 10, (7, 1): 11}
 
 
 def place(slot, quarter):
@@ -107,8 +111,8 @@
         del refs[:n]
         return got
 
-    source, near, cross, own_stats, far_stats, member, params_all = take(7)
-    weights = take(2)
+    source, near, cross, own_stats, far_stats, member = take(6)
+    weights = take(4)
     if up_in or up_out:
         (skips,) = take(1)
     if up_in:
@@ -131,13 +135,17 @@
     @pl.when(info[2] == 1)
     def _():
         core = info[0] // 2
-        params_copy = pltpu.make_async_copy(params_all.at[block], ps, w_sem.at[2])
-        params_copy.start()
+        head = pl.ds(LEAD - HALF - WIDTH, WIDTH)
+        halves = (pl.ds(0, HALF), pl.ds(HALF, LEAD - HALF))
         for at in range(2):
 
             @pl.when((core == at_core) == (at == 0))
             def _():
-                pltpu.make_async_copy(weights[at], ws, w_sem.at[0]).start()
+                pltpu.make_async_copy(weights[2 + at].at[:, head], ps, w_sem.at[2]).start()
+                for n, part in enumerate(halves):
+                    pltpu.make_async_copy(
+                        weights[2 * n + at], ws.at[:, part], w_sem.at[3 * n]
+                    ).start()
 
         if up_in:
             in_copy = pltpu.make_async_copy(skips.at[block], sk_in, w_sem.at[1])
@@ -157,8 +165,9 @@
         mean = jnp.sum(jnp.where(even_kind, groups, 0.0), axis=1, keepdims=True) / MEMBERS
         mean_sq = jnp.sum(jnp.where(even_kind, 0.0, groups), axis=1, keepdims=True) / MEMBERS
         variance = jnp.maximum(mean_sq - mean * mean, 0.0)
-        params_copy.wait()
-        params = jnp.transpose(ps[...])
+        pltpu.make_async_copy(weights[2].at[:, head], ps, w_sem.at[2]).wait()
+        tailing = ps[:, 64:128].astype(F32)
+        params = tailing[:, 0:16] + tailing[:, 16:32] + tailing[:, 32:48]
         lane = lax.broadcasted_iota(jnp.int32, (CH, 16), 1)
         shift = jnp.sum(jnp.where(lane == info[1] + 8, params, 0.0), axis=1, keepdims=True)
         wide = (CH, WIDTH)
@@ -212,7 +221,8 @@
             lift_at(row)
         lift_at(2)
         lift_at(3)
-        pltpu.make_async_copy(weights[0], ws, w_sem.at[0]).wait()
+        for n, part in enumerate(halves):
+            pltpu.make_async_copy(weights[2 * n], ws.at[:, part], w_sem.at[3 * n]).wait()
         for pair in range(ROWS // 2):
             if pair:
                 lift_at(2 * pair + 2)
@@ -265,21 +275,21 @@
     )(info, *pieces)
 
 
-def block_call(block, at_core, info, source, exchanged, member, params, weights, skips, lateral_edges, lateral):
+def block_call(block, at_core, info, source, exchanged, member, weights, skips, lateral_edges, lateral):
     up_in, up_out = lateral_edges is not None, lateral is not None
     last = block == BLOCKS - 1
-    operands = [source, *exchanged, member, params, *weights]
-    specs = [VM] * 6 + [ANY] * 3
+    operands = [source, *exchanged, member, *weights]
+    specs = [VM] * 6 + [ANY] * 4
     shapes, out_specs = [WHOLE] + EXCHANGED, [VM] * 4
     if last:
         shapes, out_specs = shapes[:1], out_specs[:1]
     scratch = [
-        pltpu.VMEM((CH, TAPS), BF),
-        pltpu.VMEM((16, CH), F32),
+        pltpu.VMEM((CH, LEAD), BF),
+        pltpu.VMEM((CH, WIDTH), BF),
         pltpu.VMEM((CAT, (ROWS + 2) * WIDTH), BF),
         pltpu.VMEM((CH, WIDTH), F32),
         pltpu.VMEM((CH, WIDTH), F32),
-        pltpu.SemaphoreType.DMA((3,)),
+        pltpu.SemaphoreType.DMA((4,)),
     ]
     if up_in or up_out:
         operands.append(skips)
@@ -302,7 +312,7 @@
         scratch_shapes=scratch,
         compiler_params=pltpu.CompilerParams(vmem_limit_bytes=28 * MIB),
         cost_estimate=pl.CostEstimate(
-            flops=2 * OWN * WIDTH * TAPS, bytes_accessed=4 * MIB, transcendentals=OWN * WIDTH
+            flops=OWN * WIDTH * TAPS // 4, bytes_accessed=MIB, transcendentals=0
         ),
         name="res_block",
     )(info, *operands)
@@ -343,7 +353,7 @@
             pltpu.SemaphoreType.DMA((2,)),
             pltpu.SemaphoreType.DMA((4,)),
         ],
-        compiler_params=pltpu.CompilerParams(vmem_limit_bytes=16 * MIB),
+        compiler_params=pltpu.CompilerParams(vmem_limit_bytes=56 * MIB),
         name="pick",
     )(info, *wholes)
 
@@ -379,13 +389,18 @@
     encoded = sinusoid(timesteps[plan], time_weight.shape[1] // 2)
     shifts = jnp.dot(encoded, time_weight[0], precision=lax.Precision.HIGHEST)
     params = jnp.concatenate([norm_gain, norm_bias, jnp.zeros((6, CH), F32), shifts], axis=0)
-    params = lax.all_gather(params, "segment")
+    high = lax.reduce_precision(params, 8, 7)
+    left = params - high
+    middle = lax.reduce_precision(left, 8, 7)
+    coded = jnp.concatenate([high, middle, left - middle], axis=0).astype(BF)
     skips = lax.all_gather(skip_weight[0].T, "segment")
-    lead = conv_weight[0].T
+    conv = conv_weight[0].T
+    padding = jnp.zeros((CH, LEAD - TAPS - STATS), BF)
+    lead = (conv[:, :HALF], jnp.concatenate([conv[:, HALF:], coded.T, padding], axis=1))
     first_up = BLOCKS - DOWN
 
-    def fetch(index, after):
-        own, _ = lax.optimization_barrier((lead, after))
+    def fetch(index, half, after):
+        own, _ = lax.optimization_barrier((lead[half], after))
         first, second = PAIRS[index]
         return lax.ppermute(own, "segment", [(first, 0), (second, 1)])
 
@@ -410,15 +425,15 @@
     weights, cores, fetched = {}, {}, {}
 
     def swap_cores(index, own):
-        both = own, lax.ppermute(own, "segment", [(b, b ^ 1) for b in range(BLOCKS)])
+        both = [own, lax.ppermute(own, "segment", [(b, b ^ 1) for b in range(BLOCKS)])]
         for at, block in enumerate(PAIRS[index]):
-            weights[block], cores[block] = both, at
-
-    swap_cores(0, lead)
-    pieces, params = lax.optimization_barrier((pieces, params))
+            weights[block], cores[block] = weights.get(block, []) + both, at
+
+    for own in lead:
+        swap_cores(0, own)
     *exchanged, source = first_call(info, pieces)
-    fetched[1] = fetch(1, pieces)
-    fetched[2] = fetch(2, source)
+    fetched[1, 0] = fetch(1, 0, pieces[0])
+    fetched[1, 1] = fetch(1, 1, source)
     wholes, edges_of, passing = [], {}, []
     for block in range(BLOCKS):
         up_in, up_out = block >= first_up, first_up - 1 <= block < BLOCKS - 1
@@ -428,9 +443,9 @@
         if block >= 1:
             sent, _ = lax.optimization_barrier((wholes[-1], (near_in, cross_in, far)))
             passing.append(hand_over(block - 1, sent))
-        if block >= 3:
-            source, near_in, cross_in, far, passing[block - 3] = lax.optimization_barrier(
-                (source, near_in, cross_in, far, passing[block - 3])
+        if block >= 4:
+            source, near_in, cross_in, far, passing[block - 4] = lax.optimization_barrier(
+                (source, near_in, cross_in, far, passing[block - 4])
             )
         whole, exchanged, summed = block_call(
             block,
@@ -439,7 +454,6 @@
             source,
             (near_in, cross_in, stats, far),
             member,
-            params,
             weights[block],
             skips,
             edges_of[BLOCKS - block] if up_in else None,
@@ -447,13 +461,13 @@
         )
         wholes.append(whole)
         source = summed if up_out else whole
-        if block in SWAP_AFTER:
-            index = SWAP_AFTER[block]
-            own, _ = lax.optimization_barrier((fetched[index], whole))
-            swap_cores(index, own)
-        if block in FETCH_AFTER:
-            index = FETCH_AFTER[block]
-            fetched[index] = fetch(index, whole)
+        for key, after in SWAP_AFTER.items():
+            if after == block:
+                own, _ = lax.optimization_barrier((fetched[key], whole))
+                swap_cores(key[0], own)
+        for key, after in FETCH_AFTER.items():
+            if after == block:
+                fetched[key] = fetch(*key, whole)
     passing.append(hand_over(BLOCKS - 1, wholes[-1]))
     held = pick((segment % 8).astype(jnp.int32)[None], passing)
     peers = [

time: 518 us -> 519 us (level)
  the two profiles are of different devices: /device:TPU:38 before, /device:TPU:4 now
where the time goes in v7:
time: 519 us; the launch traced here: 508 us
  waiting for transfers between devices  228 us (44%)
  Pallas kernels  130 us (25%)
  starting transfers between devices  107 us (21%)
  local copies, waits for them, and re-layouts  25.8 us (5%)
  between operations  16.9 us (3%)
    pallas_call x16, Pallas kernels, block_call(): pl.pallas_call(functools.partial(block_body, block, at_core, up_in, up_ou...  124 us
    all_to_all x1, waiting for transfers between devices, on_device(): lax.all_to_all(held.reshape(2 * MICRO, PIECE, WIDTH), BOTH, 0, 0, axis_in...  89.2 us
    ppermute x16, waiting for transfers between devices, hand_over(): return lax.ppermute(whole, BOTH, route)  41.1 us
    ppermute x16, waiting for transfers between devices, exchange(): lax.ppermute(stats, BOTH, both)  34.5 us
    ppermute x16, waiting for transfers between devices, exchange(): lax.ppermute(near, 'tile', other_tile)  26.6 us
    ppermute x16, starting transfers between devices, hand_over(): return lax.ppermute(whole, BOTH, route)  26.3 us
    ppermute x16, starting transfers between devices, exchange(): lax.ppermute(near, 'tile', other_tile)  22.5 us
    ppermute x14, starting transfers between devices, fetch(): return lax.ppermute(own, 'segment', [(first, 0), (second, 1)])  18 us
  transfers between devices with their start and end apart: 100, of which 45 were waited for; matrix products, arithmetic and copies ran while one was open for 2% of the time, Pallas kernels for 25%

profile of v7, /device:TPU:4, one launch (start us, length us, event | category | flops | bytes accessed | tf_op | source)
XLA Modules:
  0.0 508.2 jit_solution(14444855340906222712)
XLA Ops:
  30.7 13.8 %collective-permute-done.2.refs_2_ = bf16[960,128]{1,0:T(8,128)(2,1)S(1)} collective-permute-done((bf16[960,128]{1,0:T(8,128)(2,1)S(1)}, bf16[960,128]{1,0:T(8,128)(2,1)S(1)}, u32[]{:S(2)}, u32[]{:S(2)}) %collective-permute-start.2) | collective-permute-done | bytes 245792 | tf_op jit(solution)/shard_map/ppermute | solution.py:387
  51.8 5.6 %collective-permute-start.4 = (bf16[368,128]{1,0:T(8,128)(2,1)S(1)}, bf16[368,128]{1,0:T(8,128)(2,1)S(1)}, u32[]{:S(2)}, u32[]{:S(2)}) collective-permute-start(bf16[368,128]{1,0:T(8,128)(2,1)S(1)} %get-tuple-element.177), channel_id=1, source_target_pairs={{0,1},{1,0},{2,3},{3,2},{4,5},{5,4},{6,7},{7,6},{8,9},{9,8},{10,11... | collective-permute-start | bytes 282632 | tf_op jit(solution)/shard_map/ppermute | solution.py:414
  62.1 5.9 %res_block.16 = (bf16[3840,128]{1,0:T(8,128)(2,1)S(1)}, bf16[368,128]{1,0:T(8,128)(2,1)S(1)}, bf16[368,128]{1,0:T(8,128)(2,1)S(1)}, bf16[48,128]{1,0:T(8,128)(2,1)S(1)}) custom-call(s32[3]{0:T(128)S(1)} %pad_add_fusion.info, bf16[3840,128]{1,0:T(8,128)(2,1)S(1)} %get-tuple-element.176.refs_0_, bf16[368,128]{1,0:T(8,128)(2,1)S(1)} %collective-permute-done.4.refs_1_, ...), custom_call_target="tpu_custom_call" | custom-call | flops 353894400 | bytes 1048576 | tf_op jit(solution)/shard_map/res_block/pallas_call | solution.py:307
  75.0 9.5 %res_block.17 = (bf16[3840,128]{1,0:T(8,128)(2,1)S(1)}, bf16[368,128]{1,0:T(8,128)(2,1)S(1)}, bf16[368,128]{1,0:T(8,128)(2,1)}, bf16[48,128]{1,0:T(8,128)(2,1)S(1)}) custom-call(s32[3]{0:T(128)S(1)} %pad_add_fusion.info, bf16[3840,128]{1,0:T(8,128)(2,1)S(1)} %get-tuple-element.204.refs_0_.refs_13_, ...), custom_call_target="tpu_custom_call" | custom-call | flops 353894400 | bytes 1048576 | tf_op jit(solution)/shard_map/res_block/pallas_call | solution.py:307
  101.4 6.3 %res_block.18 = (bf16[3840,128]{1,0:T(8,128)(2,1)S(1)}, bf16[368,128]{1,0:T(8,128)(2,1)S(1)}, bf16[368,128]{1,0:T(8,128)(2,1)S(1)}, bf16[48,128]{1,0:T(8,128)(2,1)S(1)}) custom-call(s32[3]{0:T(128)S(1)} %pad_add_fusion.info, bf16[3840,128]{1,0:T(8,128)(2,1)S(1)} %copy-done.5, bf16[368,128]{1,0:T(8,128)(2,1)S(1)} %collective-permute-done.12.refs_1_.refs_11_, ...), custom_call_target="tpu_custom_call" | custom-call | flops 353894400 | bytes 1048576 | tf_op jit(solution)/shard_map/res_block/pallas_call | solution.py:307
  124.9 8.5 %res_block.19 = (bf16[3840,128]{1,0:T(8,128)(2,1)S(1)}, bf16[368,128]{1,0:T(8,128)(2,1)S(1)}, bf16[368,128]{1,0:T(8,128)(2,1)S(1)}, bf16[48,128]{1,0:T(8,128)(2,1)S(1)}) custom-call(s32[3]{0:T(128)S(1)} %pad_add_fusion.info, bf16[3840,128]{1,0:T(8,128)(2,1)S(1)} %get-tuple-element.232.refs_0_.refs_13_, ...), custom_call_target="tpu_custom_call" | custom-call | flops 353894400 | bytes 1048576 | tf_op jit(solution)/shard_map/res_block/pallas_call | solution.py:307
  139.0 5.5 %collective-permute-done.29.refs_0_ = bf16[3840,128]{1,0:T(8,128)(2,1)S(1)} collective-permute-done((bf16[3840,128]{1,0:T(8,128)(2,1)S(1)}, bf16[3840,128]{1,0:T(8,128)(2,1)S(1)}, u32[]{:S(2)}, u32[]{:S(2)}) %collective-permute-start.29) | collective-permute-done | bytes 983072 | tf_op jit(solution)/shard_map/ppermute | solution.py:421
  159.5 5.9 %res_block.20 = (bf16[3840,128]{1,0:T(8,128)(2,1)S(1)}, bf16[368,128]{1,0:T(8,128)(2,1)S(1)}, bf16[368,128]{1,0:T(8,128)(2,1)S(1)}, bf16[48,128]{1,0:T(8,128)(2,1)S(1)}) custom-call(s32[3]{0:T(128)S(1)} %pad_add_fusion.info, bf16[3840,128]{1,0:T(8,128)(2,1)S(1)} %get-tuple-element.242.refs_0_.refs_11_, ...), custom_call_target="tpu_custom_call" | custom-call | flops 353894400 | bytes 1048576 | tf_op jit(solution)/shard_map/res_block/pallas_call | solution.py:307
  174.9 7.3 %res_block.21 = (bf16[3840,128]{1,0:T(8,128)(2,1)S(1)}, bf16[368,128]{1,0:T(8,128)(2,1)S(1)}, bf16[368,128]{1,0:T(8,128)(2,1)S(1)}, bf16[48,128]{1,0:T(8,128)(2,1)S(1)}) custom-call(s32[3]{0:T(128)S(1)} %pad_add_fusion.info, bf16[3840,128]{1,0:T(8,128)(2,1)S(1)} %get-tuple-element.252.refs_0_, bf16[368,128]{1,0:T(8,128)(2,1)S(1)} %collective-permute-done.34.refs_1_, ...), custom_call_target="tpu_custom_call" | custom-call | flops 353894400 | bytes 1048576 | tf_op jit(solution)/shard_map/res_block/pallas_call | solution.py:307
  188.4 6.4 %res_block.22 = (bf16[3840,128]{1,0:T(8,128)(2,1)S(1)}, bf16[368,128]{1,0:T(8,128)(2,1)S(1)}, bf16[368,128]{1,0:T(8,128)(2,1)S(1)}, bf16[48,128]{1,0:T(8,128)(2,1)S(1)}) custom-call(s32[3]{0:T(128)S(1)} %pad_add_fusion.info, bf16[3840,128]{1,0:T(8,128)(2,1)S(1)} %get-tuple-element.262.refs_0_, bf16[368,128]{1,0:T(8,128)(2,1)S(1)} %collective-permute-done.42.refs_1_, ...), custom_call_target="tpu_custom_call" | custom-call | flops 353894400 | bytes 1048576 | tf_op jit(solution)/shard_map/res_block/pallas_call | solution.py:307
  200.7 7.3 %res_block.23 = (bf16[3840,128]{1,0:T(8,128)(2,1)S(1)}, bf16[368,128]{1,0:T(8,128)(2,1)S(1)}, bf16[368,128]{1,0:T(8,128)(2,1)S(1)}, bf16[48,128]{1,0:T(8,128)(2,1)S(1)}) custom-call(s32[3]{0:T(128)S(1)} %pad_add_fusion.info, bf16[3840,128]{1,0:T(8,128)(2,1)S(1)} %get-tuple-element.272.refs_0_, bf16[368,128]{1,0:T(8,128)(2,1)S(1)} %collective-permute-done.46.refs_1_, ...), custom_call_target="tpu_custom_call" | custom-call | flops 353894400 | bytes 1048576 | tf_op jit(solution)/shard_map/res_block/pallas_call | solution.py:307
  215.3 7.0 %res_block.24 = (bf16[3840,128]{1,0:T(8,128)(2,1)}, bf16[368,128]{1,0:T(8,128)(2,1)S(1)}, bf16[368,128]{1,0:T(8,128)(2,1)S(1)}, bf16[48,128]{1,0:T(8,128)(2,1)S(1)}) custom-call(s32[3]{0:T(128)S(1)} %pad_add_fusion.info, bf16[3840,128]{1,0:T(8,128)(2,1)S(1)} %get-tuple-element.286.refs_0_, bf16[368,128]{1,0:T(8,128)(2,1)S(1)} %collective-permute-done.50.refs_1_, ...), custom_call_target="tpu_custom_call" | custom-call | flops 353894400 | bytes 1048576 | tf_op jit(solution)/shard_map/res_block/pallas_call | solution.py:307
  234.0 11.1 %res_block.25 = (bf16[3840,128]{1,0:T(8,128)(2,1)}, bf16[368,128]{1,0:T(8,128)(2,1)S(1)}, bf16[368,128]{1,0:T(8,128)(2,1)S(1)}, bf16[48,128]{1,0:T(8,128)(2,1)S(1)}) custom-call(s32[3]{0:T(128)S(1)} %pad_add_fusion.info, bf16[3840,128]{1,0:T(8,128)(2,1)} %get-tuple-element.300.refs_0_, bf16[368,128]{1,0:T(8,128)(2,1)S(1)} %collective-permute-done.54.refs_1_, ...), custom_call_target="tpu_custom_call" | custom-call | flops 353894400 | bytes 1048576 | tf_op jit(solution)/shard_map/res_block/pallas_call | solution.py:307
  260.4 7.9 %res_block.26 = (bf16[3840,128]{1,0:T(8,128)(2,1)}, bf16[368,128]{1,0:T(8,128)(2,1)S(1)}, bf16[368,128]{1,0:T(8,128)(2,1)S(1)}, bf16[48,128]{1,0:T(8,128)(2,1)S(1)}) custom-call(s32[3]{0:T(128)S(1)} %pad_add_fusion.info, bf16[3840,128]{1,0:T(8,128)(2,1)} %get-tuple-element.310.refs_0_, bf16[368,128]{1,0:T(8,128)(2,1)S(1)} %collective-permute-done.58.refs_1_, ...), custom_call_target="tpu_custom_call" | custom-call | flops 353894400 | bytes 1048576 | tf_op jit(solution)/shard_map/res_block/pallas_call | solution.py:307
  290.2 9.0 %res_block.27 = (bf16[3840,128]{1,0:T(8,128)(2,1)S(1)}, bf16[368,128]{1,0:T(8,128)(2,1)S(1)}, bf16[368,128]{1,0:T(8,128)(2,1)S(1)}, bf16[48,128]{1,0:T(8,128)(2,1)S(1)}, f32[3840,128]{1,0:T(8,128)S(1)}) custom-call(s32[3]{0:T(128)S(1)} %pad_add_fusion.info, bf16[3840,128]{1,0:T(8,128)(2,1)} %get-tuple-element.325.refs_0_, bf16[368,128]{1,0:T(8,128)(2,1)S(1)} %copy-done.36, ...), custom_call_target="tpu_custom_call" | custom-call | flops 353894400 | bytes 1048576 | tf_op jit(solution)/shard_map/res_block/pallas_call | solution.py:307
  310.3 8.3 %res_block.28 = (bf16[3840,128]{1,0:T(8,128)(2,1)}, bf16[368,128]{1,0:T(8,128)(2,1)S(1)}, bf16[368,128]{1,0:T(8,128)(2,1)S(1)}, bf16[48,128]{1,0:T(8,128)(2,1)S(1)}, f32[3840,128]{1,0:T(8,128)S(1)}) custom-call(s32[3]{0:T(128)S(1)} %pad_add_fusion.info, f32[3840,128]{1,0:T(8,128)S(1)} %get-tuple-element.302.refs_0_, ...), custom_call_target="tpu_custom_call" | custom-call | flops 353894400 | bytes 1048576 | tf_op jit(solution)/shard_map/res_block/pallas_call | solution.py:307
  328.1 8.7 %res_block.29 = (bf16[3840,128]{1,0:T(8,128)(2,1)}, bf16[368,128]{1,0:T(8,128)(2,1)S(1)}, bf16[368,128]{1,0:T(8,128)(2,1)S(1)}, bf16[48,128]{1,0:T(8,128)(2,1)S(1)}, f32[3840,128]{1,0:T(8,128)S(1)}) custom-call(s32[3]{0:T(128)S(1)} %pad_add_fusion.info, f32[3840,128]{1,0:T(8,128)S(1)} %get-tuple-element.312.refs_0_, ...), custom_call_target="tpu_custom_call" | custom-call | flops 353894400 | bytes 1048576 | tf_op jit(solution)/shard_map/res_block/pallas_call | solution.py:307
  342.0 8.2 %res_block.30 = (bf16[3840,128]{1,0:T(8,128)(2,1)}, bf16[368,128]{1,0:T(8,128)(2,1)S(1)}, bf16[368,128]{1,0:T(8,128)(2,1)S(1)}, bf16[48,128]{1,0:T(8,128)(2,1)S(1)}, f32[3840,128]{1,0:T(8,128)S(1)}) custom-call(s32[3]{0:T(128)S(1)} %pad_add_fusion.info, f32[3840,128]{1,0:T(8,128)S(1)} %get-tuple-element.327.refs_0_, ...), custom_call_target="tpu_custom_call" | custom-call | flops 353894400 | bytes 1048576 | tf_op jit(solution)/shard_map/res_block/pallas_call | solution.py:307
  359.2 6.2 %res_block.31 = bf16[3840,128]{1,0:T(8,128)(2,1)S(1)} custom-call(s32[3]{0:T(128)S(1)} %pad_add_fusion.info, f32[3840,128]{1,0:T(8,128)S(1)} %get-tuple-element.343.refs_0_, bf16[368,128]{1,0:T(8,128)(2,1)S(1)} %collective-permute-done.90.refs_1_, bf16[368,128]{1,0:T(8,128)(2,1)S(1)} %collective-permute-done.91.refs_2_, ...), custom_call_target="tpu_custom_call" | custom-call | flops 353894400 | bytes 1048576 | tf_op jit(solution)/shard_map/res_block/pallas_call | solution.py:307
  366.8 9.3 %collective-permute-done.95.refs_13_ = bf16[3840,128]{1,0:T(8,128)(2,1)} collective-permute-done((bf16[3840,128]{1,0:T(8,128)(2,1)}, bf16[3840,128]{1,0:T(8,128)(2,1)}, u32[]{:S(2)}, u32[]{:S(2)}) %collective-permute-start.95) | collective-permute-done | bytes 983072 | tf_op jit(solution)/shard_map/ppermute | solution.py:421
  376.2 10.5 %collective-permute-done.96.refs_14_ = bf16[3840,128]{1,0:T(8,128)(2,1)} collective-permute-done((bf16[3840,128]{1,0:T(8,128)(2,1)}, bf16[3840,128]{1,0:T(8,128)(2,1)}, u32[]{:S(2)}, u32[]{:S(2)}) %collective-permute-start.96) | collective-permute-done | bytes 983072 | tf_op jit(solution)/shard_map/ppermute | solution.py:421
  386.7 10.4 %collective-permute-done.97.refs_15_ = bf16[3840,128]{1,0:T(8,128)(2,1)S(1)} collective-permute-done((bf16[3840,128]{1,0:T(8,128)(2,1)S(1)}, bf16[3840,128]{1,0:T(8,128)(2,1)S(1)}, u32[]{:S(2)}, u32[]{:S(2)}) %collective-permute-start.97) | collective-permute-done | bytes 983072 | tf_op jit(solution)/shard_map/ppermute | solution.py:421
  401.3 7.5 %all-to-all-start = ((bf16[16,960,128]{2,1,0:T(8,128)(2,1)}), bf16[16,960,128]{2,1,0:T(8,128)(2,1)}, u32[]{:S(2)}, u32[]{:S(2)}) async-start(bf16[16,960,128]{2,1,0:T(8,128)(2,1)} %bitcast.33), calls=%async_computation | async-start | bytes 7864320 | tf_op jit(solution)/shard_map/all_to_all | solution.py:478
  408.8 89.2 %all-to-all-done = bf16[16,960,128]{2,1,0:T(8,128)(2,1)} async-done(((bf16[16,960,128]{2,1,0:T(8,128)(2,1)}), bf16[16,960,128]{2,1,0:T(8,128)(2,1)}, u32[]{:S(2)}, u32[]{:S(2)}) %all-to-all-start) | async-done | bytes 3932192 | tf_op jit(solution)/shard_map/all_to_all | solution.py:478
  (328 shorter events, 215.7 us)
Async XLA Ops:
  6.6 276.1 %all-gather.3.cloned.1.call-start = ((), (), s32[]{:S(2)}) async-start(), calls=%async_computation.1 | async-start | bytes 4177920 | tf_op jit(solution)/shard_map/all_gather | solution.py:396
  15.8 46.3 %collective-permute-start.7 = (bf16[320,1536]{1,0:T(8,128)(2,1)S(1)}, bf16[320,1536]{1,0:T(8,128)(2,1)}, u32[]{:S(2)}, u32[]{:S(2)}) collective-permute-start(bf16[320,1536]{1,0:T(8,128)(2,1)S(1)} %slice.10.refs_6_), channel_id=1, source_target_pairs={{0,16},{16,0},{32,48},{48,32},{64,80},{80,64},{96,112},{112,96},{1... | collective-permute-start | bytes 2949128 | tf_op jit(solution)/shard_map/ppermute | solution.py:428
  23.7 38.4 %collective-permute-start.8 = (bf16[320,1408]{1,0:T(8,128)(2,1)S(1)}, bf16[320,1408]{1,0:T(8,128)(2,1)}, u32[]{:S(2)}, u32[]{:S(2)}) collective-permute-start(bf16[320,1408]{1,0:T(8,128)(2,1)S(1)} %concatenate.16.refs_8_), channel_id=1, source_target_pairs={{0,16},{16,0},{32,48},{48,32},{64,80},{80,64},{96,112},{112,96},{1... | collective-permute-start | bytes 2703368 | tf_op jit(solution)/shard_map/ppermute | solution.py:428
  29.3 41.6 %collective-permute-start.15 = (bf16[320,1536]{1,0:T(8,128)(2,1)S(1)}, bf16[320,1536]{1,0:T(8,128)(2,1)}, u32[]{:S(2)}, u32[]{:S(2)}) collective-permute-start(bf16[320,1536]{1,0:T(8,128)(2,1)S(1)} %slice.10.refs_6_), channel_id=1, source_target_pairs={{32,0},{96,16},{33,1},{97,17},{34,2},{98,18},{35,3},{99,19},{36,4}... | collective-permute-start | bytes 2949128 | tf_op jit(solution)/shard_map/ppermute | solution.py:405
  47.3 38.2 %collective-permute-start.17 = (bf16[320,1408]{1,0:T(8,128)(2,1)S(1)}, bf16[320,1408]{1,0:T(8,128)(2,1)}, u32[]{:S(2)}, u32[]{:S(2)}) collective-permute-start(bf16[320,1408]{1,0:T(8,128)(2,1)S(1)} %concatenate.16.refs_8_), channel_id=1, source_target_pairs={{32,0},{96,16},{33,1},{97,17},{34,2},{98,18},{35,3},{99,19},{36,4}... | collective-permute-start | bytes 2703368 | tf_op jit(solution)/shard_map/ppermute | solution.py:405
  107.9 29.8 %collective-permute-start.32 = (bf16[320,1408]{1,0:T(8,128)(2,1)S(1)}, bf16[320,1408]{1,0:T(8,128)(2,1)S(1)}, u32[]{:S(2)}, u32[]{:S(2)}) collective-permute-start(bf16[320,1408]{1,0:T(8,128)(2,1)S(1)} %concatenate.16.refs_8_), channel_id=1, source_target_pairs={{64,0},{128,16},{65,1},{129,17},{66,2},{130,18},{67,3},{131,19},{6... | collective-permute-start | bytes 2703368 | tf_op jit(solution)/shard_map/ppermute | solution.py:405
  109.2 35.4 %collective-permute-start.29 = (bf16[3840,128]{1,0:T(8,128)(2,1)S(1)}, bf16[3840,128]{1,0:T(8,128)(2,1)S(1)}, u32[]{:S(2)}, u32[]{:S(2)}) collective-permute-start(bf16[3840,128]{1,0:T(8,128)(2,1)S(1)} %get-tuple-element.204.refs_0_.refs_13_), channel_id=1, source_target_pairs={{0,0},{1,1},{17,9},{16,8},{2,2},{3,3},{19,11},{18,10},{4,4},{5,5},... | collective-permute-start | bytes 2949128 | tf_op jit(solution)/shard_map/ppermute | solution.py:421
  123.1 30.4 %collective-permute-start.38 = (bf16[320,1536]{1,0:T(8,128)(2,1)S(1)}, bf16[320,1536]{1,0:T(8,128)(2,1)S(1)}, u32[]{:S(2)}, u32[]{:S(2)}) collective-permute-start(bf16[320,1536]{1,0:T(8,128)(2,1)S(1)} %slice.10.refs_6_), channel_id=1, source_target_pairs={{80,0},{144,16},{81,1},{145,17},{82,2},{146,18},{83,3},{147,19},{8... | collective-permute-start | bytes 2949128 | tf_op jit(solution)/shard_map/ppermute | solution.py:405
  124.4 35.1 %collective-permute-start.31 = (bf16[320,1536]{1,0:T(8,128)(2,1)}, bf16[320,1536]{1,0:T(8,128)(2,1)S(1)}, u32[]{:S(2)}, u32[]{:S(2)}) collective-permute-start(bf16[320,1536]{1,0:T(8,128)(2,1)} %collective-permute-done.30.refs_6_), channel_id=1, source_target_pairs={{0,16},{16,0},{32,48},{48,32},{64,80},{80,64},{96,112},{112,96},{1... | collective-permute-start | bytes 2949128 | tf_op jit(solution)/shard_map/ppermute | solution.py:428
  137.7 29.5 %collective-permute-start.40 = (bf16[320,1408]{1,0:T(8,128)(2,1)S(1)}, bf16[320,1408]{1,0:T(8,128)(2,1)S(1)}, u32[]{:S(2)}, u32[]{:S(2)}) collective-permute-start(bf16[320,1408]{1,0:T(8,128)(2,1)S(1)} %concatenate.16.refs_8_), channel_id=1, source_target_pairs={{80,0},{144,16},{81,1},{145,17},{82,2},{146,18},{83,3},{147,19},{8... | collective-permute-start | bytes 2703368 | tf_op jit(solution)/shard_map/ppermute | solution.py:405
  173.5 37.0 %collective-permute-start.53 = (bf16[3840,128]{1,0:T(8,128)(2,1)S(1)}, bf16[3840,128]{1,0:T(8,128)(2,1)S(1)}, u32[]{:S(2)}, u32[]{:S(2)}) collective-permute-start(bf16[3840,128]{1,0:T(8,128)(2,1)S(1)} %get-tuple-element.252.refs_0_), channel_id=1, source_target_pairs={{0,64},{1,65},{17,73},{16,72},{2,66},{3,67},{19,75},{18,74},{4,68}... | collective-permute-start | bytes 2949128 | tf_op jit(solution)/shard_map/ppermute | solution.py:421
  187.0 46.9 %collective-permute-start.57 = (bf16[3840,128]{1,0:T(8,128)(2,1)S(1)}, bf16[3840,128]{1,0:T(8,128)(2,1)S(1)}, u32[]{:S(2)}, u32[]{:S(2)}) collective-permute-start(bf16[3840,128]{1,0:T(8,128)(2,1)S(1)} %get-tuple-element.262.refs_0_), channel_id=1, source_target_pairs={{0,80},{1,81},{17,89},{16,88},{2,82},{3,83},{19,91},{18,90},{4,84}... | collective-permute-start | bytes 2949128 | tf_op jit(solution)/shard_map/ppermute | solution.py:421
  199.4 46.8 %collective-permute-start.62 = (bf16[320,1536]{1,0:T(8,128)(2,1)S(1)}, bf16[320,1536]{1,0:T(8,128)(2,1)S(1)}, u32[]{:S(2)}, u32[]{:S(2)}) collective-permute-start(bf16[320,1536]{1,0:T(8,128)(2,1)S(1)} %slice.10.refs_6_), channel_id=1, source_target_pairs={{160,0},{224,16},{161,1},{225,17},{162,2},{226,18},{163,3},{227,19... | collective-permute-start | bytes 2949128 | tf_op jit(solution)/shard_map/ppermute | solution.py:405
  209.3 38.3 %collective-permute-start.64 = (bf16[320,1408]{1,0:T(8,128)(2,1)S(1)}, bf16[320,1408]{1,0:T(8,128)(2,1)S(1)}, u32[]{:S(2)}, u32[]{:S(2)}) collective-permute-start(bf16[320,1408]{1,0:T(8,128)(2,1)S(1)} %concatenate.16.refs_8_), channel_id=1, source_target_pairs={{160,0},{224,16},{161,1},{225,17},{162,2},{226,18},{163,3},{227,19... | collective-permute-start | bytes 2703368 | tf_op jit(solution)/shard_map/ppermute | solution.py:405
  222.3 30.0 %collective-permute-start.72 = (bf16[320,1408]{1,0:T(8,128)(2,1)S(1)}, bf16[320,1408]{1,0:T(8,128)(2,1)S(1)}, u32[]{:S(2)}, u32[]{:S(2)}) collective-permute-start(bf16[320,1408]{1,0:T(8,128)(2,1)S(1)} %concatenate.16.refs_8_), channel_id=1, source_target_pairs={{176,0},{192,16},{177,1},{193,17},{178,2},{194,18},{179,3},{195,19... | collective-permute-start | bytes 2703368 | tf_op jit(solution)/shard_map/ppermute | solution.py:405
  259.1 41.2 %collective-permute-start.82 = (bf16[320,1536]{1,0:T(8,128)(2,1)S(1)}, bf16[320,1536]{1,0:T(8,128)(2,1)}, u32[]{:S(2)}, u32[]{:S(2)}) collective-permute-start(bf16[320,1536]{1,0:T(8,128)(2,1)S(1)} %slice.10.refs_6_), channel_id=1, source_target_pairs={{208,0},{240,16},{209,1},{241,17},{210,2},{242,18},{211,3},{243,19... | collective-permute-start | bytes 2949128 | tf_op jit(solution)/shard_map/ppermute | solution.py:405
  273.4 29.6 %collective-permute-start.84 = (bf16[320,1408]{1,0:T(8,128)(2,1)S(1)}, bf16[320,1408]{1,0:T(8,128)(2,1)}, u32[]{:S(2)}, u32[]{:S(2)}) collective-permute-start(bf16[320,1408]{1,0:T(8,128)(2,1)S(1)} %concatenate.16.refs_8_), channel_id=1, source_target_pairs={{208,0},{240,16},{209,1},{241,17},{210,2},{242,18},{211,3},{243,19... | collective-permute-start | bytes 2703368 | tf_op jit(solution)/shard_map/ppermute | solution.py:405
  277.6 31.2 %collective-permute-start.77 = (bf16[3840,128]{1,0:T(8,128)(2,1)}, bf16[3840,128]{1,0:T(8,128)(2,1)}, u32[]{:S(2)}, u32[]{:S(2)}) collective-permute-start(bf16[3840,128]{1,0:T(8,128)(2,1)} %get-tuple-element.300.refs_0_), channel_id=1, source_target_pairs={{0,0},{1,1},{17,9},{16,8},{2,2},{3,3},{19,11},{18,10},{4,4},{5,5},... | collective-permute-start | bytes 2949128 | tf_op jit(solution)/shard_map/ppermute | solution.py:421
  280.4 38.1 %collective-permute-start.81 = (bf16[3840,128]{1,0:T(8,128)(2,1)}, bf16[3840,128]{1,0:T(8,128)(2,1)}, u32[]{:S(2)}, u32[]{:S(2)}) collective-permute-start(bf16[3840,128]{1,0:T(8,128)(2,1)} %get-tuple-element.310.refs_0_), channel_id=1, source_target_pairs={{0,16},{1,17},{17,25},{16,24},{2,18},{3,19},{19,27},{18,26},{4,20}... | collective-permute-start | bytes 2949128 | tf_op jit(solution)/shard_map/ppermute | solution.py:421
  307.5 31.6 %collective-permute-start.89 = (bf16[3840,128]{1,0:T(8,128)(2,1)}, bf16[3840,128]{1,0:T(8,128)(2,1)S(1)}, u32[]{:S(2)}, u32[]{:S(2)}) collective-permute-start(bf16[3840,128]{1,0:T(8,128)(2,1)} %get-tuple-element.325.refs_0_), channel_id=1, source_target_pairs={{0,32},{1,33},{17,41},{16,40},{2,34},{3,35},{19,43},{18,42},{4,36}... | collective-permute-start | bytes 2949128 | tf_op jit(solution)/shard_map/ppermute | solution.py:421
  308.8 45.9 %collective-permute-start.93 = (bf16[3840,128]{1,0:T(8,128)(2,1)S(1)}, bf16[3840,128]{1,0:T(8,128)(2,1)S(1)}, u32[]{:S(2)}, u32[]{:S(2)}) collective-permute-start(bf16[3840,128]{1,0:T(8,128)(2,1)S(1)} %get-tuple-element.335), channel_id=1, source_target_pairs={{0,48},{1,49},{17,57},{16,56},{2,50},{3,51},{19,59},{18,58},{4,52}... | collective-permute-start | bytes 2949128 | tf_op jit(solution)/shard_map/ppermute | solution.py:421
  356.9 29.8 %collective-permute-start.96 = (bf16[3840,128]{1,0:T(8,128)(2,1)}, bf16[3840,128]{1,0:T(8,128)(2,1)}, u32[]{:S(2)}, u32[]{:S(2)}) collective-permute-start(bf16[3840,128]{1,0:T(8,128)(2,1)} %get-tuple-element.342), channel_id=1, source_target_pairs={{0,96},{1,97},{17,105},{16,104},{2,98},{3,99},{19,107},{18,106},{4... | collective-permute-start | bytes 2949128 | tf_op jit(solution)/shard_map/ppermute | solution.py:421
  365.5 31.7 %collective-permute-start.97 = (bf16[3840,128]{1,0:T(8,128)(2,1)S(1)}, bf16[3840,128]{1,0:T(8,128)(2,1)S(1)}, u32[]{:S(2)}, u32[]{:S(2)}) collective-permute-start(bf16[3840,128]{1,0:T(8,128)(2,1)S(1)} %res_block.31), channel_id=1, source_target_pairs={{0,112},{1,113},{17,121},{16,120},{2,114},{3,115},{19,123},{18,122... | collective-permute-start | bytes 2949128 | tf_op jit(solution)/shard_map/ppermute | solution.py:421
  401.3 96.7 %all-to-all-start = ((bf16[16,960,128]{2,1,0:T(8,128)(2,1)}), bf16[16,960,128]{2,1,0:T(8,128)(2,1)}, u32[]{:S(2)}, u32[]{:S(2)}) async-start(bf16[16,960,128]{2,1,0:T(8,128)(2,1)} %bitcast.33), calls=%async_computation | async-start | bytes 7864320 | tf_op jit(solution)/shard_map/all_to_all | solution.py:478
  (131 other events, 1377.2 us)
Sparse Core Ops, SparseCore 0:
  99.7 49.0 all-gather.2

commit v8 on v7

--- a/solution.py
+++ b/solution.py
@@ -31,6 +31,8 @@
 FETCH_AFTER |= {(5, 0): 5, (5, 1): 6, (6, 0): 7, (6, 1): 8, (7, 0): 9, (7, 1): 10}
 SWAP_AFTER = {(1, 0): 0, (1, 1): 1, (2, 0): 1, (2, 1): 2, (3, 0): 2, (3, 1): 3, (4, 0): 3, (4, 1): 4}
 SWAP_AFTER |= {(5, 0): 6, (5, 1): 7, (6, 0): 8, (6, 1): 9, (7, 0): 10, (7, 1): 11}
+
+DONE_BY = {14: [11, 12], 15: [13]}
 
 
 def place(slot, quarter):
@@ -430,9 +432,10 @@
             weights[block], cores[block] = weights.get(block, []) + both, at
 
     for own in lead:
+        own, _ = lax.optimization_barrier((own, pieces))
         swap_cores(0, own)
     *exchanged, source = first_call(info, pieces)
-    fetched[1, 0] = fetch(1, 0, pieces[0])
+    fetched[1, 0] = fetch(1, 0, pieces)
     fetched[1, 1] = fetch(1, 1, source)
     wholes, edges_of, passing = [], {}, []
     for block in range(BLOCKS):
@@ -443,10 +446,11 @@
         if block >= 1:
             sent, _ = lax.optimization_barrier((wholes[-1], (near_in, cross_in, far)))
             passing.append(hand_over(block - 1, sent))
-        if block >= 4:
-            source, near_in, cross_in, far, passing[block - 4] = lax.optimization_barrier(
-                (source, near_in, cross_in, far, passing[block - 4])
-            )
+        for arrived in DONE_BY.get(block, [block - 3]):
+            if arrived >= 0:
+                source, near_in, cross_in, far, passing[arrived] = lax.optimization_barrier(
+                    (source, near_in, cross_in, far, passing[arrived])
+                )
         whole, exchanged, summed = block_call(
             block,
             cores[block],

time: 519 us -> 521 us (level)
  the two profiles are of different devices: /device:TPU:4 before, /device:TPU:34 now
where the time goes in v8:
time: 521 us; the launch traced here: 511 us
  waiting for transfers between devices  202 us (39%)
  starting transfers between devices  192 us (37%)
  Pallas kernels  74.1 us (14%)
  local copies, waits for them, and re-layouts  23.5 us (5%)
  between operations  17.2 us (3%)
    all_to_all x1, waiting for transfers between devices, on_device(): lax.all_to_all(held.reshape(2 * MICRO, PIECE, WIDTH), BOTH, 0, 0, axis_in...  89.1 us
    pallas_call x16, Pallas kernels, block_call(): pl.pallas_call(functools.partial(block_body, block, at_core, up_in, up_ou...  70.3 us
    all_to_all x1, starting transfers between devices, on_device(): lax.all_to_all(held.reshape(2 * MICRO, PIECE, WIDTH), BOTH, 0, 0, axis_in...  62.3 us
    ppermute x14, starting transfers between devices, fetch(): return lax.ppermute(own, 'segment', [(first, 0), (second, 1)])  58.9 us
    ppermute x16, waiting for transfers between devices, exchange(): lax.ppermute(stats, BOTH, both)  31 us
    ppermute x16, waiting for transfers between devices, exchange(): lax.ppermute(near, 'tile', other_tile)  29.2 us
    ppermute x16, waiting for transfers between devices, hand_over(): return lax.ppermute(whole, BOTH, route)  25.6 us
    ppermute x16, starting transfers between devices, exchange(): lax.ppermute(stats, BOTH, both)  21.8 us
  transfers between devices with their start and end apart: 100, of which 38 were waited for; matrix products, arithmetic and copies ran while one was open for 2% of the time, Pallas kernels for 14%

profile of v8, /device:TPU:34, one launch (start us, length us, event | category | flops | bytes accessed | tf_op | source)
XLA Modules:
  0.0 510.8 jit_solution(10647064406780827463)
XLA Ops:
  24.8 3.1 collective-permute-done.6.refs_4_
  28.0 4.6 collective-permute-done.4.refs_1_
  40.4 9.4 %res_block.17 = (bf16[3840,128]{1,0:T(8,128)(2,1)}, bf16[368,128]{1,0:T(8,128)(2,1)S(1)}, bf16[368,128]{1,0:T(8,128)(2,1)S(1)}, bf16[48,128]{1,0:T(8,128)(2,1)S(1)}) custom-call(s32[3]{0:T(128)S(1)} %pad_add_fusion.info, bf16[3840,128]{1,0:T(8,128)(2,1)S(1)} %get-tuple-element.208.refs_0_.refs_13_, ...), custom_call_target="tpu_custom_call" | custom-call | flops 353894400 | bytes 1048576 | tf_op jit(solution)/shard_map/res_block/pallas_call | solution.py:309
  55.3 4.4 collective-permute-done.12.refs_1_.refs_11_
  63.3 38.9 %collective-permute-start.31 = (bf16[320,1536]{1,0:T(8,128)(2,1)S(1)}, bf16[320,1536]{1,0:T(8,128)(2,1)}, u32[]{:S(2)}, u32[]{:S(2)}) collective-permute-start(bf16[320,1536]{1,0:T(8,128)(2,1)S(1)} %slice.10.refs_6_), channel_id=1, source_target_pairs={{64,0},{128,16},{65,1},{129,17},{66,2},{130,18},{67,3},{131,19},{6... | collective-permute-start | bytes 2949128 | tf_op jit(solution)/shard_map/ppermute | solution.py:407
  109.1 6.1 %collective-permute-start.33 = (bf16[320,1408]{1,0:T(8,128)(2,1)S(1)}, bf16[320,1408]{1,0:T(8,128)(2,1)S(1)}, u32[]{:S(2)}, u32[]{:S(2)}) collective-permute-start(bf16[320,1408]{1,0:T(8,128)(2,1)S(1)} %concatenate.16.refs_8_), channel_id=1, source_target_pairs={{64,0},{128,16},{65,1},{129,17},{66,2},{130,18},{67,3},{131,19},{6... | collective-permute-start | bytes 2703368 | tf_op jit(solution)/shard_map/ppermute | solution.py:407
  123.0 8.4 %res_block.19 = (bf16[3840,128]{1,0:T(8,128)(2,1)S(1)}, bf16[368,128]{1,0:T(8,128)(2,1)S(1)}, bf16[368,128]{1,0:T(8,128)(2,1)S(1)}, bf16[48,128]{1,0:T(8,128)(2,1)S(1)}) custom-call(s32[3]{0:T(128)S(1)} %pad_add_fusion.info, bf16[3840,128]{1,0:T(8,128)(2,1)S(1)} %get-tuple-element.236.refs_0_.refs_13_, ...), custom_call_target="tpu_custom_call" | custom-call | flops 353894400 | bytes 1048576 | tf_op jit(solution)/shard_map/res_block/pallas_call | solution.py:309
  131.4 17.2 %collective-permute-done.33.refs_8_ = bf16[320,1408]{1,0:T(8,128)(2,1)S(1)} collective-permute-done((bf16[320,1408]{1,0:T(8,128)(2,1)S(1)}, bf16[320,1408]{1,0:T(8,128)(2,1)S(1)}, u32[]{:S(2)}, u32[]{:S(2)}) %collective-permute-start.33) | collective-permute-done | bytes 901152 | tf_op jit(solution)/shard_map/ppermute | solution.py:407
  149.4 5.7 %collective-permute-start.29 = (bf16[48,128]{1,0:T(8,128)(2,1)S(1)}, bf16[48,128]{1,0:T(8,128)(2,1)S(1)}, u32[]{:S(2)}, u32[]{:S(2)}) collective-permute-start(bf16[48,128]{1,0:T(8,128)(2,1)S(1)} %get-tuple-element.221.refs_3_), channel_id=1, source_target_pairs={{0,17},{1,16},{2,19},{3,18},{4,21},{5,20},{6,23},{7,22},{8,25},{9,... | collective-permute-start | bytes 36872 | tf_op jit(solution)/shard_map/ppermute | solution.py:418
  161.2 3.5 collective-permute-start.42
  169.4 3.9 collective-permute-done.35.refs_1_
  175.4 7.0 %res_block.21 = (bf16[3840,128]{1,0:T(8,128)(2,1)S(1)}, bf16[368,128]{1,0:T(8,128)(2,1)S(1)}, bf16[368,128]{1,0:T(8,128)(2,1)S(1)}, bf16[48,128]{1,0:T(8,128)(2,1)S(1)}) custom-call(s32[3]{0:T(128)S(1)} %pad_add_fusion.info, bf16[3840,128]{1,0:T(8,128)(2,1)S(1)} %get-tuple-element.260.refs_0_, bf16[368,128]{1,0:T(8,128)(2,1)S(1)} %collective-permute-done.35.refs_1_, ...), custom_call_target="tpu_custom_call" | custom-call | flops 353894400 | bytes 1048576 | tf_op jit(solution)/shard_map/res_block/pallas_call | solution.py:309
  195.1 7.8 %res_block.23 = (bf16[3840,128]{1,0:T(8,128)(2,1)S(1)}, bf16[368,128]{1,0:T(8,128)(2,1)S(1)}, bf16[368,128]{1,0:T(8,128)(2,1)S(1)}, bf16[48,128]{1,0:T(8,128)(2,1)S(1)}) custom-call(s32[3]{0:T(128)S(1)} %pad_add_fusion.info, bf16[3840,128]{1,0:T(8,128)(2,1)S(1)} %get-tuple-element.280.refs_0_, bf16[368,128]{1,0:T(8,128)(2,1)S(1)} %collective-permute-done.47.refs_1_, ...), custom_call_target="tpu_custom_call" | custom-call | flops 353894400 | bytes 1048576 | tf_op jit(solution)/shard_map/res_block/pallas_call | solution.py:309
  207.3 4.0 collective-permute-done.51.refs_1_
  223.2 9.2 %res_block.25 = (bf16[3840,128]{1,0:T(8,128)(2,1)}, bf16[368,128]{1,0:T(8,128)(2,1)S(1)}, bf16[368,128]{1,0:T(8,128)(2,1)S(1)}, bf16[48,128]{1,0:T(8,128)(2,1)S(1)}) custom-call(s32[3]{0:T(128)S(1)} %pad_add_fusion.info, bf16[3840,128]{1,0:T(8,128)(2,1)S(1)} %get-tuple-element.304.refs_0_, bf16[368,128]{1,0:T(8,128)(2,1)S(1)} %collective-permute-done.55.refs_1_, ...), custom_call_target="tpu_custom_call" | custom-call | flops 353894400 | bytes 1048576 | tf_op jit(solution)/shard_map/res_block/pallas_call | solution.py:309
  236.7 3.8 collective-permute-done.59.refs_1_
  257.7 25.6 %collective-permute-done.70.refs_8_ = bf16[3840,128]{1,0:T(8,128)(2,1)S(1)} collective-permute-done((bf16[3840,128]{1,0:T(8,128)(2,1)S(1)}, bf16[3840,128]{1,0:T(8,128)(2,1)S(1)}, u32[]{:S(2)}, u32[]{:S(2)}) %collective-permute-start.70) | collective-permute-done | bytes 983072 | tf_op jit(solution)/shard_map/ppermute | solution.py:423
  293.4 8.6 %res_block.27 = (bf16[3840,128]{1,0:T(8,128)(2,1)S(1)}, bf16[368,128]{1,0:T(8,128)(2,1)S(1)}, bf16[368,128]{1,0:T(8,128)(2,1)S(1)}, bf16[48,128]{1,0:T(8,128)(2,1)S(1)}, f32[3840,128]{1,0:T(8,128)S(1)}) custom-call(s32[3]{0:T(128)S(1)} %pad_add_fusion.info, bf16[3840,128]{1,0:T(8,128)(2,1)} %get-tuple-element.328.refs_0_, bf16[368,128]{1,0:T(8,128)(2,1)S(1)} %copy-done.33, ...), custom_call_target="tpu_custom_call" | custom-call | flops 353894400 | bytes 1048576 | tf_op jit(solution)/shard_map/res_block/pallas_call | solution.py:309
  319.0 8.1 %res_block.29 = (bf16[3840,128]{1,0:T(8,128)(2,1)S(1)}, bf16[368,128]{1,0:T(8,128)(2,1)S(1)}, bf16[368,128]{1,0:T(8,128)(2,1)S(1)}, bf16[48,128]{1,0:T(8,128)(2,1)S(1)}, f32[3840,128]{1,0:T(8,128)S(1)}) custom-call(s32[3]{0:T(128)S(1)} %pad_add_fusion.info, f32[3840,128]{1,0:T(8,128)S(1)} %get-tuple-element.330.refs_0_, ...), custom_call_target="tpu_custom_call" | custom-call | flops 353894400 | bytes 1048576 | tf_op jit(solution)/shard_map/res_block/pallas_call | solution.py:309
  340.9 3.2 res_block.31
  345.8 3.2 pick.1
  349.0 62.3 %all-to-all-start = ((bf16[16,960,128]{2,1,0:T(8,128)(2,1)}), bf16[16,960,128]{2,1,0:T(8,128)(2,1)}, u32[]{:S(2)}, u32[]{:S(2)}) async-start(bf16[16,960,128]{2,1,0:T(8,128)(2,1)} %bitcast.33), calls=%async_computation | async-start | bytes 7864320 | tf_op jit(solution)/shard_map/all_to_all | solution.py:482
  411.3 89.1 %all-to-all-done = bf16[16,960,128]{2,1,0:T(8,128)(2,1)} async-done(((bf16[16,960,128]{2,1,0:T(8,128)(2,1)}), bf16[16,960,128]{2,1,0:T(8,128)(2,1)}, u32[]{:S(2)}, u32[]{:S(2)}) %all-to-all-start) | async-done | bytes 3932192 | tf_op jit(solution)/shard_map/all_to_all | solution.py:482
  500.3 3.1 constant_dynamic-slice_fusion
  (320 shorter events, 153.5 us)
Async XLA Ops:
  6.5 279.3 %all-gather.3.cloned.1.call-start = ((), (), s32[]{:S(2)}) async-start(), calls=%async_computation.1 | async-start | bytes 4177920 | tf_op jit(solution)/shard_map/all_gather | solution.py:398
  23.2 26.6 %collective-permute-start.17 = (bf16[320,1408]{1,0:T(8,128)(2,1)S(1)}, bf16[320,1408]{1,0:T(8,128)(2,1)}, u32[]{:S(2)}, u32[]{:S(2)}) collective-permute-start(bf16[320,1408]{1,0:T(8,128)(2,1)S(1)} %concatenate.16.refs_8_), channel_id=1, source_target_pairs={{32,0},{96,16},{33,1},{97,17},{34,2},{98,18},{35,3},{99,19},{36,4}... | collective-permute-start | bytes 2703368 | tf_op jit(solution)/shard_map/ppermute | solution.py:407
  34.5 27.8 %collective-permute-start.23 = (bf16[320,1536]{1,0:T(8,128)(2,1)S(1)}, bf16[320,1536]{1,0:T(8,128)(2,1)S(1)}, u32[]{:S(2)}, u32[]{:S(2)}) collective-permute-start(bf16[320,1536]{1,0:T(8,128)(2,1)S(1)} %slice.10.refs_6_), channel_id=1, source_target_pairs={{48,0},{112,16},{49,1},{113,17},{50,2},{114,18},{51,3},{115,19},{5... | collective-permute-start | bytes 2949128 | tf_op jit(solution)/shard_map/ppermute | solution.py:407
  39.6 64.5 %collective-permute-start.16 = (bf16[320,1536]{1,0:T(8,128)(2,1)}, bf16[320,1536]{1,0:T(8,128)(2,1)}, u32[]{:S(2)}, u32[]{:S(2)}) collective-permute-start(bf16[320,1536]{1,0:T(8,128)(2,1)} %collective-permute-done.15.refs_6_), channel_id=1, source_target_pairs={{0,16},{16,0},{32,48},{48,32},{64,80},{80,64},{96,112},{112,96},{1... | collective-permute-start | bytes 2949128 | tf_op jit(solution)/shard_map/ppermute | solution.py:430
  49.8 54.3 %collective-permute-start.18 = (bf16[320,1408]{1,0:T(8,128)(2,1)}, bf16[320,1408]{1,0:T(8,128)(2,1)}, u32[]{:S(2)}, u32[]{:S(2)}) collective-permute-start(bf16[320,1408]{1,0:T(8,128)(2,1)} %collective-permute-done.17.refs_8_), channel_id=1, source_target_pairs={{0,16},{16,0},{32,48},{48,32},{64,80},{80,64},{96,112},{112,96},{1... | collective-permute-start | bytes 2703368 | tf_op jit(solution)/shard_map/ppermute | solution.py:430
  49.9 55.6 %collective-permute-start.25 = (bf16[320,1408]{1,0:T(8,128)(2,1)S(1)}, bf16[320,1408]{1,0:T(8,128)(2,1)}, u32[]{:S(2)}, u32[]{:S(2)}) collective-permute-start(bf16[320,1408]{1,0:T(8,128)(2,1)S(1)} %concatenate.16.refs_8_), channel_id=1, source_target_pairs={{48,0},{112,16},{49,1},{113,17},{50,2},{114,18},{51,3},{115,19},{5... | collective-permute-start | bytes 2703368 | tf_op jit(solution)/shard_map/ppermute | solution.py:407
  61.0 54.2 %collective-permute-start.22 = (bf16[3840,128]{1,0:T(8,128)(2,1)S(1)}, bf16[3840,128]{1,0:T(8,128)(2,1)}, u32[]{:S(2)}, u32[]{:S(2)}) collective-permute-start(bf16[3840,128]{1,0:T(8,128)(2,1)S(1)} %get-tuple-element.208.refs_0_.refs_13_), channel_id=1, source_target_pairs={{0,0},{1,1},{17,9},{16,8},{2,2},{3,3},{19,11},{18,10},{4,4},{5,5},... | collective-permute-start | bytes 2949128 | tf_op jit(solution)/shard_map/ppermute | solution.py:423
  63.3 53.8 %collective-permute-start.31 = (bf16[320,1536]{1,0:T(8,128)(2,1)S(1)}, bf16[320,1536]{1,0:T(8,128)(2,1)}, u32[]{:S(2)}, u32[]{:S(2)}) collective-permute-start(bf16[320,1536]{1,0:T(8,128)(2,1)S(1)} %slice.10.refs_6_), channel_id=1, source_target_pairs={{64,0},{128,16},{65,1},{129,17},{66,2},{130,18},{67,3},{131,19},{6... | collective-permute-start | bytes 2949128 | tf_op jit(solution)/shard_map/ppermute | solution.py:407
  109.1 39.5 %collective-permute-start.33 = (bf16[320,1408]{1,0:T(8,128)(2,1)S(1)}, bf16[320,1408]{1,0:T(8,128)(2,1)S(1)}, u32[]{:S(2)}, u32[]{:S(2)}) collective-permute-start(bf16[320,1408]{1,0:T(8,128)(2,1)S(1)} %concatenate.16.refs_8_), channel_id=1, source_target_pairs={{64,0},{128,16},{65,1},{129,17},{66,2},{130,18},{67,3},{131,19},{6... | collective-permute-start | bytes 2703368 | tf_op jit(solution)/shard_map/ppermute | solution.py:407
  119.9 29.4 %collective-permute-start.30 = (bf16[3840,128]{1,0:T(8,128)(2,1)}, bf16[3840,128]{1,0:T(8,128)(2,1)S(1)}, u32[]{:S(2)}, u32[]{:S(2)}) collective-permute-start(bf16[3840,128]{1,0:T(8,128)(2,1)} %get-tuple-element.222.refs_0_.refs_13_), channel_id=1, source_target_pairs={{0,16},{1,17},{17,25},{16,24},{2,18},{3,19},{19,27},{18,26},{4,20}... | collective-permute-start | bytes 2949128 | tf_op jit(solution)/shard_map/ppermute | solution.py:423
  120.7 34.4 %collective-permute-start.39 = (bf16[320,1536]{1,0:T(8,128)(2,1)S(1)}, bf16[320,1536]{1,0:T(8,128)(2,1)S(1)}, u32[]{:S(2)}, u32[]{:S(2)}) collective-permute-start(bf16[320,1536]{1,0:T(8,128)(2,1)S(1)} %slice.10.refs_6_), channel_id=1, source_target_pairs={{80,0},{144,16},{81,1},{145,17},{82,2},{146,18},{83,3},{147,19},{8... | collective-permute-start | bytes 2949128 | tf_op jit(solution)/shard_map/ppermute | solution.py:407
  121.4 39.1 %collective-permute-start.32 = (bf16[320,1536]{1,0:T(8,128)(2,1)}, bf16[320,1536]{1,0:T(8,128)(2,1)S(1)}, u32[]{:S(2)}, u32[]{:S(2)}) collective-permute-start(bf16[320,1536]{1,0:T(8,128)(2,1)} %collective-permute-done.31.refs_6_), channel_id=1, source_target_pairs={{0,16},{16,0},{32,48},{48,32},{64,80},{80,64},{96,112},{112,96},{1... | collective-permute-start | bytes 2949128 | tf_op jit(solution)/shard_map/ppermute | solution.py:430
  193.7 25.6 %collective-permute-start.58 = (bf16[3840,128]{1,0:T(8,128)(2,1)S(1)}, bf16[3840,128]{1,0:T(8,128)(2,1)S(1)}, u32[]{:S(2)}, u32[]{:S(2)}) collective-permute-start(bf16[3840,128]{1,0:T(8,128)(2,1)S(1)} %get-tuple-element.280.refs_0_), channel_id=1, source_target_pairs={{0,96},{1,97},{17,105},{16,104},{2,98},{3,99},{19,107},{18,106},{4... | collective-permute-start | bytes 2949128 | tf_op jit(solution)/shard_map/ppermute | solution.py:423
  215.8 27.7 %collective-permute-start.62 = (bf16[3840,128]{1,0:T(8,128)(2,1)S(1)}, bf16[3840,128]{1,0:T(8,128)(2,1)S(1)}, u32[]{:S(2)}, u32[]{:S(2)}) collective-permute-start(bf16[3840,128]{1,0:T(8,128)(2,1)S(1)} %get-tuple-element.290.refs_0_), channel_id=1, source_target_pairs={{0,112},{1,113},{17,121},{16,120},{2,114},{3,115},{19,123},{18,122... | collective-permute-start | bytes 2949128 | tf_op jit(solution)/shard_map/ppermute | solution.py:423
  218.6 26.3 %collective-permute-start.64 = (bf16[320,1536]{1,0:T(8,128)(2,1)S(1)}, bf16[320,1536]{1,0:T(8,128)(2,1)S(1)}, u32[]{:S(2)}, u32[]{:S(2)}) collective-permute-start(bf16[320,1536]{1,0:T(8,128)(2,1)S(1)} %collective-permute-done.63.refs_6_), channel_id=1, source_target_pairs={{0,16},{16,0},{32,48},{48,32},{64,80},{80,64},{96,112},{112,96},{1... | collective-permute-start | bytes 2949128 | tf_op jit(solution)/shard_map/ppermute | solution.py:430
  221.6 27.4 %collective-permute-start.73 = (bf16[320,1408]{1,0:T(8,128)(2,1)S(1)}, bf16[320,1408]{1,0:T(8,128)(2,1)}, u32[]{:S(2)}, u32[]{:S(2)}) collective-permute-start(bf16[320,1408]{1,0:T(8,128)(2,1)S(1)} %concatenate.16.refs_8_), channel_id=1, source_target_pairs={{176,0},{192,16},{177,1},{193,17},{178,2},{194,18},{179,3},{195,19... | collective-permute-start | bytes 2703368 | tf_op jit(solution)/shard_map/ppermute | solution.py:407
  243.5 39.8 %collective-permute-start.70 = (bf16[3840,128]{1,0:T(8,128)(2,1)S(1)}, bf16[3840,128]{1,0:T(8,128)(2,1)S(1)}, u32[]{:S(2)}, u32[]{:S(2)}) collective-permute-start(bf16[3840,128]{1,0:T(8,128)(2,1)S(1)} %get-tuple-element.304.refs_0_), channel_id=1, source_target_pairs={{0,0},{1,1},{17,9},{16,8},{2,2},{3,3},{19,11},{18,10},{4,4},{5,5},... | collective-permute-start | bytes 2949128 | tf_op jit(solution)/shard_map/ppermute | solution.py:423
  244.8 40.1 %collective-permute-start.72 = (bf16[320,1536]{1,0:T(8,128)(2,1)S(1)}, bf16[320,1536]{1,0:T(8,128)(2,1)S(1)}, u32[]{:S(2)}, u32[]{:S(2)}) collective-permute-start(bf16[320,1536]{1,0:T(8,128)(2,1)S(1)} %collective-permute-done.71.refs_6_), channel_id=1, source_target_pairs={{0,16},{16,0},{32,48},{48,32},{64,80},{80,64},{96,112},{112,96},{1... | collective-permute-start | bytes 2949128 | tf_op jit(solution)/shard_map/ppermute | solution.py:430
  253.6 32.3 %collective-permute-start.74 = (bf16[320,1408]{1,0:T(8,128)(2,1)}, bf16[320,1408]{1,0:T(8,128)(2,1)}, u32[]{:S(2)}, u32[]{:S(2)}) collective-permute-start(bf16[320,1408]{1,0:T(8,128)(2,1)} %collective-permute-done.73.refs_8_), channel_id=1, source_target_pairs={{0,16},{16,0},{32,48},{48,32},{64,80},{80,64},{96,112},{112,96},{1... | collective-permute-start | bytes 2703368 | tf_op jit(solution)/shard_map/ppermute | solution.py:430
  254.5 47.5 %collective-permute-start.85 = (bf16[320,1408]{1,0:T(8,128)(2,1)S(1)}, bf16[320,1408]{1,0:T(8,128)(2,1)}, u32[]{:S(2)}, u32[]{:S(2)}) collective-permute-start(bf16[320,1408]{1,0:T(8,128)(2,1)S(1)} %concatenate.16.refs_8_), channel_id=1, source_target_pairs={{208,0},{240,16},{209,1},{241,17},{210,2},{242,18},{211,3},{243,19... | collective-permute-start | bytes 2703368 | tf_op jit(solution)/shard_map/ppermute | solution.py:407
  256.1 47.3 %collective-permute-start.78 = (bf16[3840,128]{1,0:T(8,128)(2,1)}, bf16[3840,128]{1,0:T(8,128)(2,1)}, u32[]{:S(2)}, u32[]{:S(2)}) collective-permute-start(bf16[3840,128]{1,0:T(8,128)(2,1)} %get-tuple-element.318.refs_0_), channel_id=1, source_target_pairs={{0,16},{1,17},{17,25},{16,24},{2,18},{3,19},{19,27},{18,26},{4,20}... | collective-permute-start | bytes 2949128 | tf_op jit(solution)/shard_map/ppermute | solution.py:423
  283.3 35.7 %collective-permute-start.82 = (bf16[3840,128]{1,0:T(8,128)(2,1)}, bf16[3840,128]{1,0:T(8,128)(2,1)}, u32[]{:S(2)}, u32[]{:S(2)}) collective-permute-start(bf16[3840,128]{1,0:T(8,128)(2,1)} %get-tuple-element.328.refs_0_), channel_id=1, source_target_pairs={{0,32},{1,33},{17,41},{16,40},{2,34},{3,35},{19,43},{18,42},{4,36}... | collective-permute-start | bytes 2949128 | tf_op jit(solution)/shard_map/ppermute | solution.py:423
  285.9 33.1 %collective-permute-start.84 = (bf16[320,1536]{1,0:T(8,128)(2,1)}, bf16[320,1536]{1,0:T(8,128)(2,1)}, u32[]{:S(2)}, u32[]{:S(2)}) collective-permute-start(bf16[320,1536]{1,0:T(8,128)(2,1)} %collective-permute-done.83.refs_6_), channel_id=1, source_target_pairs={{0,16},{16,0},{32,48},{48,32},{64,80},{80,64},{96,112},{112,96},{1... | collective-permute-start | bytes 2949128 | tf_op jit(solution)/shard_map/ppermute | solution.py:430
  349.0 151.3 %all-to-all-start = ((bf16[16,960,128]{2,1,0:T(8,128)(2,1)}), bf16[16,960,128]{2,1,0:T(8,128)(2,1)}, u32[]{:S(2)}, u32[]{:S(2)}) async-start(bf16[16,960,128]{2,1,0:T(8,128)(2,1)} %bitcast.33), calls=%async_computation | async-start | bytes 7864320 | tf_op jit(solution)/shard_map/all_to_all | solution.py:482
  (127 other events, 1056.0 us)
Sparse Core Ops, SparseCore 0:
  104.1 42.3 all-gather.2

commit v9 on v8

--- a/solution.py
+++ b/solution.py
@@ -14,6 +14,7 @@
 TAPS = 9 * CH
 ROWS = 12
 PIECE = 3 * CH
+PART = PIECE // 2
 OWN = ROWS * CH
 MEMBERS = float(48 * WIDTH * GROUP)
 MIB = 1024 * 1024
@@ -322,42 +323,80 @@
 
 
 def pick_body(info, *refs):
-    wholes, out, held, in_sem, out_sem = refs[:BLOCKS], *refs[BLOCKS:]
+    wholes, (kept, sent, held, in_sem, out_sem) = refs[:8], refs[8:]
     for at in range(8):
 
         @pl.when(info[0] == at)
         def _():
-            arrivals = [
-                pltpu.make_async_copy(wholes[at + 8 * n], held.at[n], in_sem.at[n])
-                for n in range(2)
-            ]
-            leaves = [
-                pltpu.make_async_copy(held.at[n // 2], out.at[n], out_sem.at[n]) for n in range(4)
-            ]
-            for arrive in arrivals:
-                arrive.start()
-            for n, leave in enumerate(leaves):
-                if n % 2 == 0:
-                    arrivals[n // 2].wait()
-                leave.start()
-            for leave in leaves:
-                leave.wait()
+            arrive = pltpu.make_async_copy(wholes[at], held, in_sem.at[0])
+            arrive.start()
+            arrive.wait()
+
+    leaves = []
+    for chunk in range(4):
+        for n, out in enumerate((kept, sent)):
+            half = info[1] if n == 0 else 1 - info[1]
+            rows = pl.ds(pl.multiple_of(chunk * PIECE + half * PART, PART), PART)
+            leaves.append(
+                pltpu.make_async_copy(held.at[rows], out.at[chunk], out_sem.at[2 * chunk + n])
+            )
+    for leave in leaves:
+        leave.start()
+    for leave in leaves:
+        leave.wait()
 
 
 def pick(info, wholes):
     return pl.pallas_call(
         pick_body,
-        out_shape=jax.ShapeDtypeStruct((4, OWN, WIDTH), BF),
-        in_specs=[SM] + [ANY] * BLOCKS,
-        out_specs=ANY,
+        out_shape=[jax.ShapeDtypeStruct((4, PART, WIDTH), BF)] * 2,
+        in_specs=[SM] + [ANY] * 8,
+        out_specs=[ANY] * 2,
         scratch_shapes=[
-            pltpu.VMEM((2, OWN, WIDTH), BF),
-            pltpu.SemaphoreType.DMA((2,)),
-            pltpu.SemaphoreType.DMA((4,)),
+            pltpu.VMEM((OWN, WIDTH), BF),
+            pltpu.SemaphoreType.DMA((1,)),
+            pltpu.SemaphoreType.DMA((8,)),
         ],
         compiler_params=pltpu.CompilerParams(vmem_limit_bytes=56 * MIB),
         name="pick",
     )(info, *wholes)
+
+
+def join_body(info, *refs):
+    parts, (out, held, in_sem, out_sem) = refs[:4], refs[4:]
+    copies = []
+    for n, part in enumerate(parts):
+        first = info[0] if n % 2 == 0 else 1 - info[0]
+        rows = pl.ds(n // 2 * 8 + 4 * (1 - first), 4)
+        copies.append(
+            (
+                pltpu.make_async_copy(part, held.at[n], in_sem.at[n]),
+                pltpu.make_async_copy(held.at[n], out.at[rows], out_sem.at[n]),
+            )
+        )
+    for arrive, _ in copies:
+        arrive.start()
+    for arrive, leave in copies:
+        arrive.wait()
+        leave.start()
+    for _, leave in copies:
+        leave.wait()
+
+
+def join(info, parts):
+    return pl.pallas_call(
+        join_body,
+        out_shape=jax.ShapeDtypeStruct((16, PART, WIDTH), BF),
+        in_specs=[SM] + [ANY] * 4,
+        out_specs=ANY,
+        scratch_shapes=[
+            pltpu.VMEM((4, 4, PART, WIDTH), BF),
+            pltpu.SemaphoreType.DMA((4,)),
+            pltpu.SemaphoreType.DMA((4,)),
+        ],
+        compiler_params=pltpu.CompilerParams(vmem_limit_bytes=56 * MIB),
+        name="join",
+    )(info, *parts)
 
 
 def sinusoid(steps, half_width):
@@ -437,6 +476,12 @@
     *exchanged, source = first_call(info, pieces)
     fetched[1, 0] = fetch(1, 0, pieces)
     fetched[1, 1] = fetch(1, 1, source)
+    which = jnp.stack([segment % 8, odd]).astype(jnp.int32)
+
+    def halves_of(outputs):
+        kept, sent = pick(which, outputs)
+        return kept, lax.ppermute(sent, "tile", [(t, t ^ 1) for t in range(TILES)])
+
     wholes, edges_of, passing = [], {}, []
     for block in range(BLOCKS):
         up_in, up_out = block >= first_up, first_up - 1 <= block < BLOCKS - 1
@@ -451,6 +496,8 @@
                 source, near_in, cross_in, far, passing[arrived] = lax.optimization_barrier(
                     (source, near_in, cross_in, far, passing[arrived])
                 )
+        if block == 15:
+            source, early = lax.optimization_barrier((source, early))
         whole, exchanged, summed = block_call(
             block,
             cores[block],
@@ -465,6 +512,8 @@
         )
         wholes.append(whole)
         source = summed if up_out else whole
+        if block == 12:
+            early = halves_of(passing[:8])
         for key, after in SWAP_AFTER.items():
             if after == block:
                 own, _ = lax.optimization_barrier((fetched[key], whole))
@@ -473,19 +522,15 @@
             if after == block:
                 fetched[key] = fetch(*key, whole)
     passing.append(hand_over(BLOCKS - 1, wholes[-1]))
-    held = pick((segment % 8).astype(jnp.int32)[None], passing)
+    late = halves_of(passing[8:])
+    kept_first = (odd == tile // 8).astype(jnp.int32)[None]
+    held = join(kept_first, [*early, *late])
     peers = [
         [(s + 8 * far) * TILES + 8 * side + z for far in range(2) for z in range(8)]
         for s in range(8)
         for side in range(2)
     ]
-    got = lax.all_to_all(
-        held.reshape(2 * MICRO, PIECE, WIDTH), BOTH, 0, 0, axis_index_groups=peers, tiled=True
-    )
-    parity = (tile % 8) // 4 ^ tile // 8
-    out = lax.dynamic_index_in_dim(
-        got.reshape(MICRO, 2, PIECE, WIDTH), parity, 1, keepdims=False
-    )
+    out = lax.all_to_all(held, BOTH, 0, 0, axis_index_groups=peers, tiled=True)
     out = out.reshape(1, MICRO, 3, CH, WIDTH)
     return out.transpose(0, 1, 2, 4, 3)
 

time: 521 us -> 508 us (0.975)
  the two profiles are of different devices: /device:TPU:34 before, /device:TPU:32 now
where the time goes in v9:
time: 508 us; the launch traced here: 498 us
  waiting for transfers between devices  136 us (27%)
  Pallas kernels  135 us (27%)
  starting transfers between devices  112 us (22%)
  blocking collectives  54.8 us (11%)
  local copies, waits for them, and re-layouts  39 us (8%)
  between operations  17.1 us (3%)
    pallas_call x16, Pallas kernels, block_call(): pl.pallas_call(functools.partial(block_body, block, at_core, up_in, up_ou...  123 us
    all_to_all x1, blocking collectives, on_device(): out = lax.all_to_all(held, BOTH, 0, 0, axis_index_groups=peers, tiled=True)  54.8 us
    ppermute x16, waiting for transfers between devices, exchange(): lax.ppermute(stats, BOTH, both)  34.9 us
    ppermute x16, waiting for transfers between devices, exchange(): lax.ppermute(near, 'tile', other_tile)  33.9 us
    unnamed x128, local copies, waits for them, and re-layouts  32.6 us
    ppermute x16, starting transfers between devices, hand_over(): return lax.ppermute(whole, BOTH, route)  27.7 us
    ppermute x16, starting transfers between devices, exchange(): lax.ppermute(stats, BOTH, both)  26.4 us
    ppermute x14, waiting for transfers between devices, fetch(): return lax.ppermute(own, 'segment', [(first, 0), (second, 1)])  23.1 us
  transfers between devices with their start and end apart: 101, of which 39 were waited for; matrix products, arithmetic and copies ran while one was open for 2% of the time, Pallas kernels for 26%

profile of v9, /device:TPU:32, one launch (start us, length us, event | category | flops | bytes accessed | tf_op | source)
XLA Modules:
  0.0 497.7 jit_solution(4889339534486648632)
XLA Ops:
  23.0 11.5 %collective-permute-done.refs_0_ = bf16[960,128]{1,0:T(8,128)(2,1)S(1)} collective-permute-done((bf16[960,128]{1,0:T(8,128)(2,1)S(1)}, bf16[960,128]{1,0:T(8,128)(2,1)S(1)}, u32[]{:S(2)}, u32[]{:S(2)}) %collective-permute-start) | collective-permute-done | bytes 245792 | tf_op jit(solution)/shard_map/ppermute | solution.py:428
  54.1 5.9 %res_block.16 = (bf16[3840,128]{1,0:T(8,128)(2,1)S(1)}, bf16[368,128]{1,0:T(8,128)(2,1)S(1)}, bf16[368,128]{1,0:T(8,128)(2,1)S(1)}, bf16[48,128]{1,0:T(8,128)(2,1)S(1)}) custom-call(s32[3]{0:T(128)S(1)} %pad_add_fusion.info, bf16[3840,128]{1,0:T(8,128)(2,1)S(1)} %get-tuple-element.194.refs_0_, bf16[368,128]{1,0:T(8,128)(2,1)S(1)} %collective-permute-done.4.refs_1_, ...), custom_call_target="tpu_custom_call" | custom-call | flops 353894400 | bytes 1048576 | tf_op jit(solution)/shard_map/res_block/pallas_call | solution.py:310
  67.1 9.6 %res_block.17 = (bf16[3840,128]{1,0:T(8,128)(2,1)}, bf16[368,128]{1,0:T(8,128)(2,1)S(1)}, bf16[368,128]{1,0:T(8,128)(2,1)S(1)}, bf16[48,128]{1,0:T(8,128)(2,1)S(1)}) custom-call(s32[3]{0:T(128)S(1)} %pad_add_fusion.info, bf16[3840,128]{1,0:T(8,128)(2,1)S(1)} %get-tuple-element.215.refs_0_.refs_13_, ...), custom_call_target="tpu_custom_call" | custom-call | flops 353894400 | bytes 1048576 | tf_op jit(solution)/shard_map/res_block/pallas_call | solution.py:310
  93.8 6.7 %collective-permute-start.24 = (bf16[320,1536]{1,0:T(8,128)(2,1)}, bf16[320,1536]{1,0:T(8,128)(2,1)S(1)}, u32[]{:S(2)}, u32[]{:S(2)}) collective-permute-start(bf16[320,1536]{1,0:T(8,128)(2,1)} %copy-done.11), channel_id=1, source_target_pairs={{0,16},{16,0},{32,48},{48,32},{64,80},{80,64},{96,112},{112,96},{1... | collective-permute-start | bytes 2949128 | tf_op jit(solution)/shard_map/ppermute | solution.py:469
  100.5 7.0 %res_block.18 = (bf16[3840,128]{1,0:T(8,128)(2,1)S(1)}, bf16[368,128]{1,0:T(8,128)(2,1)S(1)}, bf16[368,128]{1,0:T(8,128)(2,1)S(1)}, bf16[48,128]{1,0:T(8,128)(2,1)S(1)}) custom-call(s32[3]{0:T(128)S(1)} %pad_add_fusion.info, bf16[3840,128]{1,0:T(8,128)(2,1)} %get-tuple-element.228.refs_0_.refs_13_, ...), custom_call_target="tpu_custom_call" | custom-call | flops 353894400 | bytes 1048576 | tf_op jit(solution)/shard_map/res_block/pallas_call | solution.py:310
  120.8 8.5 %res_block.19 = (bf16[3840,128]{1,0:T(8,128)(2,1)S(1)}, bf16[368,128]{1,0:T(8,128)(2,1)S(1)}, bf16[368,128]{1,0:T(8,128)(2,1)S(1)}, bf16[48,128]{1,0:T(8,128)(2,1)S(1)}) custom-call(s32[3]{0:T(128)S(1)} %pad_add_fusion.info, bf16[3840,128]{1,0:T(8,128)(2,1)S(1)} %get-tuple-element.241.refs_0_.refs_13_, ...), custom_call_target="tpu_custom_call" | custom-call | flops 353894400 | bytes 1048576 | tf_op jit(solution)/shard_map/res_block/pallas_call | solution.py:310
  129.4 23.0 %collective-permute-done.33.refs_8_ = bf16[320,1408]{1,0:T(8,128)(2,1)S(1)} collective-permute-done((bf16[320,1408]{1,0:T(8,128)(2,1)S(1)}, bf16[320,1408]{1,0:T(8,128)(2,1)S(1)}, u32[]{:S(2)}, u32[]{:S(2)}) %collective-permute-start.33) | collective-permute-done | bytes 901152 | tf_op jit(solution)/shard_map/ppermute | solution.py:446
  158.3 4.6 collective-permute-done.27.refs_1_.refs_11_
  164.4 6.0 %res_block.20 = (bf16[3840,128]{1,0:T(8,128)(2,1)S(1)}, bf16[368,128]{1,0:T(8,128)(2,1)S(1)}, bf16[368,128]{1,0:T(8,128)(2,1)S(1)}, bf16[48,128]{1,0:T(8,128)(2,1)S(1)}) custom-call(s32[3]{0:T(128)S(1)} %pad_add_fusion.info, bf16[3840,128]{1,0:T(8,128)(2,1)S(1)} %get-tuple-element.254.refs_0_.refs_11_, ...), custom_call_target="tpu_custom_call" | custom-call | flops 353894400 | bytes 1048576 | tf_op jit(solution)/shard_map/res_block/pallas_call | solution.py:310
  184.9 7.3 %res_block.21 = (bf16[3840,128]{1,0:T(8,128)(2,1)S(1)}, bf16[368,128]{1,0:T(8,128)(2,1)S(1)}, bf16[368,128]{1,0:T(8,128)(2,1)S(1)}, bf16[48,128]{1,0:T(8,128)(2,1)S(1)}) custom-call(s32[3]{0:T(128)S(1)} %pad_add_fusion.info, bf16[3840,128]{1,0:T(8,128)(2,1)S(1)} %get-tuple-element.263.refs_0_, bf16[368,128]{1,0:T(8,128)(2,1)S(1)} %collective-permute-done.35.refs_1_, ...), custom_call_target="tpu_custom_call" | custom-call | flops 353894400 | bytes 1048576 | tf_op jit(solution)/shard_map/res_block/pallas_call | solution.py:310
  198.5 6.3 %res_block.22 = (bf16[3840,128]{1,0:T(8,128)(2,1)S(1)}, bf16[368,128]{1,0:T(8,128)(2,1)S(1)}, bf16[368,128]{1,0:T(8,128)(2,1)S(1)}, bf16[48,128]{1,0:T(8,128)(2,1)S(1)}) custom-call(s32[3]{0:T(128)S(1)} %pad_add_fusion.info, bf16[3840,128]{1,0:T(8,128)(2,1)S(1)} %get-tuple-element.272.refs_0_, bf16[368,128]{1,0:T(8,128)(2,1)S(1)} %collective-permute-done.43.refs_1_, ...), custom_call_target="tpu_custom_call" | custom-call | flops 353894400 | bytes 1048576 | tf_op jit(solution)/shard_map/res_block/pallas_call | solution.py:310
  213.1 8.1 %res_block.23 = (bf16[3840,128]{1,0:T(8,128)(2,1)S(1)}, bf16[368,128]{1,0:T(8,128)(2,1)S(1)}, bf16[368,128]{1,0:T(8,128)(2,1)S(1)}, bf16[48,128]{1,0:T(8,128)(2,1)S(1)}) custom-call(s32[3]{0:T(128)S(1)} %pad_add_fusion.info, bf16[3840,128]{1,0:T(8,128)(2,1)S(1)} %get-tuple-element.281.refs_0_, bf16[368,128]{1,0:T(8,128)(2,1)S(1)} %collective-permute-done.47.refs_1_, ...), custom_call_target="tpu_custom_call" | custom-call | flops 353894400 | bytes 1048576 | tf_op jit(solution)/shard_map/res_block/pallas_call | solution.py:310
  234.0 6.0 %res_block.24 = (bf16[3840,128]{1,0:T(8,128)(2,1)S(1)}, bf16[368,128]{1,0:T(8,128)(2,1)S(1)}, bf16[368,128]{1,0:T(8,128)(2,1)S(1)}, bf16[48,128]{1,0:T(8,128)(2,1)S(1)}) custom-call(s32[3]{0:T(128)S(1)} %pad_add_fusion.info, bf16[3840,128]{1,0:T(8,128)(2,1)S(1)} %get-tuple-element.290.refs_0_, bf16[368,128]{1,0:T(8,128)(2,1)S(1)} %collective-permute-done.51.refs_1_, ...), custom_call_target="tpu_custom_call" | custom-call | flops 353894400 | bytes 1048576 | tf_op jit(solution)/shard_map/res_block/pallas_call | solution.py:310
  248.9 9.4 %res_block.25 = (bf16[3840,128]{1,0:T(8,128)(2,1)}, bf16[368,128]{1,0:T(8,128)(2,1)S(1)}, bf16[368,128]{1,0:T(8,128)(2,1)S(1)}, bf16[48,128]{1,0:T(8,128)(2,1)S(1)}) custom-call(s32[3]{0:T(128)S(1)} %pad_add_fusion.info, bf16[3840,128]{1,0:T(8,128)(2,1)S(1)} %get-tuple-element.303.refs_0_, bf16[368,128]{1,0:T(8,128)(2,1)S(1)} %collective-permute-done.55.refs_1_, ...), custom_call_target="tpu_custom_call" | custom-call | flops 353894400 | bytes 1048576 | tf_op jit(solution)/shard_map/res_block/pallas_call | solution.py:310
  270.5 7.9 %res_block.26 = (bf16[3840,128]{1,0:T(8,128)(2,1)}, bf16[368,128]{1,0:T(8,128)(2,1)S(1)}, bf16[368,128]{1,0:T(8,128)(2,1)S(1)}, bf16[48,128]{1,0:T(8,128)(2,1)S(1)}) custom-call(s32[3]{0:T(128)S(1)} %pad_add_fusion.info, bf16[3840,128]{1,0:T(8,128)(2,1)} %get-tuple-element.316.refs_0_, bf16[368,128]{1,0:T(8,128)(2,1)S(1)} %collective-permute-done.59.refs_1_, ...), custom_call_target="tpu_custom_call" | custom-call | flops 353894400 | bytes 1048576 | tf_op jit(solution)/shard_map/res_block/pallas_call | solution.py:310
  279.3 9.7 %collective-permute-start.69 = (bf16[48,128]{1,0:T(8,128)(2,1)S(1)}, bf16[48,128]{1,0:T(8,128)(2,1)S(1)}, u32[]{:S(2)}, u32[]{:S(2)}) collective-permute-start(bf16[48,128]{1,0:T(8,128)(2,1)S(1)} %get-tuple-element.302.refs_3_), channel_id=1, source_target_pairs={{0,17},{1,16},{2,19},{3,18},{4,21},{5,20},{6,23},{7,22},{8,25},{9,... | collective-permute-start | bytes 36872 | tf_op jit(solution)/shard_map/ppermute | solution.py:457
  311.0 9.8 %res_block.27 = (bf16[3840,128]{1,0:T(8,128)(2,1)}, bf16[368,128]{1,0:T(8,128)(2,1)S(1)}, bf16[368,128]{1,0:T(8,128)(2,1)S(1)}, bf16[48,128]{1,0:T(8,128)(2,1)S(1)}, f32[3840,128]{1,0:T(8,128)S(1)}) custom-call(s32[3]{0:T(128)S(1)} %pad_add_fusion.info, bf16[3840,128]{1,0:T(8,128)(2,1)} %get-tuple-element.325.refs_0_, bf16[368,128]{1,0:T(8,128)(2,1)S(1)} %copy-done.42, ...), custom_call_target="tpu_custom_call" | custom-call | flops 353894400 | bytes 1048576 | tf_op jit(solution)/shard_map/res_block/pallas_call | solution.py:310
  326.7 8.1 %res_block.28 = (bf16[3840,128]{1,0:T(8,128)(2,1)}, bf16[368,128]{1,0:T(8,128)(2,1)S(1)}, bf16[368,128]{1,0:T(8,128)(2,1)S(1)}, bf16[48,128]{1,0:T(8,128)(2,1)S(1)}, f32[3840,128]{1,0:T(8,128)S(1)}) custom-call(s32[3]{0:T(128)S(1)} %pad_add_fusion.info, f32[3840,128]{1,0:T(8,128)S(1)} %get-tuple-element.317.refs_0_, ...), custom_call_target="tpu_custom_call" | custom-call | flops 353894400 | bytes 1048576 | tf_op jit(solution)/shard_map/res_block/pallas_call | solution.py:310
  345.0 10.0 %res_block.29 = (bf16[3840,128]{1,0:T(8,128)(2,1)}, bf16[368,128]{1,0:T(8,128)(2,1)S(1)}, bf16[368,128]{1,0:T(8,128)(2,1)S(1)}, bf16[48,128]{1,0:T(8,128)(2,1)S(1)}, f32[3840,128]{1,0:T(8,128)S(1)}) custom-call(s32[3]{0:T(128)S(1)} %pad_add_fusion.info, f32[3840,128]{1,0:T(8,128)S(1)} %get-tuple-element.326.refs_0_, ...), custom_call_target="tpu_custom_call" | custom-call | flops 353894400 | bytes 1048576 | tf_op jit(solution)/shard_map/res_block/pallas_call | solution.py:310
  377.1 7.2 %res_block.30 = (bf16[3840,128]{1,0:T(8,128)(2,1)S(1)}, bf16[368,128]{1,0:T(8,128)(2,1)S(1)}, bf16[368,128]{1,0:T(8,128)(2,1)S(1)}, bf16[48,128]{1,0:T(8,128)(2,1)S(1)}, f32[3840,128]{1,0:T(8,128)S(1)}) custom-call(s32[3]{0:T(128)S(1)} %pad_add_fusion.info, f32[3840,128]{1,0:T(8,128)S(1)} %copy-done.28, bf16[368,128]{1,0:T(8,128)(2,1)S(1)} %copy-done.38, ...), custom_call_target="tpu_custom_call" | custom-call | flops 353894400 | bytes 1048576 | tf_op jit(solution)/shard_map/res_block/pallas_call | solution.py:310
  391.7 6.3 %res_block.31 = bf16[3840,128]{1,0:T(8,128)(2,1)S(1)} custom-call(s32[3]{0:T(128)S(1)} %pad_add_fusion.info, f32[3840,128]{1,0:T(8,128)S(1)} %get-tuple-element.377.refs_0_, bf16[368,128]{1,0:T(8,128)(2,1)S(1)} %collective-permute-done.92.refs_1_, bf16[368,128]{1,0:T(8,128)(2,1)S(1)} %collective-permute-done.93.refs_2_, ...), custom_call_target="tpu_custom_call" | custom-call | flops 353894400 | bytes 1048576 | tf_op jit(solution)/shard_map/res_block/pallas_call | solution.py:310
  403.4 9.6 %collective-permute-done.98.refs_7_ = bf16[3840,128]{1,0:T(8,128)(2,1)S(1)} collective-permute-done((bf16[3840,128]{1,0:T(8,128)(2,1)S(1)}, bf16[3840,128]{1,0:T(8,128)(2,1)S(1)}, u32[]{:S(2)}, u32[]{:S(2)}) %collective-permute-start.98) | collective-permute-done | bytes 983072 | tf_op jit(solution)/shard_map/ppermute | solution.py:462
  417.9 12.1 %collective-permute-done.99.refs_3_ = bf16[4,480,128]{2,1,0:T(8,128)(2,1)S(1)} collective-permute-done((bf16[4,480,128]{2,1,0:T(8,128)(2,1)}, bf16[4,480,128]{2,1,0:T(8,128)(2,1)S(1)}, u32[]{:S(2)}, u32[]{:S(2)}) %collective-permute-start.99) | collective-permute-done | bytes 491552 | tf_op jit(solution)/shard_map/ppermute | solution.py:483
  433.2 54.8 %all_to_all.5 = bf16[16,480,128]{2,1,0:T(8,128)(2,1)S(1)} all-to-all(bf16[16,480,128]{2,1,0:T(8,128)(2,1)} %join.1), channel_id=1, replica_groups={{0,1,2,3,4,5,6,7,128,129,130,131,132,133,134,135},{8,9,10,11,12,13,14,1..., dimensions={0} | all-to-all | bytes 3932160 | tf_op jit(solution)/shard_map/all_to_all | solution.py:533
  (350 shorter events, 225.1 us)
Async XLA Ops:
  6.5 296.9 %all-gather.3.cloned.1.call-start = ((), (), s32[]{:S(2)}) async-start(), calls=%async_computation.1 | async-start | bytes 4177920 | tf_op jit(solution)/shard_map/all_gather | solution.py:437
  40.9 35.8 %collective-permute-start.17 = (bf16[320,1408]{1,0:T(8,128)(2,1)S(1)}, bf16[320,1408]{1,0:T(8,128)(2,1)}, u32[]{:S(2)}, u32[]{:S(2)}) collective-permute-start(bf16[320,1408]{1,0:T(8,128)(2,1)S(1)} %concatenate.16.refs_8_), channel_id=1, source_target_pairs={{32,0},{96,16},{33,1},{97,17},{34,2},{98,18},{35,3},{99,19},{36,4}... | collective-permute-start | bytes 2703368 | tf_op jit(solution)/shard_map/ppermute | solution.py:446
  60.0 29.6 %collective-permute-start.23 = (bf16[320,1536]{1,0:T(8,128)(2,1)S(1)}, bf16[320,1536]{1,0:T(8,128)(2,1)S(1)}, u32[]{:S(2)}, u32[]{:S(2)}) collective-permute-start(bf16[320,1536]{1,0:T(8,128)(2,1)S(1)} %slice.10.refs_6_), channel_id=1, source_target_pairs={{48,0},{112,16},{49,1},{113,17},{50,2},{114,18},{51,3},{115,19},{5... | collective-permute-start | bytes 2949128 | tf_op jit(solution)/shard_map/ppermute | solution.py:446
  77.3 30.8 %collective-permute-start.25 = (bf16[320,1408]{1,0:T(8,128)(2,1)S(1)}, bf16[320,1408]{1,0:T(8,128)(2,1)}, u32[]{:S(2)}, u32[]{:S(2)}) collective-permute-start(bf16[320,1408]{1,0:T(8,128)(2,1)S(1)} %concatenate.16.refs_8_), channel_id=1, source_target_pairs={{48,0},{112,16},{49,1},{113,17},{50,2},{114,18},{51,3},{115,19},{5... | collective-permute-start | bytes 2703368 | tf_op jit(solution)/shard_map/ppermute | solution.py:446
  111.4 41.0 %collective-permute-start.33 = (bf16[320,1408]{1,0:T(8,128)(2,1)S(1)}, bf16[320,1408]{1,0:T(8,128)(2,1)S(1)}, u32[]{:S(2)}, u32[]{:S(2)}) collective-permute-start(bf16[320,1408]{1,0:T(8,128)(2,1)S(1)} %concatenate.16.refs_8_), channel_id=1, source_target_pairs={{64,0},{128,16},{65,1},{129,17},{66,2},{130,18},{67,3},{131,19},{6... | collective-permute-start | bytes 2703368 | tf_op jit(solution)/shard_map/ppermute | solution.py:446
  117.8 36.0 %collective-permute-start.30 = (bf16[3840,128]{1,0:T(8,128)(2,1)}, bf16[3840,128]{1,0:T(8,128)(2,1)S(1)}, u32[]{:S(2)}, u32[]{:S(2)}) collective-permute-start(bf16[3840,128]{1,0:T(8,128)(2,1)} %get-tuple-element.228.refs_0_.refs_13_), channel_id=1, source_target_pairs={{0,16},{1,17},{17,25},{16,24},{2,18},{3,19},{19,27},{18,26},{4,20}... | collective-permute-start | bytes 2949128 | tf_op jit(solution)/shard_map/ppermute | solution.py:462
  119.4 38.8 %collective-permute-start.39 = (bf16[320,1536]{1,0:T(8,128)(2,1)S(1)}, bf16[320,1536]{1,0:T(8,128)(2,1)S(1)}, u32[]{:S(2)}, u32[]{:S(2)}) collective-permute-start(bf16[320,1536]{1,0:T(8,128)(2,1)S(1)} %slice.10.refs_6_), channel_id=1, source_target_pairs={{80,0},{144,16},{81,1},{145,17},{82,2},{146,18},{83,3},{147,19},{8... | collective-permute-start | bytes 2949128 | tf_op jit(solution)/shard_map/ppermute | solution.py:446
  120.7 43.7 %collective-permute-start.32 = (bf16[320,1536]{1,0:T(8,128)(2,1)}, bf16[320,1536]{1,0:T(8,128)(2,1)S(1)}, u32[]{:S(2)}, u32[]{:S(2)}) collective-permute-start(bf16[320,1536]{1,0:T(8,128)(2,1)} %collective-permute-done.31.refs_6_), channel_id=1, source_target_pairs={{0,16},{16,0},{32,48},{48,32},{64,80},{80,64},{96,112},{112,96},{1... | collective-permute-start | bytes 2949128 | tf_op jit(solution)/shard_map/ppermute | solution.py:469
  171.0 27.5 %collective-permute-start.46 = (bf16[3840,128]{1,0:T(8,128)(2,1)S(1)}, bf16[3840,128]{1,0:T(8,128)(2,1)S(1)}, u32[]{:S(2)}, u32[]{:S(2)}) collective-permute-start(bf16[3840,128]{1,0:T(8,128)(2,1)S(1)} %get-tuple-element.254.refs_0_.refs_11_), channel_id=1, source_target_pairs={{0,48},{1,49},{17,57},{16,56},{2,50},{3,51},{19,59},{18,58},{4,52}... | collective-permute-start | bytes 2949128 | tf_op jit(solution)/shard_map/ppermute | solution.py:462
  181.6 31.6 %collective-permute-start.50 = (bf16[3840,128]{1,0:T(8,128)(2,1)S(1)}, bf16[3840,128]{1,0:T(8,128)(2,1)}, u32[]{:S(2)}, u32[]{:S(2)}) collective-permute-start(bf16[3840,128]{1,0:T(8,128)(2,1)S(1)} %get-tuple-element.263.refs_0_), channel_id=1, source_target_pairs={{0,64},{1,65},{17,73},{16,72},{2,66},{3,67},{19,75},{18,74},{4,68}... | collective-permute-start | bytes 2949128 | tf_op jit(solution)/shard_map/ppermute | solution.py:462
  197.2 35.4 %collective-permute-start.54 = (bf16[3840,128]{1,0:T(8,128)(2,1)S(1)}, bf16[3840,128]{1,0:T(8,128)(2,1)S(1)}, u32[]{:S(2)}, u32[]{:S(2)}) collective-permute-start(bf16[3840,128]{1,0:T(8,128)(2,1)S(1)} %get-tuple-element.272.refs_0_), channel_id=1, source_target_pairs={{0,80},{1,81},{17,89},{16,88},{2,82},{3,83},{19,91},{18,90},{4,84}... | collective-permute-start | bytes 2949128 | tf_op jit(solution)/shard_map/ppermute | solution.py:462
  209.2 30.8 %collective-permute-start.63 = (bf16[320,1536]{1,0:T(8,128)(2,1)S(1)}, bf16[320,1536]{1,0:T(8,128)(2,1)S(1)}, u32[]{:S(2)}, u32[]{:S(2)}) collective-permute-start(bf16[320,1536]{1,0:T(8,128)(2,1)S(1)} %slice.10.refs_6_), channel_id=1, source_target_pairs={{160,0},{224,16},{161,1},{225,17},{162,2},{226,18},{163,3},{227,19... | collective-permute-start | bytes 2949128 | tf_op jit(solution)/shard_map/ppermute | solution.py:446
  210.5 34.8 %collective-permute-start.58 = (bf16[3840,128]{1,0:T(8,128)(2,1)S(1)}, bf16[3840,128]{1,0:T(8,128)(2,1)S(1)}, u32[]{:S(2)}, u32[]{:S(2)}) collective-permute-start(bf16[3840,128]{1,0:T(8,128)(2,1)S(1)} %get-tuple-element.281.refs_0_), channel_id=1, source_target_pairs={{0,96},{1,97},{17,105},{16,104},{2,98},{3,99},{19,107},{18,106},{4... | collective-permute-start | bytes 2949128 | tf_op jit(solution)/shard_map/ppermute | solution.py:462
  211.8 29.1 %collective-permute-start.65 = (bf16[320,1408]{1,0:T(8,128)(2,1)S(1)}, bf16[320,1408]{1,0:T(8,128)(2,1)S(1)}, u32[]{:S(2)}, u32[]{:S(2)}) collective-permute-start(bf16[320,1408]{1,0:T(8,128)(2,1)S(1)} %concatenate.16.refs_8_), channel_id=1, source_target_pairs={{160,0},{224,16},{161,1},{225,17},{162,2},{226,18},{163,3},{227,19... | collective-permute-start | bytes 2703368 | tf_op jit(solution)/shard_map/ppermute | solution.py:446
  232.6 30.2 %collective-permute-start.62 = (bf16[3840,128]{1,0:T(8,128)(2,1)S(1)}, bf16[3840,128]{1,0:T(8,128)(2,1)S(1)}, u32[]{:S(2)}, u32[]{:S(2)}) collective-permute-start(bf16[3840,128]{1,0:T(8,128)(2,1)S(1)} %get-tuple-element.290.refs_0_), channel_id=1, source_target_pairs={{0,112},{1,113},{17,121},{16,120},{2,114},{3,115},{19,123},{18,122... | collective-permute-start | bytes 2949128 | tf_op jit(solution)/shard_map/ppermute | solution.py:462
  247.6 31.7 %collective-permute-start.73 = (bf16[320,1408]{1,0:T(8,128)(2,1)S(1)}, bf16[320,1408]{1,0:T(8,128)(2,1)}, u32[]{:S(2)}, u32[]{:S(2)}) collective-permute-start(bf16[320,1408]{1,0:T(8,128)(2,1)S(1)} %concatenate.16.refs_8_), channel_id=1, source_target_pairs={{176,0},{192,16},{177,1},{193,17},{178,2},{194,18},{179,3},{195,19... | collective-permute-start | bytes 2703368 | tf_op jit(solution)/shard_map/ppermute | solution.py:446
  261.5 33.1 %collective-permute-start.83 = (bf16[320,1536]{1,0:T(8,128)(2,1)S(1)}, bf16[320,1536]{1,0:T(8,128)(2,1)}, u32[]{:S(2)}, u32[]{:S(2)}) collective-permute-start(bf16[320,1536]{1,0:T(8,128)(2,1)S(1)} %slice.10.refs_6_), channel_id=1, source_target_pairs={{208,0},{240,16},{209,1},{241,17},{210,2},{242,18},{211,3},{243,19... | collective-permute-start | bytes 2949128 | tf_op jit(solution)/shard_map/ppermute | solution.py:446
  269.6 28.2 %collective-permute-start.72 = (bf16[320,1536]{1,0:T(8,128)(2,1)S(1)}, bf16[320,1536]{1,0:T(8,128)(2,1)S(1)}, u32[]{:S(2)}, u32[]{:S(2)}) collective-permute-start(bf16[320,1536]{1,0:T(8,128)(2,1)S(1)} %collective-permute-done.71.refs_6_), channel_id=1, source_target_pairs={{0,16},{16,0},{32,48},{48,32},{64,80},{80,64},{96,112},{112,96},{1... | collective-permute-start | bytes 2949128 | tf_op jit(solution)/shard_map/ppermute | solution.py:469
  269.8 31.2 %collective-permute-start.70 = (bf16[3840,128]{1,0:T(8,128)(2,1)S(1)}, bf16[3840,128]{1,0:T(8,128)(2,1)S(1)}, u32[]{:S(2)}, u32[]{:S(2)}) collective-permute-start(bf16[3840,128]{1,0:T(8,128)(2,1)S(1)} %get-tuple-element.303.refs_0_), channel_id=1, source_target_pairs={{0,0},{1,1},{17,9},{16,8},{2,2},{3,3},{19,11},{18,10},{4,4},{5,5},... | collective-permute-start | bytes 2949128 | tf_op jit(solution)/shard_map/ppermute | solution.py:462
  298.7 46.3 %collective-permute-start.82 = (bf16[3840,128]{1,0:T(8,128)(2,1)}, bf16[3840,128]{1,0:T(8,128)(2,1)}, u32[]{:S(2)}, u32[]{:S(2)}) collective-permute-start(bf16[3840,128]{1,0:T(8,128)(2,1)} %get-tuple-element.325.refs_0_), channel_id=1, source_target_pairs={{0,32},{1,33},{17,41},{16,40},{2,34},{3,35},{19,43},{18,42},{4,36}... | collective-permute-start | bytes 2949128 | tf_op jit(solution)/shard_map/ppermute | solution.py:462
  302.0 43.1 %collective-permute-start.84 = (bf16[320,1536]{1,0:T(8,128)(2,1)}, bf16[320,1536]{1,0:T(8,128)(2,1)}, u32[]{:S(2)}, u32[]{:S(2)}) collective-permute-start(bf16[320,1536]{1,0:T(8,128)(2,1)} %collective-permute-done.83.refs_6_), channel_id=1, source_target_pairs={{0,16},{16,0},{32,48},{48,32},{64,80},{80,64},{96,112},{112,96},{1... | collective-permute-start | bytes 2949128 | tf_op jit(solution)/shard_map/ppermute | solution.py:469
  340.5 29.7 %collective-permute-start.90 = (bf16[3840,128]{1,0:T(8,128)(2,1)}, bf16[3840,128]{1,0:T(8,128)(2,1)}, u32[]{:S(2)}, u32[]{:S(2)}) collective-permute-start(bf16[3840,128]{1,0:T(8,128)(2,1)} %get-tuple-element.339), channel_id=1, source_target_pairs={{0,48},{1,49},{17,57},{16,56},{2,50},{3,51},{19,59},{18,58},{4,52}... | collective-permute-start | bytes 2949128 | tf_op jit(solution)/shard_map/ppermute | solution.py:462
  342.7 27.4 %collective-permute-start.91 = (bf16[3840,128]{1,0:T(8,128)(2,1)}, bf16[3840,128]{1,0:T(8,128)(2,1)}, u32[]{:S(2)}, u32[]{:S(2)}) collective-permute-start(bf16[3840,128]{1,0:T(8,128)(2,1)} %get-tuple-element.345), channel_id=1, source_target_pairs={{0,64},{1,65},{17,73},{16,72},{2,66},{3,67},{19,75},{18,74},{4,68}... | collective-permute-start | bytes 2949128 | tf_op jit(solution)/shard_map/ppermute | solution.py:462
  362.6 28.4 %collective-permute-start.95 = (bf16[3840,128]{1,0:T(8,128)(2,1)}, bf16[3840,128]{1,0:T(8,128)(2,1)}, u32[]{:S(2)}, u32[]{:S(2)}) collective-permute-start(bf16[3840,128]{1,0:T(8,128)(2,1)} %get-tuple-element.355), channel_id=1, source_target_pairs={{0,80},{1,81},{17,89},{16,88},{2,82},{3,83},{19,91},{18,90},{4,84}... | collective-permute-start | bytes 2949128 | tf_op jit(solution)/shard_map/ppermute | solution.py:462
  (140 other events, 1286.3 us)
Sparse Core Ops, SparseCore 0:
  93.9 57.5 all-gather.2
